TPU v7x, 128 devices: a whole 4x4x4 slice. The times are simulated.
128 devices in a mesh: lon: 16 (over y, x_hi, core), lat: 8 (over z, x_lo).
Axes of the slice: x: 4 (x_hi: 2, x_lo: 2; x = x_hi * 2 + x_lo), y: 4, z: 4, core: 2. Of those that a mesh axis runs over, the one named last changes fastest.
Arguments:
- field: bfloat16 [78, 512, 2048], P(None, 'lat', 'lon'), may hold values from -6 to 6
- first_kernel: bfloat16 [48, 78, 5, 5], replicated, may hold values from -0.125 to 0.125
- norm_gain: float32 [48], replicated, may hold values from 0.25 to 1.75
- second_kernel: bfloat16 [78, 48, 5, 5], replicated, may hold values from -0.1875 to 0.1875
- cotangent: bfloat16 [78, 512, 2048], P(None, 'lat', 'lon'), may hold values from -6 to 6
Outputs:
- output: bfloat16 [78, 512, 2048], P(None, 'lat', 'lon')
- grad_field: bfloat16 [78, 512, 2048], P(None, 'lat', 'lon')
- grad_first: float32 [48, 78, 5, 5], replicated
- grad_second: float32 [78, 48, 5, 5], replicated
- grad_gain: float32 [48], replicated
All inputs are finite; a program needn't handle non-finite values.
Results may differ from a plain program's by a relative error of at most 0.0039.
Values may be sent and summed in bfloat16 or wider, within the bound.
No kernel may reach another device: no remote copies, remote signals or barrier semaphores. Data moves between devices by JAX's collectives and lax.ppermute only.
A program may use at most 128 MiB of HBM per device.

v0:
```python
import jax
import jax.numpy as jnp
from jax import lax
from jax.sharding import PartitionSpec as P

EPS = 1e-05


def passed_along(block, axis, distance):
    devices = range(lax.axis_size(axis))
    route = [((i - distance) % len(devices), i) for i in devices]
    return lax.ppermute(block, axis, route)


def padded_2(block, sides, width, periodic):
    for axis, dim in sides:
        count = lax.axis_size(axis)
        forward = [(i, i + 1) for i in range(count - 1)]
        if periodic:
            forward.append((count - 1, 0))
        backward = [(target, source) for source, target in forward]
        low = lax.ppermute(
            lax.slice_in_dim(block, block.shape[dim] - width, None, axis=dim), axis, forward
        )
        high = lax.ppermute(lax.slice_in_dim(block, 0, width, axis=dim), axis, backward)
        block = jnp.concatenate([low, block, high], axis=dim)
    return block


def as_sent(shard):
    return jax.tree.map(lambda a: a.astype(jnp.bfloat16) if a.dtype == jnp.float32 else a, shard)


def conv_valid(padded, kernel):
    return lax.conv_general_dilated(
        padded[None],
        kernel,
        (1, 1),
        "VALID",
        dimension_numbers=("NCHW", "OIHW", "NCHW"),
        preferred_element_type=jnp.float32,
    )[0]


def turn_kernel(kernel):
    return jnp.transpose(kernel, (1, 0, 2, 3))[:, :, ::-1, ::-1]


def conv_back(grad, kernel):
    wide = jnp.pad(grad, ((0, 0), (4, 4), (4, 4)))
    return conv_valid(wide, turn_kernel(kernel))


def kernel_grad(padded, grad):
    result = lax.conv_general_dilated(
        padded[None],
        grad[None],
        (1, 1),
        "VALID",
        dimension_numbers=("CNHW", "IOHW", "NCHW"),
        preferred_element_type=jnp.float32,
    )
    return jnp.transpose(result, (1, 0, 2, 3))


def pole_fill(tall, block):
    height = block.shape[1]
    rims = jnp.concatenate([block[:, 1::-1], block[:, height - 1 : height - 3 : -1]], axis=1)
    across = passed_along(rims, "lon", lax.axis_size("lon") // 2)
    top = jnp.where(lax.axis_index("lat") == 0, across[:, 0:2], tall[:, 0:2])
    bottom = jnp.where(
        lax.axis_index("lat") == lax.axis_size("lat") - 1,
        across[:, 2:4],
        tall[:, height + 2 : height + 4],
    )
    return jnp.concatenate([top, tall[:, 2 : height + 2], bottom], axis=1)


def pad_field(block):
    tall = padded_2(block, (("lat", 1),), 2, False)
    tall = pole_fill(tall, block)
    return padded_2(tall, (("lon", 2),), 2, True)


def pad_adjoint(grown):
    rows = grown.shape[1]
    height = rows - 4
    width = grown.shape[2] - 4
    side = padded_2(as_sent(grown), (("lon", 2),), 2, True).astype(grown.dtype)
    inner = grown[:, :, 2 : width + 2]
    left_part = inner[:, :, 0:2] + side[:, :, 0:2]
    right_part = inner[:, :, width - 2 : width] + side[:, :, width + 6 : width + 8]
    inner = jnp.concatenate([left_part, inner[:, :, 2 : width - 2], right_part], axis=2)
    rims = jnp.concatenate([inner[:, 1::-1], inner[:, rows - 1 : rows - 3 : -1]], axis=1)
    across = passed_along(as_sent(rims), "lon", lax.axis_size("lon") // 2).astype(rims.dtype)
    upper_pole = inner[:, 2:4] + jnp.where(lax.axis_index("lat") == 0, across[:, 0:2], 0.0)
    lower_pole = inner[:, height : height + 2] + jnp.where(
        lax.axis_index("lat") == lax.axis_size("lat") - 1, across[:, 2:4], 0.0
    )
    inner = jnp.concatenate(
        [inner[:, 0:2], upper_pole, inner[:, 4:height], lower_pole, inner[:, height + 2 : rows]],
        axis=1,
    )
    stack = padded_2(as_sent(inner), (("lat", 1),), 2, False).astype(inner.dtype)
    upper_rows = inner[:, 2:4] + stack[:, 0:2]
    lower_rows = inner[:, height : height + 2] + stack[:, rows + 2 : rows + 4]
    return jnp.concatenate([upper_rows, inner[:, 4:height], lower_rows], axis=1)


def back_through(grad, kernel):
    return pad_adjoint(conv_back(grad, kernel))


def per_device(field, first_kernel, norm_gain, second_kernel, cotangent):
    padded_in = pad_field(field)
    pre = conv_valid(padded_in, first_kernel)
    scale = lax.rsqrt(jnp.mean(pre * pre, axis=0, keepdims=True) + EPS)
    normed = pre * scale * norm_gain[:, None, None]
    active = jax.nn.silu(normed).astype(jnp.bfloat16)
    padded_act = pad_field(active)
    output = (field.astype(jnp.float32) + conv_valid(padded_act, second_kernel)).astype(
        jnp.bfloat16
    )
    second_local = kernel_grad(padded_act, cotangent)
    grad_act = back_through(cotangent, second_kernel)
    sig = jax.nn.sigmoid(normed)
    grad_normed = grad_act * sig * (1.0 + normed * (1.0 - sig))
    gain_local = jnp.sum(grad_normed * pre * scale, axis=(1, 2))
    scaled = grad_normed * norm_gain[:, None, None]
    grad_pre = scale * scaled - pre * (scale * scale * scale) * jnp.mean(
        scaled * pre, axis=0, keepdims=True
    )
    grad_pre = grad_pre.astype(jnp.bfloat16)
    first_local = kernel_grad(padded_in, grad_pre)
    grad_field = (cotangent.astype(jnp.float32) + back_through(grad_pre, first_kernel)).astype(
        jnp.bfloat16
    )
    first_total, second_total, gain_total = lax.psum(
        (first_local, second_local, gain_local), ("lon", "lat")
    )
    cells = field.shape[1] * field.shape[2] * lax.axis_size("lon") * lax.axis_size("lat")
    factor = 1.0 / jnp.sqrt(jnp.float32(cells))
    return (output, grad_field, first_total * factor, second_total * factor, gain_total * factor)


def solution(mesh):
    placed = (P(None, "lat", "lon"), P(), P(), P(), P(None, "lat", "lon"))
    return jax.shard_map(
        per_device,
        mesh=mesh,
        in_specs=placed,
        out_specs=(P(None, "lat", "lon"), P(None, "lat", "lon"), P(), P(), P()),
        check_vma=False,
    )
```

profile of v0, /device:TPU:1, one launch (start us, length us, event | category | flops | bytes accessed | tf_op | source)
XLA Modules:
  0.0 623.0 jit_solution(17947061775156895542)
XLA Ops:
  11.6 4.6 collective-permute-start.1
  22.7 18.0 %broadcast_select_fusion.1 = f32[68,8,17,48]{3,1,2,0:T(8,128)} fusion(pred[8,17]{0,1:T(8,128)(4,1)S(1)} %copy-done.36, bf16[78,48,5,5]{0,1,3,2:T(8,128)(2,1)S(1)} %copy-done.33, bf16[78,72,1,7,4]{0,3,4,1,2:T(8,128)(2,1)S(1)} %slice.230, bf16[78,72,1,8,17]{0,3,4,1,2:T(8,128)(2,1)S(1)} %copy.153), kind=kOutput, calls=%fused_computation.43 | convolution fusion | flops 1737330432 | bytes 3805000 | tf_op jit(solution)/shard_map/conv_general_dilated | solution.py:35
  40.7 5.9 copy.154
  48.8 4.7 copy.178
  76.2 5.1 copy.172
  110.5 16.1 %fusion.82 = (bf16[1,78,68,132]{1,3,2,0:T(8,128)(2,1)}, bf16[78,68,1,132]{0,3,1,2:T(8,128)(2,1)S(1)}) fusion(bf16[78,68,2]{0,2,1:T(2,128)(2,1)S(1)} %collective-permute-done.4, bf16[78,2,128]{0,2,1:T(8,128)(2,1)S(1)} %copy.136, bf16[78,64,128]{0,2,1:T(8,128)(2,1)S(1)} %copy-done.9, bf16[78,2,128]{0,2,1:T(8,128)(2,1)S(1)} %copy.134, ...), kind=kLoop, calls=%fused_computation.143 | loop fusion | flops 7001280 | bytes 4200768 | tf_op jit(solution)/shard_map/broadcast_in_dim | solution.py:36
  128.1 17.0 %broadcast_select_fusion.3 = f32[64,8,17,48]{3,1,2,0:T(8,128)} fusion(pred[8,17]{0,1:T(8,128)(4,1)S(1)} %copy-done.35, bf16[48,78,5,5]{1,0,3,2:T(8,128)(2,1)S(1)} %copy-done, bf16[78,68,1,7,4]{0,3,4,1,2:T(8,128)(2,1)S(1)} %slice.220, bf16[78,68,1,8,17]{0,3,4,1,2:T(8,128)(2,1)S(1)} %copy.139), kind=kOutput, calls=%fused_computation.45 | convolution fusion | flops 1635153024 | bytes 3598216 | tf_op jit(solution)/shard_map/conv_general_dilated | solution.py:35
  145.1 5.8 copy.140
  161.4 5.7 collective-permute-start.6
  169.7 72.5 %psum.23 = f32[48]{0:T(128)S(1)} all-reduce(f32[48]{0:T(128)S(1)} %get-tuple-element.30), channel_id=1, replica_groups=mesh['lon'=16,'lat'=8] {'lon','lat'}, use_global_device_ids=true, to_apply=%region_5.6 | all-reduce | flops 48 | bytes 384 | tf_op jit(solution)/shard_map/psum | solution.py:138
  250.2 4.9 copy.162
  256.4 11.3 %broadcast_select_fusion = f32[68,8,17,78]{3,1,2,0:T(8,128)S(1)} fusion(pred[8,17]{0,1:T(8,128)(4,1)S(1)} %copy-done.36, bf16[48,78,5,5]{1,0,3,2:T(8,128)(2,1)S(1)} %copy-done, bf16[48,72,1,7,4]{0,3,4,1,2:T(8,128)(2,1)S(1)} %slice.244, bf16[48,72,1,8,17]{0,3,4,1,2:T(8,128)(2,1)} %copy.162), kind=kOutput, calls=%fused_computation.42 | convolution fusion | flops 1735430656 | bytes 4206280 | tf_op jit(solution)/shard_map/conv_general_dilated | solution.py:35
  274.8 7.0 %copy.169 = bf16[1,48,64,128]{1,0,3,2:T(2,128)(2,1)} copy(bf16[1,48,64,128]{3,1,2,0:T(8,128)(2,1)S(1)} %fusion.50) | data formatting | bytes 1572864 | tf_op jit(solution)/shard_map/convert_element_type | solution.py:133
  281.8 52.5 %fusion.4 = f32[48,78,5,5]{1,0,3,2:T(8,128)} fusion(bf16[1,48,64,128]{1,0,3,2:T(2,128)(2,1)} %copy.169, bf16[1,78,68,132]{1,3,2,0:T(8,128)(2,1)} %get-tuple-element.59), kind=kOutput, calls=%fused_computation.10 | convolution fusion | flops 1533542400 | bytes 2561088 | tf_op jit(solution)/shard_map/transpose | solution.py:63
  344.2 4.6 collective-permute-start.18
  351.7 4.7 collective-permute-start.9
  361.5 5.0 slice.252
  372.0 5.5 copy.180
  383.9 10.7 %broadcast_select_fusion.2 = f32[64,8,17,78]{3,1,2,0:T(8,128)S(1)} fusion(pred[8,17]{0,1:T(8,128)(4,1)S(1)} %copy-done.35, bf16[78,48,5,5]{0,1,3,2:T(8,128)(2,1)S(1)} %copy-done.34, bf16[48,68,1,7,4]{0,3,4,1,2:T(8,128)(2,1)S(1)} %slice.228, bf16[48,68,1,8,17]{0,3,4,1,2:T(8,128)(2,1)} %copy.148), kind=kOutput, calls=%fused_computation.44 | convolution fusion | flops 1633357824 | bytes 3973576 | tf_op jit(solution)/shard_map/conv_general_dilated | solution.py:35
  397.4 7.8 %copy.171 = bf16[1,48,68,132]{1,0,3,2:T(2,128)(2,1)} copy(bf16[1,48,68,132]{3,1,2,0:T(8,128)(2,1)S(1)} %copy-done.18) | data formatting | bytes 1723392 | tf_op jit(solution)/shard_map/broadcast_in_dim | solution.py:36
  405.2 52.2 %fusion.98 = f32[78,48,5,5]{0,1,3,2:T(8,128)} fusion(bf16[1,48,68,132]{1,0,3,2:T(2,128)(2,1)} %copy.171, bf16[1,78,64,128]{1,0,3,2:T(2,128)(2,1)} %copy.172), kind=kOutput, calls=%fused_computation.156 | convolution fusion | flops 1533542400 | bytes 2514048 | tf_op jit(solution)/shard_map/transpose | solution.py:63
  461.8 4.3 copy.173
  468.6 14.5 %concatenate.79 = bf16[78,72,128]{0,1,2:T(8,128)(2,1)S(1)} concatenate(bf16[78,2,128]{0,1,2:T(2,128)(2,1)} %collective-permute-done.18, bf16[78,2,128]{0,1,2:T(2,128)(2,1)} %get-tuple-element.53, bf16[78,2,128]{0,1,2:T(2,128)(2,1)S(1)} %get-tuple-element.36, bf16[78,60,128]{0,1,2:T(8,128)(2,1)} %slice.293, bf16[78,2,128]{0,1,2:T(2,128)(2,1)S(1)} %get-tuple-element.49, ...), dimensions={1} | concatenate | bytes 2875392 | tf_op jit(solution)/shard_map/concatenate | solution.py:26
  490.2 121.9 %all-reduce.5.cloned.1.call-done = (f32[48,78,5,5]{1,0,3,2:T(8,128)}, f32[78,48,5,5]{0,1,3,2:T(8,128)}) async-done(((f32[48,78,5,5]{1,0,3,2:T(8,128)}, f32[78,48,5,5]{0,1,3,2:T(8,128)}), (f32[48,78,5,5]{1,0,3,2:T(8,128)}, f32[78,48,5,5]{0,1,3,2:T(8,128)})) %all-reduce.5.cloned.1.call-update) | async-done | bytes 748816 | tf_op jit(solution)/shard_map/psum | solution.py:138
  (210 shorter events, 145.8 us)
Async XLA Ops:
  7.2 120.8 %copy-start = (bf16[48,78,5,5]{1,0,3,2:T(8,128)(2,1)S(1)}, bf16[48,78,5,5]{1,0,3,2:T(8,128)(2,1)}, u32[]{:S(2)}) copy-start(bf16[48,78,5,5]{1,0,3,2:T(8,128)(2,1)} %param.6) | copy-start | bytes 561604
  7.2 604.9 %all-reduce.5.cloned.1.call-start = ((), (), s32[]{:S(2)}) async-start(), calls=%async_computation | async-start | bytes 2457600 | tf_op jit(solution)/shard_map/psum | solution.py:138
  11.6 86.4 %collective-permute-start.1 = (bf16[78,2,128]{0,1,2:T(2,128)(2,1)}, bf16[78,2,128]{0,1,2:T(2,128)(2,1)}, u32[]{:S(2)}, u32[]{:S(2)}) collective-permute-start(bf16[78,2,128]{0,1,2:T(2,128)(2,1)} %get-tuple-element.63), channel_id=1, source_target_pairs={{0,1},{1,2},{2,3},{3,4},{4,5},{5,6},{6,7},{8,9},{9,10},{10,11},{11... | collective-permute-start | bytes 119816 | tf_op jit(solution)/shard_map/ppermute | solution.py:22
  16.2 81.9 %collective-permute-start.2 = (bf16[78,2,128]{0,1,2:T(2,128)(2,1)}, bf16[78,2,128]{0,1,2:T(2,128)(2,1)}, u32[]{:S(2)}, u32[]{:S(2)}) collective-permute-start(bf16[78,2,128]{0,1,2:T(2,128)(2,1)} %get-tuple-element.64), channel_id=1, source_target_pairs={{1,0},{2,1},{3,2},{4,3},{5,4},{6,5},{7,6},{9,8},{10,9},{11,10},{12... | collective-permute-start | bytes 119816 | tf_op jit(solution)/shard_map/ppermute | solution.py:25
  59.1 22.9 %collective-permute-start.11 = (bf16[48,68,2]{1,0,2:T(8,128)(2,1)S(1)}, bf16[48,68,2]{1,0,2:T(8,128)(2,1)S(1)}, u32[]{:S(2)}, u32[]{:S(2)}) collective-permute-start(bf16[48,68,2]{1,0,2:T(8,128)(2,1)S(1)} %copy.157), channel_id=1, source_target_pairs={{8,0},{16,8},{24,16},{32,24},{40,32},{48,40},{56,48},{64,56},{72,6... | collective-permute-start | bytes 39176 | tf_op jit(solution)/shard_map/ppermute | solution.py:25
  61.9 19.3 %collective-permute-start.10 = (bf16[48,68,2]{1,0,2:T(8,128)(2,1)S(1)}, bf16[48,68,2]{1,0,2:T(8,128)(2,1)S(1)}, u32[]{:S(2)}, u32[]{:S(2)}) collective-permute-start(bf16[48,68,2]{1,0,2:T(8,128)(2,1)S(1)} %copy.156), channel_id=1, source_target_pairs={{0,8},{8,16},{16,24},{24,32},{32,40},{40,48},{48,56},{56,64},{64,7... | collective-permute-start | bytes 39176 | tf_op jit(solution)/shard_map/ppermute | solution.py:22
  67.3 30.7 %collective-permute-start = (bf16[78,4,128]{0,1,2:T(4,128)(2,1)}, bf16[78,4,128]{0,1,2:T(4,128)(2,1)}, u32[]{:S(2)}, u32[]{:S(2)}) collective-permute-start(bf16[78,4,128]{0,1,2:T(4,128)(2,1)} %pad_maximum_fusion.7), channel_id=1, source_target_pairs={{64,0},{72,8},{80,16},{88,24},{96,32},{104,40},{112,48},{120,56},{... | collective-permute-start | bytes 239624 | tf_op jit(solution)/shard_map/ppermute | solution.py:12
  89.0 5.3 collective-permute-start.13
  96.5 12.0 %collective-permute-start.14 = (bf16[48,2,128]{2,0,1:T(8,128)(2,1)S(1)}, bf16[48,2,128]{2,0,1:T(8,128)(2,1)S(1)}, u32[]{:S(2)}, u32[]{:S(2)}) collective-permute-start(bf16[48,2,128]{2,0,1:T(8,128)(2,1)S(1)} %get-tuple-element.44), channel_id=1, source_target_pairs={{1,0},{2,1},{3,2},{4,3},{5,4},{6,5},{7,6},{9,8},{10,9},{11,10},{12... | collective-permute-start | bytes 73736 | tf_op jit(solution)/shard_map/ppermute | solution.py:25
  97.9 5.3 collective-permute-start.12
  100.3 10.2 %collective-permute-start.3 = (bf16[78,68,2]{0,2,1:T(2,128)(2,1)S(1)}, bf16[78,68,2]{0,2,1:T(2,128)(2,1)S(1)}, u32[]{:S(2)}, u32[]{:S(2)}) collective-permute-start(bf16[78,68,2]{0,2,1:T(2,128)(2,1)S(1)} %get-tuple-element.61), channel_id=1, source_target_pairs={{0,8},{8,16},{16,24},{24,32},{32,40},{40,48},{48,56},{56,64},{64,7... | collective-permute-start | bytes 63656 | tf_op jit(solution)/shard_map/ppermute | solution.py:22
  102.2 8.3 %collective-permute-start.4 = (bf16[78,68,2]{0,2,1:T(2,128)(2,1)S(1)}, bf16[78,68,2]{0,2,1:T(2,128)(2,1)S(1)}, u32[]{:S(2)}, u32[]{:S(2)}) collective-permute-start(bf16[78,68,2]{0,2,1:T(2,128)(2,1)S(1)} %get-tuple-element.62), channel_id=1, source_target_pairs={{8,0},{16,8},{24,16},{32,24},{40,32},{48,40},{56,48},{64,56},{72,6... | collective-permute-start | bytes 63656 | tf_op jit(solution)/shard_map/ppermute | solution.py:25
  161.4 187.4 %collective-permute-start.6 = (bf16[48,2,128]{2,0,1:T(8,128)(2,1)}, bf16[48,2,128]{2,0,1:T(8,128)(2,1)}, u32[]{:S(2)}, u32[]{:S(2)}) collective-permute-start(bf16[48,2,128]{2,0,1:T(8,128)(2,1)} %get-tuple-element.75), channel_id=1, source_target_pairs={{0,1},{1,2},{2,3},{3,4},{4,5},{5,6},{6,7},{8,9},{9,10},{10,11},{11... | collective-permute-start | bytes 73736 | tf_op jit(solution)/shard_map/ppermute | solution.py:22
  168.4 180.4 %collective-permute-start.7 = (bf16[48,2,128]{2,0,1:T(8,128)(2,1)}, bf16[48,2,128]{2,0,1:T(8,128)(2,1)}, u32[]{:S(2)}, u32[]{:S(2)}) collective-permute-start(bf16[48,2,128]{2,0,1:T(8,128)(2,1)} %get-tuple-element.76), channel_id=1, source_target_pairs={{1,0},{2,1},{3,2},{4,3},{5,4},{6,5},{7,6},{9,8},{10,9},{11,10},{12... | collective-permute-start | bytes 73736 | tf_op jit(solution)/shard_map/ppermute | solution.py:25
  244.0 104.8 %collective-permute-start.5 = (bf16[48,4,128]{2,0,1:T(8,128)(2,1)}, bf16[48,4,128]{2,0,1:T(8,128)(2,1)}, u32[]{:S(2)}, u32[]{:S(2)}) collective-permute-start(bf16[48,4,128]{2,0,1:T(8,128)(2,1)} %pad_maximum_fusion.11), channel_id=1, source_target_pairs={{64,0},{72,8},{80,16},{88,24},{96,32},{104,40},{112,48},{120,56},{... | collective-permute-start | bytes 147464 | tf_op jit(solution)/shard_map/ppermute | solution.py:12
  271.2 63.8 %collective-permute-start.15 = (bf16[78,68,2]{0,1,2:T(8,128)(2,1)S(1)}, bf16[78,68,2]{0,1,2:T(8,128)(2,1)S(1)}, u32[]{:S(2)}, u32[]{:S(2)}) collective-permute-start(bf16[78,68,2]{0,1,2:T(8,128)(2,1)S(1)} %get-tuple-element.57), channel_id=1, source_target_pairs={{0,8},{8,16},{16,24},{24,32},{32,40},{40,48},{48,56},{56,64},{64,7... | collective-permute-start | bytes 63656 | tf_op jit(solution)/shard_map/ppermute | solution.py:22
  273.8 61.3 %collective-permute-start.16 = (bf16[78,68,2]{0,1,2:T(8,128)(2,1)S(1)}, bf16[78,68,2]{0,1,2:T(8,128)(2,1)S(1)}, u32[]{:S(2)}, u32[]{:S(2)}) collective-permute-start(bf16[78,68,2]{0,1,2:T(8,128)(2,1)S(1)} %get-tuple-element.58), channel_id=1, source_target_pairs={{8,0},{16,8},{24,16},{32,24},{40,32},{48,40},{56,48},{64,56},{72,6... | collective-permute-start | bytes 63656 | tf_op jit(solution)/shard_map/ppermute | solution.py:25
  274.8 59.6 %slice-start = ((s8[5013504]{0:T(1024)(128)(4,1)}), s8[819200]{0:T(1024)(128)(4,1)S(1)}, s32[]{:S(2)}) async-start(s8[5013504]{0:T(1024)(128)(4,1)} %bitcast.108), calls=%async_computation.1 | async-start | bytes 1638400
  340.7 127.8 %collective-permute-start.19 = (bf16[78,2,128]{0,1,2:T(2,128)(2,1)}, bf16[78,2,128]{0,1,2:T(2,128)(2,1)}, u32[]{:S(2)}, u32[]{:S(2)}) collective-permute-start(bf16[78,2,128]{0,1,2:T(2,128)(2,1)} %get-tuple-element.53), channel_id=1, source_target_pairs={{1,0},{2,1},{3,2},{4,3},{5,4},{6,5},{7,6},{9,8},{10,9},{11,10},{12... | collective-permute-start | bytes 119816 | tf_op jit(solution)/shard_map/ppermute | solution.py:25
  344.2 124.4 %collective-permute-start.18 = (bf16[78,2,128]{0,1,2:T(2,128)(2,1)}, bf16[78,2,128]{0,1,2:T(2,128)(2,1)}, u32[]{:S(2)}, u32[]{:S(2)}) collective-permute-start(bf16[78,2,128]{0,1,2:T(2,128)(2,1)} %get-tuple-element.54), channel_id=1, source_target_pairs={{0,1},{1,2},{2,3},{3,4},{4,5},{5,6},{6,7},{8,9},{9,10},{10,11},{11... | collective-permute-start | bytes 119816 | tf_op jit(solution)/shard_map/ppermute | solution.py:22
  351.7 16.8 %collective-permute-start.9 = (bf16[48,68,2]{1,0,2:T(8,128)(2,1)S(1)}, bf16[48,68,2]{1,0,2:T(8,128)(2,1)S(1)}, u32[]{:S(2)}, u32[]{:S(2)}) collective-permute-start(bf16[48,68,2]{1,0,2:T(8,128)(2,1)S(1)} %copy.143), channel_id=1, source_target_pairs={{8,0},{16,8},{24,16},{32,24},{40,32},{48,40},{56,48},{64,56},{72,6... | collective-permute-start | bytes 39176 | tf_op jit(solution)/shard_map/ppermute | solution.py:25
  356.4 11.4 %collective-permute-start.8 = (bf16[48,68,2]{1,0,2:T(8,128)(2,1)S(1)}, bf16[48,68,2]{1,0,2:T(8,128)(2,1)S(1)}, u32[]{:S(2)}, u32[]{:S(2)}) collective-permute-start(bf16[48,68,2]{1,0,2:T(8,128)(2,1)S(1)} %copy.142), channel_id=1, source_target_pairs={{0,8},{8,16},{16,24},{24,32},{32,40},{40,48},{48,56},{56,64},{64,7... | collective-permute-start | bytes 39176 | tf_op jit(solution)/shard_map/ppermute | solution.py:22
  366.5 99.7 %collective-permute-start.17 = (bf16[78,4,128]{0,1,2:T(4,128)(2,1)}, bf16[78,4,128]{0,1,2:T(4,128)(2,1)}, u32[]{:S(2)}, u32[]{:S(2)}) collective-permute-start(bf16[78,4,128]{0,1,2:T(4,128)(2,1)} %pad_maximum_fusion.8), channel_id=1, source_target_pairs={{64,0},{72,8},{80,16},{88,24},{96,32},{104,40},{112,48},{120,56},{... | collective-permute-start | bytes 239624 | tf_op jit(solution)/shard_map/ppermute | solution.py:12
  485.9 130.0 %copy-start.1 = (bf16[48,78,5,5]{1,0,3,2:T(8,128)(2,1)S(1)}, bf16[48,78,5,5]{1,0,3,2:T(8,128)(2,1)}, u32[]{:S(2)}) copy-start(bf16[48,78,5,5]{1,0,3,2:T(8,128)(2,1)} %param.6) | copy-start | bytes 561604
  (36 other events, 257.8 us)
Sparse Core Ops, SparseCore 0:
  466.3 145.7 all-reduce.4
where the time goes:
time: 629 us; the launch traced here: 623 us
  matrix products  162 us (26%)
  local copies, waits for them, and re-layouts  153 us (24%)
  waiting for transfers between devices  122 us (19%)
  blocking collectives  72.5 us (12%)
  other arithmetic  55.9 us (9%)
  starting transfers between devices  42.8 us (7%)
  between operations  15.1 us (2%)
    psum x1, waiting for transfers between devices, per_device(): lax.psum((first_local, second_local, gain_local), ('lon', 'lat'))  122 us
    transpose x2, matrix products, kernel_grad(): return jnp.transpose(result, (1, 0, 2, 3))  105 us
    psum x1, blocking collectives, per_device(): lax.psum((first_local, second_local, gain_local), ('lon', 'lat'))  72.5 us
    conv_general_dilated x4, matrix products, conv_valid(): lax.conv_general_dilated(padded[None], kernel, (1, 1), 'VALID', dimension...  56.9 us
    unnamed x91, local copies, waits for them, and re-layouts  44.3 us
    conv_general_dilated x14, local copies, waits for them, and re-layouts, conv_valid(): lax.conv_general_dilated(padded[None], kernel, (1, 1), 'VALID', dimension...  33.1 us
    ppermute x8, starting transfers between devices, padded_2(): lax.ppermute(lax.slice_in_dim(block, block.shape[dim] - width, None, axis...  25.7 us
    broadcast_in_dim x2, other arithmetic, conv_valid(): padded[None]  18.9 us
  transfers between devices with their start and end apart: 21, of which 2 were waited for; matrix products, arithmetic and copies ran while one was open for 49% of the time, Pallas kernels for 0%

commit v1 on v0

v1 whole, which is shorter than its diff:
```python
import functools

import jax
import jax.numpy as jnp
from jax import lax
from jax.experimental import pallas as pl
from jax.experimental.pallas import tpu as pltpu
from jax.sharding import PartitionSpec as P

EPS = 1e-05
BF = jnp.bfloat16
F32 = jnp.float32
AXES = ("lon", "lat")
CP = 80
VMEM = 56 * 1024 * 1024


def dot(a, b):
    return jnp.dot(a, b, preferred_element_type=F32)


def dot_nt(a, b):
    return lax.dot_general(a, b, (((1,), (1,)), ((), ())), preferred_element_type=F32)


def lanes_of(shape):
    return lax.broadcasted_iota(jnp.int32, shape, len(shape) - 1)


def edge_columns(read, rows, channels):
    pair = lanes_of((channels, 128)) // 2

    def body(r, found):
        low, high = found
        x = read(r)
        low = jnp.where(pair == r, pltpu.roll(x, 2 * r, 1), low)
        high = jnp.where(pair == r, pltpu.roll(x, lax.rem(2 * r + 2, 128), 1), high)
        return low, high

    zero = jnp.zeros((channels, 128), BF)
    return lax.fori_loop(0, rows, body, (zero, zero))


def shifted(x, right, left, row):
    lane = lanes_of(x.shape)
    back = lax.rem(128 - 2 * row, 128)
    right = pltpu.roll(right, back, 1)
    left = pltpu.roll(left, lax.rem(254 - 2 * row, 128), 1)
    return [
        pltpu.roll(jnp.where(lane >= 126, left, x), 2, 1),
        pltpu.roll(jnp.where(lane >= 127, left, x), 1, 1),
        x,
        pltpu.roll(jnp.where(lane < 1, right, x), 127, 1),
        pltpu.roll(jnp.where(lane < 2, right, x), 126, 1),
    ]


def store_shifted(out, at, x, right, left, row):
    c = x.shape[0]
    for q, piece in enumerate(shifted(x, right, left, row)):
        out[at, q * c : (q + 1) * c, :] = piece


def fill_shifted(out, read_main, right, left, rows, halo):
    def body(r, carry):
        store_shifted(out, r + 2, read_main(r), right(), left(), r)
        return carry

    lax.fori_loop(0, rows, body, 0)
    for at, x, far_right, far_left, row in halo:
        store_shifted(out, at, x, far_right, far_left, row)


def wide(ref, start, count):
    return jnp.concatenate([ref[start + t] for t in range(count)], axis=1)


def add_taps(acc, start, y, m, count, flip=None):
    for t in range(count):
        cols = slice(t * 128, (t + 1) * 128)
        for p in range(5):
            part = y[p * m : (p + 1) * m, cols]
            if flip is not None:
                part = jnp.where(flip[t], y[(4 - p) * m : (5 - p) * m, cols], part)
            acc[start[t] + 4 - p] = acc[start[t] + 4 - p] + part


def conv_rows(acc, stack, weight, m, rows, flip=None):
    acc[...] = jnp.zeros(acc.shape, F32)

    def body(i, carry):
        first = 2 + 4 * i
        y = dot(weight[...], wide(stack, first, 4))
        add_taps(acc, [first + t for t in range(4)], y, m, 4)
        return carry

    lax.fori_loop(0, rows // 4, body, 0)
    outer = (0, 1, rows + 2, rows + 3)
    y = dot(weight[...], jnp.concatenate([stack[i] for i in outer], axis=1))
    add_taps(acc, outer, y, m, 4, flip)


def row_stack(ref, i):
    return ref[pl.ds(i, 5)].reshape(5 * ref.shape[1], 128)


def correlate(stack, grown, rows, flip=None):
    n = 5 * grown.shape[1]

    def body(i, total):
        first = 2 + 4 * i
        right = jnp.concatenate([row_stack(grown, first + t) for t in range(4)], axis=1)
        return total + dot_nt(wide(stack, first, 4), right)

    total = lax.fori_loop(0, rows // 4, body, jnp.zeros((stack.shape[1], n), F32))
    outer = (0, 1, rows + 2, rows + 3)
    pieces = []
    for t, i in enumerate(outer):
        piece = row_stack(grown, i)
        if flip is not None:
            turned = jnp.concatenate([grown[i + 4 - m] for m in range(5)], axis=0)
            piece = jnp.where(flip[t], turned, piece)
        pieces.append(piece)
    left = jnp.concatenate([stack[i] for i in outer], axis=1)
    return total + dot_nt(left, jnp.concatenate(pieces, axis=1))


def pack_kernel(rows_ref, field, cot, main, low, high, rim_1, rim_2):
    height = field.shape[1]
    lost = CP - field.shape[0]
    for which, source in enumerate((field, cot)):
        for b in range(height // 16):
            block = source[:, b * 16 : (b + 1) * 16, :].astype(F32)
            block = jnp.concatenate([block, jnp.zeros((lost, 16, 128), F32)], axis=0)
            main[which, b * 16 : (b + 1) * 16] = jnp.swapaxes(block, 0, 1).astype(BF)
        low[which], high[which] = edge_columns(lambda r: main[which, r], height, CP)
        for t in range(2):
            rim_1[which, t] = main[which, rows_ref[t]]
            rim_2[which, t] = main[which, rows_ref[2 + t]]


def halo_slabs(rows_ref, odd, rim_1, rim_2, far_1, far_2, which, lo, hi):
    got = []
    for side in range(2):
        upper = side == 0
        pick = odd if upper else jnp.logical_not(odd)
        far = [jnp.where(pick, far_1[which, k], far_2[which, k]) for k in range(2)]
        for t in range(2):
            slab = jnp.where(pick, rim_1[which, t], rim_2[which, t])
            got.append((slab, far[0], far[1], rows_ref[4 + 2 * side + t]))
    return got


def first_kernel_body(
    rows_ref, main, right, left, rim_1, rim_2, far_1, far_2, w_1, w_2, gain,
    both, low, high, out_1, out_2, grads, gain_grad,
    stack_1, stack_2, acc_1, acc_2, grown_1, grown_2,
):
    height = main.shape[1]
    hid = gain.shape[0]
    odd = rows_ref[8] == 1
    top = rows_ref[9] == 1
    bottom = rows_ref[10] == 1
    flip = (top, top, bottom, bottom)
    outer = (0, 1, height + 2, height + 3)
    for which, stack in enumerate((stack_1, stack_2)):
        halo = halo_slabs(rows_ref, odd, rim_1, rim_2, far_1, far_2, which, None, None)
        fill_shifted(
            stack, lambda r: main[which, r], lambda: right[which], lambda: left[which], height,
            [(outer[t],) + halo[t] for t in range(4)],
        )
    conv_rows(acc_1, stack_1, w_1, hid, height)
    conv_rows(acc_2, stack_2, w_2, hid, height, flip)
    for grown in (grown_1, grown_2):
        grown[0:4] = jnp.zeros((4, hid, 128), BF)
        grown[height + 4 : height + 8] = jnp.zeros((4, hid, 128), BF)
    spread = jnp.broadcast_to(gain[...], (hid, 128))

    def cells(r, total):
        pre = acc_1[r + 4]
        grad_act = acc_2[r + 4]
        scale = lax.rsqrt(jnp.mean(pre * pre, axis=0, keepdims=True) + EPS)
        unit = pre * scale
        normed = unit * spread
        sig = 1.0 / (1.0 + jnp.exp(-normed))
        active = (normed * sig).astype(BF)
        grad_normed = grad_act * sig * (1.0 + normed * (1.0 - sig))
        g2 = grad_normed * spread
        mean = jnp.mean(g2 * pre, axis=0, keepdims=True)
        grad_pre = (scale * g2 - pre * (scale * scale * scale * mean)).astype(BF)
        grown_1[r + 4] = grad_pre
        grown_2[r + 4] = active
        both[r, 0:hid] = active
        both[r, hid : 2 * hid] = grad_pre
        return total + grad_normed * unit

    total = lax.fori_loop(0, height, cells, jnp.zeros((hid, 128), F32))
    gain_grad[...] = jnp.broadcast_to(jnp.sum(total, axis=1, keepdims=True), (hid, 128))
    low[...], high[...] = edge_columns(lambda r: both[r], height, 2 * hid)
    for t in range(2):
        out_1[t] = both[rows_ref[t]]
        out_2[t] = both[rows_ref[2 + t]]
    n = 5 * hid
    grads[0, :, 0:n] = correlate(stack_1, grown_1, height)
    grads[1, :, 0:n] = correlate(stack_2, grown_2, height, flip)


def second_kernel_body(
    rows_ref, both, right, left, rim_1, rim_2, far_1, far_2, w_1, w_2, field, cot,
    output, grad_field, stack, acc,
):
    height = field.shape[1]
    channels = field.shape[0]
    hid = both.shape[1] // 2
    odd = rows_ref[8] == 1
    top = rows_ref[9] == 1
    bottom = rows_ref[10] == 1
    outer = (0, 1, height + 2, height + 3)
    for which, (weight, base, out) in enumerate(
        ((w_1, field, output), (w_2, cot, grad_field))
    ):
        part = slice(which * hid, (which + 1) * hid)
        halo = []
        for side in range(2):
            pick = odd if side == 0 else jnp.logical_not(odd)
            far = [jnp.where(pick, far_1[k, part], far_2[k, part]) for k in range(2)]
            for t in range(2):
                slab = jnp.where(pick, rim_1[t, part], rim_2[t, part])
                halo.append((outer[2 * side + t], slab, far[0], far[1], rows_ref[4 + 2 * side + t]))
        fill_shifted(
            stack, lambda r: both[r, part], lambda: right[part], lambda: left[part], height, halo
        )
        flip = (top, top, bottom, bottom) if which == 1 else None
        conv_rows(acc, stack, weight, CP, height, flip)
        for b in range(height // 16):
            rows = slice(b * 16, (b + 1) * 16)
            block = jnp.swapaxes(acc[b * 16 + 4 : b * 16 + 20], 0, 1)[0:channels]
            out[:, rows, :] = (base[:, rows, :].astype(F32) + block).astype(BF)


def call(body, outs, scratch, args, flops):
    in_specs = [pl.BlockSpec(memory_space=pltpu.SMEM)]
    in_specs += [pl.BlockSpec(memory_space=pltpu.VMEM)] * (len(args) - 1)
    return pl.pallas_call(
        body,
        out_shape=[jax.ShapeDtypeStruct(s, t) for s, t in outs],
        in_specs=in_specs,
        out_specs=[pl.BlockSpec(memory_space=pltpu.VMEM)] * len(outs),
        scratch_shapes=[pltpu.VMEM(s, t) for s, t in scratch],
        compiler_params=pltpu.CompilerParams(vmem_limit_bytes=VMEM),
        cost_estimate=pl.CostEstimate(flops=flops, bytes_accessed=8 << 20, transcendentals=0),
    )(*args)


def exchange_columns(low, high):
    count = lax.axis_size("lon")
    up = [(i, (i + 1) % count) for i in range(count)]
    down = [(t, s) for s, t in up]
    right = lax.ppermute(low, "lon", down)
    left = lax.ppermute(high, "lon", up)
    return right, left


def row_routes(lon, lat):
    def at(x, y):
        return (x % lon) * lat + y

    one, two = [], []
    for x in range(lon):
        for y in range(lat):
            one.append((at(x, y), at(x, y + 1 if y % 2 == 0 else y - 1)))
            if y == 0 or y == lat - 1:
                two.append((at(x, y), at(x + lon // 2, y)))
            else:
                two.append((at(x, y), at(x, y - 1 if y % 2 == 0 else y + 1)))
    return one, two


def place_numbers(height):
    lat = lax.axis_index("lat")
    last = lax.axis_size("lat") - 1
    odd = lat % 2
    top = (lat == 0).astype(jnp.int32)
    bottom = (lat == last).astype(jnp.int32)
    h = height
    send_1 = [jnp.where(odd == 1, 0, h - 2), jnp.where(odd == 1, 1, h - 1)]
    send_2 = [
        jnp.where(odd == 1, h - 2 + bottom, top),
        jnp.where(odd == 1, h - 1 - bottom, 1 - top),
    ]
    got = [
        jnp.where(top == 1, 1, h - 2),
        jnp.where(top == 1, 0, h - 1),
        jnp.where(bottom == 1, h - 1, 0),
        jnp.where(bottom == 1, h - 2, 1),
    ]
    values = send_1 + send_2 + got + [odd, top, bottom]
    return jnp.stack([jnp.asarray(v, jnp.int32) for v in values])


def grown_sum(flat):
    got = lax.all_to_all(flat, AXES, 0, 0)
    total = jnp.sum(got.astype(F32), axis=0)
    return total


def taps(kernel, order, pads):
    out = jnp.transpose(kernel, order)
    return jnp.pad(out, pads)


def per_device(field, first_kernel, norm_gain, second_kernel, cotangent):
    channels, height, width = field.shape
    hid = norm_gain.shape[0]
    devices = lax.axis_size("lon") * lax.axis_size("lat")
    lost = CP - channels
    numbers = place_numbers(height)
    one, two = row_routes(lax.axis_size("lon"), lax.axis_size("lat"))
    flops = 2 * height * 128 * 25 * channels * hid

    main, low, high, rim_1, rim_2 = call(
        pack_kernel,
        [
            ((2, height, CP, 128), BF), ((2, CP, 128), BF), ((2, CP, 128), BF),
            ((2, 2, CP, 128), BF), ((2, 2, CP, 128), BF),
        ],
        [],
        (numbers, field, cotangent),
        flops // 8,
    )
    right, left = exchange_columns(low, high)
    sides = jnp.stack([right, left], axis=1)
    rim_1, far_1 = lax.ppermute((rim_1, sides), AXES, one)
    rim_2, far_2 = lax.ppermute((rim_2, sides), AXES, two)

    def flipped(k):
        return k[:, :, ::-1, ::-1]

    w_1 = taps(first_kernel, (2, 0, 3, 1), ((0, 0), (0, 0), (0, 0), (0, lost))).reshape(5 * hid, 5 * CP)
    w_2 = taps(flipped(second_kernel), (2, 1, 3, 0), ((0, 0), (0, 0), (0, 0), (0, lost))).reshape(5 * hid, 5 * CP)
    w_3 = taps(second_kernel, (2, 0, 3, 1), ((0, 0), (0, lost), (0, 0), (0, 0))).reshape(5 * CP, 5 * hid)
    w_4 = taps(flipped(first_kernel), (2, 1, 3, 0), ((0, 0), (0, lost), (0, 0), (0, 0))).reshape(5 * CP, 5 * hid)

    both, low, high, out_1, out_2, grads, gain_grad = call(
        first_kernel_body,
        [
            ((height, 2 * hid, 128), BF), ((2 * hid, 128), BF), ((2 * hid, 128), BF),
            ((2, 2 * hid, 128), BF), ((2, 2 * hid, 128), BF),
            ((2, 5 * CP, 256), F32), ((hid, 128), F32),
        ],
        [
            ((height + 4, 5 * CP, 128), BF), ((height + 4, 5 * CP, 128), BF),
            ((height + 8, hid, 128), F32), ((height + 8, hid, 128), F32),
            ((height + 8, hid, 128), BF), ((height + 8, hid, 128), BF),
        ],
        (numbers, main, right, left, rim_1, rim_2, far_1, far_2, w_1, w_2, norm_gain[:, None]),
        4 * flops,
    )

    n = 5 * hid
    rows = -(-(2 * 5 * CP * 2 + hid) // (16 * devices)) * 16
    flat = jnp.concatenate(
        [
            grads[:, :, 0:128].reshape(-1, 128),
            jnp.pad(grads[:, :, 128:n], ((0, 0), (0, 0), (0, 256 - n))).reshape(-1, 128),
            gain_grad,
        ],
        axis=0,
    )
    flat = jnp.pad(flat, ((0, rows * devices - flat.shape[0]), (0, 0))).astype(BF)
    got = lax.all_to_all(flat.reshape(devices, rows, 128), AXES, 0, 0)
    factor = 1.0 / jnp.sqrt(F32(height * width * devices))
    mine = (jnp.sum(got.astype(F32), axis=0) * factor).astype(BF)
    all_rows = lax.all_to_all(jnp.broadcast_to(mine, (devices, rows, 128)), AXES, 0, 0)
    all_rows = all_rows.reshape(-1, 128)

    right, left = exchange_columns(low, high)
    sides = jnp.stack([right, left], axis=0)
    out_1, far_1 = lax.ppermute((out_1, sides), AXES, one)
    out_2, far_2 = lax.ppermute((out_2, sides), AXES, two)
    output, grad_field = call(
        second_kernel_body,
        [(field.shape, BF), (field.shape, BF)],
        [((height + 4, 5 * hid, 128), BF), ((height + 8, CP, 128), F32)],
        (numbers, both, right, left, out_1, out_2, far_1, far_2, w_3, w_4, field, cotangent),
        2 * flops,
    )

    size = 2 * 5 * CP
    sums = jnp.concatenate(
        [all_rows[0:size], all_rows[size : 2 * size, 0 : n - 128]], axis=1
    ).astype(F32).reshape(2, 5, CP, 5, hid)[:, :, 0:channels]
    grad_first = jnp.transpose(sums[0], (3, 1, 2, 0))[:, :, ::-1, :]
    grad_second = jnp.transpose(sums[1], (1, 3, 2, 0))[:, :, :, ::-1]
    grad_gain = all_rows[2 * size : 2 * size + hid, 0].astype(F32)
    return output, grad_field, grad_first, grad_second, grad_gain


def solution(mesh):
    placed = (P(None, "lat", "lon"), P(), P(), P(), P(None, "lat", "lon"))
    return jax.shard_map(
        per_device,
        mesh=mesh,
        in_specs=placed,
        out_specs=(P(None, "lat", "lon"), P(None, "lat", "lon"), P(), P(), P()),
        check_vma=False,
    )
```

time: 629 us -> 171 us (0.27)
  matrix products: 162 us -> 0 us
  local copies, waits for them, and re-layouts: 153 us -> 15.7 us
  waiting for transfers between devices: 122 us -> 7.35 us
  Pallas kernels: 0 us -> 104 us
  blocking collectives: 72.5 us -> 0 us
  other arithmetic: 55.9 us -> 2.87 us
  between operations: 15.1 us -> 1.06 us
    psum x1 -> x0, waiting for transfers between devices: 122 us -> none  [per_device(): lax.psum((first_local, second_local, gain_local), ('lon', 'lat'))]
    transpose x2 -> x0, matrix products: 105 us -> none  [kernel_grad(): return jnp.transpose(result, (1, 0, 2, 3))]
    pallas_call x0 -> x3, Pallas kernels: none -> 104 us  [call(): pl.pallas_call(body, out_shape=[jax.ShapeDtypeStruct(s, t) for s, t in ou...]
    psum x1 -> x0, blocking collectives: 72.5 us -> none  [per_device(): lax.psum((first_local, second_local, gain_local), ('lon', 'lat'))]
    conv_general_dilated x4 -> x0, matrix products: 56.9 us -> none  [conv_valid(): lax.conv_general_dilated(padded[None], kernel, (1, 1), 'VALID', dimension...]
    unnamed x91 -> x46, local copies, waits for them, and re-layouts: 44.3 us -> 4.45 us
    conv_general_dilated x14 -> x0, local copies, waits for them, and re-layouts: 33.1 us -> none  [conv_valid(): lax.conv_general_dilated(padded[None], kernel, (1, 1), 'VALID', dimension...]
    slice x13 -> x4, local copies, waits for them, and re-layouts: 21.5 us -> 0.06 us  [the longest x1 0.02 us: per_device(): grads[:, :, 0:128].reshape(-1, 128)]
  transfers between devices with their start and end apart: 21 -> 14, of which waited for: 2 -> 3; matrix products, arithmetic and copies ran while one was open for 49% -> 5% of each run, Pallas kernels for 0% -> 20%
where the time goes in v1:
time: 171 us
  Pallas kernels  104 us (61%)
  starting transfers between devices  39.5 us (23%)
  local copies, waits for them, and re-layouts  15.7 us (9%)
  waiting for transfers between devices  7.35 us (4%)
  other arithmetic  2.87 us (2%)
    pallas_call x3, Pallas kernels, call(): pl.pallas_call(body, out_shape=[jax.ShapeDtypeStruct(s, t) for s, t in ou...  104 us
    all_to_all x1, starting transfers between devices, per_device(): got = lax.all_to_all(flat.reshape(devices, rows, 128), AXES, 0, 0)  12 us
    all_to_all x1, waiting for transfers between devices, per_device(): got = lax.all_to_all(flat.reshape(devices, rows, 128), AXES, 0, 0)  6.33 us
    ppermute x2, starting transfers between devices, per_device(): rim_2, far_2 = lax.ppermute((rim_2, sides), AXES, two)  5.72 us
    ppermute x2, starting transfers between devices, per_device(): out_2, far_2 = lax.ppermute((out_2, sides), AXES, two)  5.52 us
    ppermute x2, starting transfers between devices, exchange_columns(): left = lax.ppermute(high, 'lon', up)  4.91 us
    all_to_all x1, starting transfers between devices, per_device(): lax.all_to_all(jnp.broadcast_to(mine, (devices, rows, 128)), AXES, 0, 0)  4.76 us
    unnamed x46, local copies, waits for them, and re-layouts  4.45 us
  transfers between devices with their start and end apart: 14, of which 3 were waited for; matrix products, arithmetic and copies ran while one was open for 5% of the time, Pallas kernels for 20%

profile of v1, /device:TPU:1, one launch (start us, length us, event | category | flops | bytes accessed | tf_op | source)
XLA Modules:
  0.0 170.6 jit_solution(8727839095305587465)
XLA Ops:
  1.3 15.0 %shard_map.92 = (bf16[2,64,80,128]{3,2,1,0:T(8,128)(2,1)}, bf16[2,80,128]{2,1,0:T(8,128)(2,1)}, bf16[2,80,128]{2,1,0:T(8,128)(2,1)}, bf16[2,2,80,128]{3,2,1,0:T(8,128)(2,1)}, bf16[2,2,80,128]{3,2,1,0:T(8,128)(2,1)}) custom-call(s32[11]{0:T(128)} %stack.65.rows_ref, bf16[78,64,128]{2,1,0:T(8,128)(2,1)} %field.3, bf16[78,64,128]{2,1,0:T(8,128)(2,1)} %cot.3), custom_call_target="tpu_custom_call" | custom-call | flops 191692800 | bytes 8388608 | tf_op jit(solution)/shard_map/pallas_call | solution.py:244
  16.3 1.4 collective-permute-start
  17.7 2.7 %collective-permute-start.1 = (bf16[2,80,128]{2,1,0:T(8,128)(2,1)}, bf16[2,80,128]{2,1,0:T(8,128)(2,1)S(1)}, u32[]{:S(2)}, u32[]{:S(2)}) collective-permute-start(bf16[2,80,128]{2,1,0:T(8,128)(2,1)} %get-tuple-element.21), channel_id=1, source_target_pairs={{0,8},{8,16},{16,24},{24,32},{32,40},{40,48},{48,56},{56,64},{64,7... | collective-permute-start | bytes 122888 | tf_op jit(solution)/shard_map/ppermute | solution.py:260
  20.4 1.1 collective-permute-start.2
  21.6 2.9 %collective-permute-start.3 = (bf16[2,2,80,128]{3,2,1,0:T(8,128)(2,1)}, bf16[2,2,80,128]{3,2,1,0:T(8,128)(2,1)S(1)}, u32[]{:S(2)}, u32[]{:S(2)}) collective-permute-start(bf16[2,2,80,128]{3,2,1,0:T(8,128)(2,1)} %get-tuple-element.23), channel_id=1, source_target_pairs={{0,64},{1,2},{2,1},{3,4},{4,3},{5,6},{6,5},{7,71},{8,72},{9,10},{1... | collective-permute-start | bytes 245768 | tf_op jit(solution)/shard_map/ppermute | solution.py:334
  24.6 2.8 %collective-permute-start.5 = (bf16[2,2,80,128]{3,2,1,0:T(8,128)(2,1)S(1)}, bf16[2,2,80,128]{3,2,1,0:T(8,128)(2,1)S(1)}, u32[]{:S(2)}, u32[]{:S(2)}) collective-permute-start(bf16[2,2,80,128]{3,2,1,0:T(8,128)(2,1)S(1)} %pad_maximum_fusion), channel_id=1, source_target_pairs={{0,64},{1,2},{2,1},{3,4},{4,3},{5,6},{6,5},{7,71},{8,72},{9,10},{1... | collective-permute-start | bytes 245768 | tf_op jit(solution)/shard_map/ppermute | solution.py:334
  27.7 0.9 reshape.44.w_2
  29.0 0.9 reshape.43.w_1
  31.3 54.7 %shard_map.93 = (bf16[64,96,128]{2,1,0:T(8,128)(2,1)}, bf16[96,128]{1,0:T(8,128)(2,1)}, bf16[96,128]{1,0:T(8,128)(2,1)}, bf16[2,96,128]{2,1,0:T(8,128)(2,1)}, bf...) custom-call(s32[11]{0:T(128)} %stack.65.rows_ref, ...), custom_call_target="tpu_custom_call" | custom-call | flops 6134169600 | bytes 8388608 | tf_op jit(solution)/shard_map/pallas_call | solution.py:244
  86.1 1.2 convert.17
  88.2 12.0 %all-to-all-start = ((bf16[128,16,128]{2,1,0:T(8,128)(2,1)}), bf16[128,16,128]{2,1,0:T(8,128)(2,1)S(1)}, u32[]{:S(2)}, u32[]{:S(2)}) async-start(bf16[128,16,128]{2,1,0:T(8,128)(2,1)} %bitcast.22), calls=%async_computation | async-start | bytes 1048576 | tf_op jit(solution)/shard_map/all_to_all | solution.py:371
  100.2 1.1 collective-permute-start.6
  101.3 2.2 %collective-permute-start.7 = (bf16[96,128]{1,0:T(8,128)(2,1)S(1)}, bf16[96,128]{1,0:T(8,128)(2,1)S(1)}, u32[]{:S(2)}, u32[]{:S(2)}) collective-permute-start(bf16[96,128]{1,0:T(8,128)(2,1)S(1)} %copy-done.18), channel_id=1, source_target_pairs={{0,8},{8,16},{16,24},{24,32},{32,40},{40,48},{48,56},{56,64},{64,7... | collective-permute-start | bytes 73736 | tf_op jit(solution)/shard_map/ppermute | solution.py:260
  103.5 1.4 collective-permute-start.8
  104.9 2.7 %collective-permute-start.9 = (bf16[2,96,128]{2,1,0:T(8,128)(2,1)S(1)}, bf16[2,96,128]{2,1,0:T(8,128)(2,1)S(1)}, u32[]{:S(2)}, u32[]{:S(2)}) collective-permute-start(bf16[2,96,128]{2,1,0:T(8,128)(2,1)S(1)} %copy-done.12), channel_id=1, source_target_pairs={{0,64},{1,2},{2,1},{3,4},{4,3},{5,6},{6,5},{7,71},{8,72},{9,10},{1... | collective-permute-start | bytes 147464 | tf_op jit(solution)/shard_map/ppermute | solution.py:380
  107.6 6.3 %all-to-all-done = bf16[128,16,128]{2,1,0:T(8,128)(2,1)S(1)} async-done(((bf16[128,16,128]{2,1,0:T(8,128)(2,1)}), bf16[128,16,128]{2,1,0:T(8,128)(2,1)S(1)}, u32[]{:S(2)}, u32[]{:S(2)}) %all-to-all-start) | async-done | bytes 524320 | tf_op jit(solution)/shard_map/all_to_all | solution.py:371
  115.0 4.8 %all-to-all-start.1 = ((bf16[128,16,128]{2,1,0:T(8,128)(2,1)}), bf16[128,16,128]{2,1,0:T(8,128)(2,1)S(1)}, u32[]{:S(2)}, u32[]{:S(2)}) async-start(bf16[128,16,128]{2,1,0:T(8,128)(2,1)} %broadcast_in_dim.7), calls=%async_computation.1 | async-start | bytes 1048576 | tf_op jit(solution)/shard_map/all_to_all | solution.py:374
  119.8 1.5 collective-permute-start.10
  121.3 2.8 %collective-permute-start.11 = (bf16[2,96,128]{2,1,0:T(8,128)(2,1)S(1)}, bf16[2,96,128]{2,1,0:T(8,128)(2,1)S(1)}, u32[]{:S(2)}, u32[]{:S(2)}) collective-permute-start(bf16[2,96,128]{2,1,0:T(8,128)(2,1)S(1)} %pad_maximum_fusion.1), channel_id=1, source_target_pairs={{0,64},{1,2},{2,1},{3,4},{4,3},{5,6},{6,5},{7,71},{8,72},{9,10},{1... | collective-permute-start | bytes 147464 | tf_op jit(solution)/shard_map/ppermute | solution.py:380
  124.8 1.1 reshape.54.w_2
  126.6 1.1 reshape.53.w_1
  129.4 34.4 %shard_map.94 = (bf16[78,64,128]{2,1,0:T(8,128)(2,1)}, bf16[78,64,128]{2,1,0:T(8,128)(2,1)}) custom-call(s32[11]{0:T(128)} %stack.65.rows_ref, bf16[64,96,128]{2,1,0:T(8,128)(2,1)} %get-tuple-element.24.both, bf16[96,128]{1,0:T(8,128)(2,1)} %copy-done.5, bf16[96,128]{1,0:T(8,128)(2,1)} %copy-done.6, bf16[2,96,128]{2,1,0:T(8,128)(2,1)} %copy-done.14, ...), custom_call_target="tpu_custom_call" | custom-call | flops 3067084800 | bytes 8388608 | tf_op jit(solution)/shard_map/pallas_call | solution.py:244
  165.7 1.1 slice_bitcast_fusion
  166.8 1.3 rev.14
  (85 shorter events, 12.0 us)
Async XLA Ops:
  0.6 26.8 %copy-start.1 = (bf16[78,48,5,5]{0,1,3,2:T(8,128)(2,1)S(1)}, bf16[78,48,5,5]{0,1,3,2:T(8,128)(2,1)}, u32[]{:S(2)}) copy-start(bf16[78,48,5,5]{0,1,3,2:T(8,128)(2,1)} %param.8) | copy-start | bytes 561604
  16.3 8.2 %collective-permute-start = (bf16[2,80,128]{2,1,0:T(8,128)(2,1)}, bf16[2,80,128]{2,1,0:T(8,128)(2,1)S(1)}, u32[]{:S(2)}, u32[]{:S(2)}) collective-permute-start(bf16[2,80,128]{2,1,0:T(8,128)(2,1)} %get-tuple-element.20), channel_id=1, source_target_pairs={{8,0},{16,8},{24,16},{32,24},{40,32},{48,40},{56,48},{64,56},{72,6... | collective-permute-start | bytes 122888 | tf_op jit(solution)/shard_map/ppermute | solution.py:259
  17.7 6.8 %collective-permute-start.1 = (bf16[2,80,128]{2,1,0:T(8,128)(2,1)}, bf16[2,80,128]{2,1,0:T(8,128)(2,1)S(1)}, u32[]{:S(2)}, u32[]{:S(2)}) collective-permute-start(bf16[2,80,128]{2,1,0:T(8,128)(2,1)} %get-tuple-element.21), channel_id=1, source_target_pairs={{0,8},{8,16},{16,24},{24,32},{32,40},{40,48},{48,56},{56,64},{64,7... | collective-permute-start | bytes 122888 | tf_op jit(solution)/shard_map/ppermute | solution.py:260
  20.4 10.2 %collective-permute-start.2 = (bf16[2,2,80,128]{3,2,1,0:T(8,128)(2,1)}, bf16[2,2,80,128]{3,2,1,0:T(8,128)(2,1)S(1)}, u32[]{:S(2)}, u32[]{:S(2)}) collective-permute-start(bf16[2,2,80,128]{3,2,1,0:T(8,128)(2,1)} %get-tuple-element.22), channel_id=1, source_target_pairs={{0,1},{1,0},{2,3},{3,2},{4,5},{5,4},{6,7},{7,6},{8,9},{9,8},{10,11... | collective-permute-start | bytes 245768 | tf_op jit(solution)/shard_map/ppermute | solution.py:333
  21.6 9.0 %collective-permute-start.3 = (bf16[2,2,80,128]{3,2,1,0:T(8,128)(2,1)}, bf16[2,2,80,128]{3,2,1,0:T(8,128)(2,1)S(1)}, u32[]{:S(2)}, u32[]{:S(2)}) collective-permute-start(bf16[2,2,80,128]{3,2,1,0:T(8,128)(2,1)} %get-tuple-element.23), channel_id=1, source_target_pairs={{0,64},{1,2},{2,1},{3,4},{4,3},{5,6},{6,5},{7,71},{8,72},{9,10},{1... | collective-permute-start | bytes 245768 | tf_op jit(solution)/shard_map/ppermute | solution.py:334
  24.5 4.2 %copy-start.2 = (bf16[2,80,128]{2,1,0:T(8,128)(2,1)}, bf16[2,80,128]{2,1,0:T(8,128)(2,1)S(1)}, u32[]{:S(2)}) copy-start(bf16[2,80,128]{2,1,0:T(8,128)(2,1)S(1)} %collective-permute-done.right) | copy-start | bytes 122884
  24.5 4.2 %copy-start.3 = (bf16[2,80,128]{2,1,0:T(8,128)(2,1)}, bf16[2,80,128]{2,1,0:T(8,128)(2,1)S(1)}, u32[]{:S(2)}) copy-start(bf16[2,80,128]{2,1,0:T(8,128)(2,1)S(1)} %collective-permute-done.1.left) | copy-start | bytes 122884
  24.5 4.2 %copy-start = (bf16[48,78,5,5]{1,0,3,2:T(8,128)(2,1)S(1)}, bf16[48,78,5,5]{1,0,3,2:T(8,128)(2,1)}, u32[]{:S(2)}) copy-start(bf16[48,78,5,5]{1,0,3,2:T(8,128)(2,1)} %param.6) | copy-start | bytes 561604
  24.5 6.1 %collective-permute-start.4 = (bf16[2,2,80,128]{3,2,1,0:T(8,128)(2,1)S(1)}, bf16[2,2,80,128]{3,2,1,0:T(8,128)(2,1)S(1)}, u32[]{:S(2)}, u32[]{:S(2)}) collective-permute-start(bf16[2,2,80,128]{3,2,1,0:T(8,128)(2,1)S(1)} %pad_maximum_fusion), channel_id=1, source_target_pairs={{0,1},{1,0},{2,3},{3,2},{4,5},{5,4},{6,7},{7,6},{8,9},{9,8},{10,11... | collective-permute-start | bytes 245768 | tf_op jit(solution)/shard_map/ppermute | solution.py:333
  24.6 6.0 %collective-permute-start.5 = (bf16[2,2,80,128]{3,2,1,0:T(8,128)(2,1)S(1)}, bf16[2,2,80,128]{3,2,1,0:T(8,128)(2,1)S(1)}, u32[]{:S(2)}, u32[]{:S(2)}) collective-permute-start(bf16[2,2,80,128]{3,2,1,0:T(8,128)(2,1)S(1)} %pad_maximum_fusion), channel_id=1, source_target_pairs={{0,64},{1,2},{2,1},{3,4},{4,3},{5,6},{6,5},{7,71},{8,72},{9,10},{1... | collective-permute-start | bytes 245768 | tf_op jit(solution)/shard_map/ppermute | solution.py:334
  87.2 13.0 %copy-start.19 = (bf16[96,128]{1,0:T(8,128)(2,1)S(1)}, bf16[96,128]{1,0:T(8,128)(2,1)}, u32[]{:S(2)}) copy-start(bf16[96,128]{1,0:T(8,128)(2,1)} %get-tuple-element.25) | copy-start | bytes 73732
  87.3 14.1 %copy-start.18 = (bf16[96,128]{1,0:T(8,128)(2,1)S(1)}, bf16[96,128]{1,0:T(8,128)(2,1)}, u32[]{:S(2)}) copy-start(bf16[96,128]{1,0:T(8,128)(2,1)} %get-tuple-element.26) | copy-start | bytes 73732
  87.3 16.3 %copy-start.13 = (bf16[2,96,128]{2,1,0:T(8,128)(2,1)S(1)}, bf16[2,96,128]{2,1,0:T(8,128)(2,1)}, u32[]{:S(2)}) copy-start(bf16[2,96,128]{2,1,0:T(8,128)(2,1)} %get-tuple-element.27) | copy-start | bytes 147460
  87.3 17.6 %copy-start.12 = (bf16[2,96,128]{2,1,0:T(8,128)(2,1)S(1)}, bf16[2,96,128]{2,1,0:T(8,128)(2,1)}, u32[]{:S(2)}) copy-start(bf16[2,96,128]{2,1,0:T(8,128)(2,1)} %get-tuple-element.28) | copy-start | bytes 147460
  88.2 25.7 %all-to-all-start = ((bf16[128,16,128]{2,1,0:T(8,128)(2,1)}), bf16[128,16,128]{2,1,0:T(8,128)(2,1)S(1)}, u32[]{:S(2)}, u32[]{:S(2)}) async-start(bf16[128,16,128]{2,1,0:T(8,128)(2,1)} %bitcast.22), calls=%async_computation | async-start | bytes 1048576 | tf_op jit(solution)/shard_map/all_to_all | solution.py:371
  100.2 19.5 %collective-permute-start.6 = (bf16[96,128]{1,0:T(8,128)(2,1)S(1)}, bf16[96,128]{1,0:T(8,128)(2,1)S(1)}, u32[]{:S(2)}, u32[]{:S(2)}) collective-permute-start(bf16[96,128]{1,0:T(8,128)(2,1)S(1)} %copy-done.19), channel_id=1, source_target_pairs={{8,0},{16,8},{24,16},{32,24},{40,32},{48,40},{56,48},{64,56},{72,6... | collective-permute-start | bytes 73736 | tf_op jit(solution)/shard_map/ppermute | solution.py:259
  101.3 18.4 %collective-permute-start.7 = (bf16[96,128]{1,0:T(8,128)(2,1)S(1)}, bf16[96,128]{1,0:T(8,128)(2,1)S(1)}, u32[]{:S(2)}, u32[]{:S(2)}) collective-permute-start(bf16[96,128]{1,0:T(8,128)(2,1)S(1)} %copy-done.18), channel_id=1, source_target_pairs={{0,8},{8,16},{16,24},{24,32},{32,40},{40,48},{48,56},{56,64},{64,7... | collective-permute-start | bytes 73736 | tf_op jit(solution)/shard_map/ppermute | solution.py:260
  103.5 24.2 %collective-permute-start.8 = (bf16[2,96,128]{2,1,0:T(8,128)(2,1)S(1)}, bf16[2,96,128]{2,1,0:T(8,128)(2,1)S(1)}, u32[]{:S(2)}, u32[]{:S(2)}) collective-permute-start(bf16[2,96,128]{2,1,0:T(8,128)(2,1)S(1)} %copy-done.13), channel_id=1, source_target_pairs={{0,1},{1,0},{2,3},{3,2},{4,5},{5,4},{6,7},{7,6},{8,9},{9,8},{10,11... | collective-permute-start | bytes 147464 | tf_op jit(solution)/shard_map/ppermute | solution.py:379
  104.9 22.8 %collective-permute-start.9 = (bf16[2,96,128]{2,1,0:T(8,128)(2,1)S(1)}, bf16[2,96,128]{2,1,0:T(8,128)(2,1)S(1)}, u32[]{:S(2)}, u32[]{:S(2)}) collective-permute-start(bf16[2,96,128]{2,1,0:T(8,128)(2,1)S(1)} %copy-done.12), channel_id=1, source_target_pairs={{0,64},{1,2},{2,1},{3,4},{4,3},{5,6},{6,5},{7,71},{8,72},{9,10},{1... | collective-permute-start | bytes 147464 | tf_op jit(solution)/shard_map/ppermute | solution.py:380
  115.0 48.8 %all-to-all-start.1 = ((bf16[128,16,128]{2,1,0:T(8,128)(2,1)}), bf16[128,16,128]{2,1,0:T(8,128)(2,1)S(1)}, u32[]{:S(2)}, u32[]{:S(2)}) async-start(bf16[128,16,128]{2,1,0:T(8,128)(2,1)} %broadcast_in_dim.7), calls=%async_computation.1 | async-start | bytes 1048576 | tf_op jit(solution)/shard_map/all_to_all | solution.py:374
  119.7 5.1 %copy-start.5 = (bf16[96,128]{1,0:T(8,128)(2,1)}, bf16[96,128]{1,0:T(8,128)(2,1)S(1)}, u32[]{:S(2)}) copy-start(bf16[96,128]{1,0:T(8,128)(2,1)S(1)} %collective-permute-done.6.right) | copy-start | bytes 73732
  119.8 5.1 %copy-start.6 = (bf16[96,128]{1,0:T(8,128)(2,1)}, bf16[96,128]{1,0:T(8,128)(2,1)S(1)}, u32[]{:S(2)}) copy-start(bf16[96,128]{1,0:T(8,128)(2,1)S(1)} %collective-permute-done.7.left) | copy-start | bytes 73732
  119.8 8.1 %collective-permute-start.10 = (bf16[2,96,128]{2,1,0:T(8,128)(2,1)S(1)}, bf16[2,96,128]{2,1,0:T(8,128)(2,1)S(1)}, u32[]{:S(2)}, u32[]{:S(2)}) collective-permute-start(bf16[2,96,128]{2,1,0:T(8,128)(2,1)S(1)} %pad_maximum_fusion.1), channel_id=1, source_target_pairs={{0,1},{1,0},{2,3},{3,2},{4,5},{5,4},{6,7},{7,6},{8,9},{9,8},{10,11... | collective-permute-start | bytes 147464 | tf_op jit(solution)/shard_map/ppermute | solution.py:379
  121.3 7.5 %collective-permute-start.11 = (bf16[2,96,128]{2,1,0:T(8,128)(2,1)S(1)}, bf16[2,96,128]{2,1,0:T(8,128)(2,1)S(1)}, u32[]{:S(2)}, u32[]{:S(2)}) collective-permute-start(bf16[2,96,128]{2,1,0:T(8,128)(2,1)S(1)} %pad_maximum_fusion.1), channel_id=1, source_target_pairs={{0,64},{1,2},{2,1},{3,4},{4,3},{5,6},{6,5},{7,71},{8,72},{9,10},{1... | collective-permute-start | bytes 147464 | tf_op jit(solution)/shard_map/ppermute | solution.py:380
  (10 other events, 9.6 us)

commit v2 on v1

--- a/solution.py
+++ b/solution.py
@@ -12,6 +12,7 @@
 F32 = jnp.float32
 AXES = ("lon", "lat")
 CP = 80
+WIRE = BF
 VMEM = 56 * 1024 * 1024
 
 
@@ -38,7 +39,7 @@
         return low, high
 
     zero = jnp.zeros((channels, 128), BF)
-    return lax.fori_loop(0, rows, body, (zero, zero))
+    return lax.fori_loop(0, rows, body, (zero, zero), unroll=16)
 
 
 def shifted(x, right, left, row):
@@ -66,7 +67,7 @@
         store_shifted(out, r + 2, read_main(r), right(), left(), r)
         return carry
 
-    lax.fori_loop(0, rows, body, 0)
+    lax.fori_loop(0, rows, body, 0, unroll=4)
     for at, x, far_right, far_left, row in halo:
         store_shifted(out, at, x, far_right, far_left, row)
 
@@ -88,13 +89,8 @@
 def conv_rows(acc, stack, weight, m, rows, flip=None):
     acc[...] = jnp.zeros(acc.shape, F32)
 
-    def body(i, carry):
-        first = 2 + 4 * i
-        y = dot(weight[...], wide(stack, first, 4))
-        add_taps(acc, [first + t for t in range(4)], y, m, 4)
-        return carry
-
-    lax.fori_loop(0, rows // 4, body, 0)
+    y = dot(weight[...], wide(stack, 2, rows))
+    add_taps(acc, range(2, rows + 2), y, m, rows)
     outer = (0, 1, rows + 2, rows + 3)
     y = dot(weight[...], jnp.concatenate([stack[i] for i in outer], axis=1))
     add_taps(acc, outer, y, m, 4, flip)
@@ -105,14 +101,9 @@
 
 
 def correlate(stack, grown, rows, flip=None):
-    n = 5 * grown.shape[1]
-
-    def body(i, total):
-        first = 2 + 4 * i
-        right = jnp.concatenate([row_stack(grown, first + t) for t in range(4)], axis=1)
-        return total + dot_nt(wide(stack, first, 4), right)
-
-    total = lax.fori_loop(0, rows // 4, body, jnp.zeros((stack.shape[1], n), F32))
+    inner = range(2, rows + 2)
+    right = jnp.concatenate([row_stack(grown, i) for i in inner], axis=1)
+    total = dot_nt(wide(stack, 2, rows), right)
     outer = (0, 1, rows + 2, rows + 3)
     pieces = []
     for t, i in enumerate(outer):
@@ -153,7 +144,7 @@
 
 def first_kernel_body(
     rows_ref, main, right, left, rim_1, rim_2, far_1, far_2, w_1, w_2, gain,
-    both, low, high, out_1, out_2, grads, gain_grad,
+    both, low, high, out_1, out_2, flat,
     stack_1, stack_2, acc_1, acc_2, grown_1, grown_2,
 ):
     height = main.shape[1]
@@ -194,61 +185,114 @@
         both[r, hid : 2 * hid] = grad_pre
         return total + grad_normed * unit
 
-    total = lax.fori_loop(0, height, cells, jnp.zeros((hid, 128), F32))
-    gain_grad[...] = jnp.broadcast_to(jnp.sum(total, axis=1, keepdims=True), (hid, 128))
+    total = lax.fori_loop(0, height, cells, jnp.zeros((hid, 128), F32), unroll=4)
     low[...], high[...] = edge_columns(lambda r: both[r], height, 2 * hid)
     for t in range(2):
         out_1[t] = both[rows_ref[t]]
         out_2[t] = both[rows_ref[2 + t]]
-    n = 5 * hid
-    grads[0, :, 0:n] = correlate(stack_1, grown_1, height)
-    grads[1, :, 0:n] = correlate(stack_2, grown_2, height, flip)
+    m = 5 * CP
+    spare = jnp.zeros((m, 256 - 5 * hid), F32)
+    for which, found in enumerate(
+        (correlate(stack_1, grown_1, height), correlate(stack_2, grown_2, height, flip))
+    ):
+        found = jnp.concatenate([found, spare], axis=1).astype(WIRE)
+        flat[2 * which * m : (2 * which + 1) * m] = found[:, 0:128]
+        flat[(2 * which + 1) * m : (2 * which + 2) * m] = found[:, 128:256]
+    used = flat.shape[0] - 4 * m
+    total = jnp.broadcast_to(jnp.sum(total, axis=1, keepdims=True), (hid, 128))
+    total = jnp.concatenate([total, jnp.zeros((used - hid, 128), F32)], axis=0)
+    flat[4 * m :] = total.astype(WIRE)
 
 
 def second_kernel_body(
-    rows_ref, both, right, left, rim_1, rim_2, far_1, far_2, w_1, w_2, field, cot,
-    output, grad_field, stack, acc,
+    which, rows_ref, both, right, left, rim_1, rim_2, far_1, far_2, weight, base, out, stack, acc,
 ):
-    height = field.shape[1]
-    channels = field.shape[0]
+    height = base.shape[1]
+    channels = base.shape[0]
     hid = both.shape[1] // 2
     odd = rows_ref[8] == 1
     top = rows_ref[9] == 1
     bottom = rows_ref[10] == 1
     outer = (0, 1, height + 2, height + 3)
-    for which, (weight, base, out) in enumerate(
-        ((w_1, field, output), (w_2, cot, grad_field))
-    ):
-        part = slice(which * hid, (which + 1) * hid)
-        halo = []
-        for side in range(2):
-            pick = odd if side == 0 else jnp.logical_not(odd)
-            far = [jnp.where(pick, far_1[k, part], far_2[k, part]) for k in range(2)]
-            for t in range(2):
-                slab = jnp.where(pick, rim_1[t, part], rim_2[t, part])
-                halo.append((outer[2 * side + t], slab, far[0], far[1], rows_ref[4 + 2 * side + t]))
-        fill_shifted(
-            stack, lambda r: both[r, part], lambda: right[part], lambda: left[part], height, halo
-        )
-        flip = (top, top, bottom, bottom) if which == 1 else None
-        conv_rows(acc, stack, weight, CP, height, flip)
-        for b in range(height // 16):
-            rows = slice(b * 16, (b + 1) * 16)
-            block = jnp.swapaxes(acc[b * 16 + 4 : b * 16 + 20], 0, 1)[0:channels]
-            out[:, rows, :] = (base[:, rows, :].astype(F32) + block).astype(BF)
-
-
-def call(body, outs, scratch, args, flops):
-    in_specs = [pl.BlockSpec(memory_space=pltpu.SMEM)]
-    in_specs += [pl.BlockSpec(memory_space=pltpu.VMEM)] * (len(args) - 1)
+    part = slice(which * hid, (which + 1) * hid)
+    halo = []
+    for side in range(2):
+        pick = odd if side == 0 else jnp.logical_not(odd)
+        far = [jnp.where(pick, far_1[k, part], far_2[k, part]) for k in range(2)]
+        for t in range(2):
+            slab = jnp.where(pick, rim_1[t, part], rim_2[t, part])
+            halo.append((outer[2 * side + t], slab, far[0], far[1], rows_ref[4 + 2 * side + t]))
+    fill_shifted(
+        stack, lambda r: both[r, part], lambda: right[part], lambda: left[part], height, halo
+    )
+    flip = (top, top, bottom, bottom) if which == 1 else None
+    conv_rows(acc, stack, weight, CP, height, flip)
+    for b in range(height // 16):
+        rows = slice(b * 16, (b + 1) * 16)
+        block = jnp.swapaxes(acc[b * 16 + 4 : b * 16 + 20], 0, 1)[0:channels]
+        out[:, rows, :] = (base[:, rows, :].astype(F32) + block).astype(BF)
+
+
+def weights_kernel(k_1, k_2, w_1, w_2, w_3, w_4):
+    hid, channels = k_1.shape[2:]
+    gap = jnp.zeros((hid, CP - channels), F32)
+
+    def plane(k, p, q):
+        return jnp.concatenate([k[p, q].astype(F32), gap], axis=1)
+
+    for p in range(5):
+        rows = slice(p * hid, (p + 1) * hid)
+        w_1[rows] = jnp.concatenate([plane(k_1, p, q) for q in range(5)], axis=1).astype(BF)
+        w_2[rows] = jnp.concatenate([plane(k_2, 4 - p, 4 - q) for q in range(5)], axis=1).astype(BF)
+        rows = slice(p * CP, (p + 1) * CP)
+        w_3[rows] = jnp.concatenate([plane(k_2, p, q) for q in range(5)], axis=0).T.astype(BF)
+        w_4[rows] = jnp.concatenate([plane(k_1, 4 - p, 4 - q) for q in range(5)], axis=0).T.astype(BF)
+
+
+def reduce_kernel(factor, got, out):
+    devices = got.shape[0]
+
+    def body(i, total):
+        return total + got[i].astype(F32)
+
+    total = lax.fori_loop(0, devices, body, jnp.zeros(got.shape[1:], F32), unroll=16)
+    mine = (total * factor).astype(BF)
+    for i in range(devices):
+        out[i] = mine
+
+
+def unpack_kernel(rows, grad_1, grad_2, gain):
+    hid, channels = grad_1.shape[2:]
+    m = 5 * CP
+    for which in range(2):
+        at = 2 * which * m
+        low = rows[at : at + m].astype(F32).T
+        high = rows[at + m : at + 2 * m].astype(F32).T
+        both = jnp.concatenate([low, high], axis=0)
+        for q in range(5):
+            part = both[0 : 5 * hid, q * CP : q * CP + channels]
+            for t in range(5):
+                piece = part[t * hid : (t + 1) * hid]
+                if which == 0:
+                    grad_1[4 - t, q] = piece
+                else:
+                    grad_2[t, 4 - q] = piece
+    gain[...] = rows[4 * m : 4 * m + hid].astype(F32).T[0:1]
+
+
+def call(body, outs, scratch, args, flops, numbers=True):
+    vmem = pl.BlockSpec(memory_space=pltpu.VMEM)
+    in_specs = [vmem] * len(args)
+    if numbers:
+        in_specs[0] = pl.BlockSpec(memory_space=pltpu.SMEM)
     return pl.pallas_call(
         body,
         out_shape=[jax.ShapeDtypeStruct(s, t) for s, t in outs],
         in_specs=in_specs,
-        out_specs=[pl.BlockSpec(memory_space=pltpu.VMEM)] * len(outs),
+        out_specs=[vmem] * len(outs),
         scratch_shapes=[pltpu.VMEM(s, t) for s, t in scratch],
         compiler_params=pltpu.CompilerParams(vmem_limit_bytes=VMEM),
-        cost_estimate=pl.CostEstimate(flops=flops, bytes_accessed=8 << 20, transcendentals=0),
+        cost_estimate=pl.CostEstimate(flops=flops, bytes_accessed=1 << 20, transcendentals=0),
     )(*args)
 
 
@@ -298,25 +342,13 @@
     return jnp.stack([jnp.asarray(v, jnp.int32) for v in values])
 
 
-def grown_sum(flat):
-    got = lax.all_to_all(flat, AXES, 0, 0)
-    total = jnp.sum(got.astype(F32), axis=0)
-    return total
-
-
-def taps(kernel, order, pads):
-    out = jnp.transpose(kernel, order)
-    return jnp.pad(out, pads)
-
-
 def per_device(field, first_kernel, norm_gain, second_kernel, cotangent):
     channels, height, width = field.shape
     hid = norm_gain.shape[0]
     devices = lax.axis_size("lon") * lax.axis_size("lat")
-    lost = CP - channels
     numbers = place_numbers(height)
     one, two = row_routes(lax.axis_size("lon"), lax.axis_size("lat"))
-    flops = 2 * height * 128 * 25 * channels * hid
+    us = 10**9
 
     main, low, high, rim_1, rim_2 = call(
         pack_kernel,
@@ -326,27 +358,27 @@
         ],
         [],
         (numbers, field, cotangent),
-        flops // 8,
+        5 * us,
     )
     right, left = exchange_columns(low, high)
     sides = jnp.stack([right, left], axis=1)
     rim_1, far_1 = lax.ppermute((rim_1, sides), AXES, one)
     rim_2, far_2 = lax.ppermute((rim_2, sides), AXES, two)
 
-    def flipped(k):
-        return k[:, :, ::-1, ::-1]
-
-    w_1 = taps(first_kernel, (2, 0, 3, 1), ((0, 0), (0, 0), (0, 0), (0, lost))).reshape(5 * hid, 5 * CP)
-    w_2 = taps(flipped(second_kernel), (2, 1, 3, 0), ((0, 0), (0, 0), (0, 0), (0, lost))).reshape(5 * hid, 5 * CP)
-    w_3 = taps(second_kernel, (2, 0, 3, 1), ((0, 0), (0, lost), (0, 0), (0, 0))).reshape(5 * CP, 5 * hid)
-    w_4 = taps(flipped(first_kernel), (2, 1, 3, 0), ((0, 0), (0, lost), (0, 0), (0, 0))).reshape(5 * CP, 5 * hid)
-
-    both, low, high, out_1, out_2, grads, gain_grad = call(
+    w_1, w_2, w_3, w_4 = call(
+        weights_kernel,
+        [((5 * hid, 5 * CP), BF)] * 2 + [((5 * CP, 5 * hid), BF)] * 2,
+        [],
+        (jnp.transpose(first_kernel, (2, 3, 0, 1)), jnp.transpose(second_kernel, (2, 3, 1, 0))),
+        4 * us,
+        numbers=False,
+    )
+    rows = -(-(4 * 5 * CP + hid) // (16 * devices)) * 16
+    both, low, high, out_1, out_2, flat = call(
         first_kernel_body,
         [
             ((height, 2 * hid, 128), BF), ((2 * hid, 128), BF), ((2 * hid, 128), BF),
-            ((2, 2 * hid, 128), BF), ((2, 2 * hid, 128), BF),
-            ((2, 5 * CP, 256), F32), ((hid, 128), F32),
+            ((2, 2 * hid, 128), BF), ((2, 2 * hid, 128), BF), ((rows * devices, 128), WIRE),
         ],
         [
             ((height + 4, 5 * CP, 128), BF), ((height + 4, 5 * CP, 128), BF),
@@ -354,46 +386,41 @@
             ((height + 8, hid, 128), BF), ((height + 8, hid, 128), BF),
         ],
         (numbers, main, right, left, rim_1, rim_2, far_1, far_2, w_1, w_2, norm_gain[:, None]),
-        4 * flops,
-    )
-
-    n = 5 * hid
-    rows = -(-(2 * 5 * CP * 2 + hid) // (16 * devices)) * 16
-    flat = jnp.concatenate(
-        [
-            grads[:, :, 0:128].reshape(-1, 128),
-            jnp.pad(grads[:, :, 128:n], ((0, 0), (0, 0), (0, 256 - n))).reshape(-1, 128),
-            gain_grad,
-        ],
-        axis=0,
-    )
-    flat = jnp.pad(flat, ((0, rows * devices - flat.shape[0]), (0, 0))).astype(BF)
+        30 * us,
+    )
+
     got = lax.all_to_all(flat.reshape(devices, rows, 128), AXES, 0, 0)
-    factor = 1.0 / jnp.sqrt(F32(height * width * devices))
-    mine = (jnp.sum(got.astype(F32), axis=0) * factor).astype(BF)
-    all_rows = lax.all_to_all(jnp.broadcast_to(mine, (devices, rows, 128)), AXES, 0, 0)
-    all_rows = all_rows.reshape(-1, 128)
+    factor = (height * width * devices) ** -0.5
+    (mine,) = call(
+        functools.partial(reduce_kernel, factor), [((devices, rows, 128), BF)], [], (got,), 10 * us,
+        numbers=False,
+    )
+    summed = lax.all_to_all(mine, AXES, 0, 0).reshape(-1, 128)
+    grad_1, grad_2, gain = call(
+        unpack_kernel,
+        [((5, 5, hid, channels), F32)] * 2 + [((1, hid), F32)],
+        [],
+        (summed,),
+        20 * us,
+        numbers=False,
+    )
+    grad_first = jnp.transpose(grad_1, (2, 3, 0, 1))
+    grad_second = jnp.transpose(grad_2, (3, 2, 0, 1))
 
     right, left = exchange_columns(low, high)
     sides = jnp.stack([right, left], axis=0)
     out_1, far_1 = lax.ppermute((out_1, sides), AXES, one)
     out_2, far_2 = lax.ppermute((out_2, sides), AXES, two)
-    output, grad_field = call(
-        second_kernel_body,
-        [(field.shape, BF), (field.shape, BF)],
-        [((height + 4, 5 * hid, 128), BF), ((height + 8, CP, 128), F32)],
-        (numbers, both, right, left, out_1, out_2, far_1, far_2, w_3, w_4, field, cotangent),
-        2 * flops,
-    )
-
-    size = 2 * 5 * CP
-    sums = jnp.concatenate(
-        [all_rows[0:size], all_rows[size : 2 * size, 0 : n - 128]], axis=1
-    ).astype(F32).reshape(2, 5, CP, 5, hid)[:, :, 0:channels]
-    grad_first = jnp.transpose(sums[0], (3, 1, 2, 0))[:, :, ::-1, :]
-    grad_second = jnp.transpose(sums[1], (1, 3, 2, 0))[:, :, :, ::-1]
-    grad_gain = all_rows[2 * size : 2 * size + hid, 0].astype(F32)
-    return output, grad_field, grad_first, grad_second, grad_gain
+    results = []
+    for which, weight, base in ((0, w_3, field), (1, w_4, cotangent)):
+        results += call(
+            functools.partial(second_kernel_body, which),
+            [(field.shape, BF)],
+            [((height + 4, 5 * hid, 128), BF), ((height + 8, CP, 128), F32)],
+            (numbers, both, right, left, out_1, out_2, far_1, far_2, weight, base),
+            2 * us,
+        )
+    return results[0], results[1], grad_first, grad_second, gain.reshape(hid)
 
 
 def solution(mesh):

time: 171 us -> 110 us (0.64)
  Pallas kernels: 104 us -> 53 us
  local copies, waits for them, and re-layouts: 15.7 us -> 4.21 us
  waiting for transfers between devices: 7.35 us -> 13.2 us
  other arithmetic: 2.87 us -> 0.02 us
    pallas_call x3 -> x7, Pallas kernels: 104 us -> 53 us  [call(): pl.pallas_call(body, out_shape=[jax.ShapeDtypeStruct(s, t) for s, t in ou...]
    reshape x4 -> x0, local copies, waits for them, and re-layouts: 4.05 us -> none  [the longest x1 1.08 us: per_device(): taps(second_kernel, (2, 0, 3, 1), ((0, 0), (0, lost), (0, 0), (0, 0)))]
    ppermute x2, waiting for transfers between devices: 0.15 us -> 2.78 us  [per_device(): out_1, far_1 = lax.ppermute((out_1, sides), AXES, one)]
    ppermute x2, waiting for transfers between devices: 0.84 us -> 3.25 us  [per_device(): out_2, far_2 = lax.ppermute((out_2, sides), AXES, two)]
    ppermute x2, starting transfers between devices: 5.72 us -> 3.71 us  [per_device(): rim_2, far_2 = lax.ppermute((rim_2, sides), AXES, two)]
    rev x2 -> x0, local copies, waits for them, and re-layouts: 1.87 us -> none  [the longest x1 1.26 us: per_device(): grad_first = jnp.transpose(sums[0], (3, 1, 2, 0))[:, :, ::-1, :]]
    unnamed x46 -> x30, local copies, waits for them, and re-layouts: 4.45 us -> 2.86 us
  transfers between devices with their start and end apart: 14 -> 14, of which waited for: 3 -> 4; matrix products, arithmetic and copies ran while one was open for 5% -> 1% of each run, Pallas kernels for 20% -> 20%
where the time goes in v2:
time: 110 us; the launch traced here: 109 us
  Pallas kernels  53 us (48%)
  starting transfers between devices  38 us (35%)
  waiting for transfers between devices  13.2 us (12%)
  local copies, waits for them, and re-layouts  4.21 us (4%)
    pallas_call x7, Pallas kernels, call(): pl.pallas_call(body, out_shape=[jax.ShapeDtypeStruct(s, t) for s, t in ou...  53 us
    all_to_all x1, starting transfers between devices, per_device(): got = lax.all_to_all(flat.reshape(devices, rows, 128), AXES, 0, 0)  12.4 us
    all_to_all x1, waiting for transfers between devices, per_device(): got = lax.all_to_all(flat.reshape(devices, rows, 128), AXES, 0, 0)  6.17 us
    ppermute x2, starting transfers between devices, per_device(): out_2, far_2 = lax.ppermute((out_2, sides), AXES, two)  5.79 us
    ppermute x2, starting transfers between devices, exchange_columns(): left = lax.ppermute(high, 'lon', up)  4.91 us
    all_to_all x1, starting transfers between devices, per_device(): summed = lax.all_to_all(mine, AXES, 0, 0).reshape(-1, 128)  4.75 us
    ppermute x2, starting transfers between devices, per_device(): rim_2, far_2 = lax.ppermute((rim_2, sides), AXES, two)  3.71 us
    ppermute x2, waiting for transfers between devices, per_device(): out_2, far_2 = lax.ppermute((out_2, sides), AXES, two)  3.25 us
  transfers between devices with their start and end apart: 14, of which 4 were waited for; matrix products, arithmetic and copies ran while one was open for 1% of the time, Pallas kernels for 20%

profile of v2, /device:TPU:1, one launch (start us, length us, event | category | flops | bytes accessed | tf_op | source)
XLA Modules:
  0.0 109.2 jit_solution(11013902610194724825)
XLA Ops:
  1.3 6.5 %shard_map.92 = (bf16[2,64,80,128]{3,2,1,0:T(8,128)(2,1)}, bf16[2,80,128]{2,1,0:T(8,128)(2,1)}, bf16[2,80,128]{2,1,0:T(8,128)(2,1)}, bf16[2,2,80,128]{3,2,1,0:T(8,128)(2,1)}, bf16[2,2,80,128]{3,2,1,0:T(8,128)(2,1)}) custom-call(s32[11]{0:T(128)} %stack.65.rows_ref, bf16[78,64,128]{2,1,0:T(8,128)(2,1)} %base.2, bf16[78,64,128]{2,1,0:T(8,128)(2,1)} %base.3), custom_call_target="tpu_custom_call" | custom-call | flops 5000000000 | bytes 1048576 | tf_op jit(solution)/shard_map/pallas_call | solution.py:288
  7.8 1.4 %collective-permute-start = (bf16[2,80,128]{2,1,0:T(8,128)(2,1)}, bf16[2,80,128]{2,1,0:T(8,128)(2,1)S(1)}, u32[]{:S(2)}, u32[]{:S(2)}) collective-permute-start(bf16[2,80,128]{2,1,0:T(8,128)(2,1)} %get-tuple-element.24), channel_id=1, source_target_pairs={{8,0},{16,8},{24,16},{32,24},{40,32},{48,40},{56,48},{64,56},{72,6... | collective-permute-start | bytes 122888 | tf_op jit(solution)/shard_map/ppermute | solution.py:303
  9.2 2.7 %collective-permute-start.1 = (bf16[2,80,128]{2,1,0:T(8,128)(2,1)}, bf16[2,80,128]{2,1,0:T(8,128)(2,1)S(1)}, u32[]{:S(2)}, u32[]{:S(2)}) collective-permute-start(bf16[2,80,128]{2,1,0:T(8,128)(2,1)} %get-tuple-element.25), channel_id=1, source_target_pairs={{0,8},{8,16},{16,24},{24,32},{32,40},{40,48},{48,56},{56,64},{64,7... | collective-permute-start | bytes 122888 | tf_op jit(solution)/shard_map/ppermute | solution.py:304
  12.0 1.1 %collective-permute-start.2 = (bf16[2,2,80,128]{3,2,1,0:T(8,128)(2,1)}, bf16[2,2,80,128]{3,2,1,0:T(8,128)(2,1)S(1)}, u32[]{:S(2)}, u32[]{:S(2)}) collective-permute-start(bf16[2,2,80,128]{3,2,1,0:T(8,128)(2,1)} %get-tuple-element.26), channel_id=1, source_target_pairs={{0,1},{1,0},{2,3},{3,2},{4,5},{5,4},{6,7},{7,6},{8,9},{9,8},{10,11... | collective-permute-start | bytes 245768 | tf_op jit(solution)/shard_map/ppermute | solution.py:365
  13.1 2.9 %collective-permute-start.3 = (bf16[2,2,80,128]{3,2,1,0:T(8,128)(2,1)}, bf16[2,2,80,128]{3,2,1,0:T(8,128)(2,1)S(1)}, u32[]{:S(2)}, u32[]{:S(2)}) collective-permute-start(bf16[2,2,80,128]{3,2,1,0:T(8,128)(2,1)} %get-tuple-element.27), channel_id=1, source_target_pairs={{0,64},{1,2},{2,1},{3,4},{4,3},{5,6},{6,5},{7,71},{8,72},{9,10},{1... | collective-permute-start | bytes 245768 | tf_op jit(solution)/shard_map/ppermute | solution.py:366
  16.1 0.8 collective-permute-start.5
  16.9 1.2 %collective-permute-start.4 = (bf16[2,2,80,128]{3,2,1,0:T(8,128)(2,1)S(1)}, bf16[2,2,80,128]{3,2,1,0:T(8,128)(2,1)S(1)}, u32[]{:S(2)}, u32[]{:S(2)}) collective-permute-start(bf16[2,2,80,128]{3,2,1,0:T(8,128)(2,1)S(1)} %pad_maximum_fusion), channel_id=1, source_target_pairs={{0,1},{1,0},{2,3},{3,2},{4,5},{5,4},{6,7},{7,6},{8,9},{9,8},{10,11... | collective-permute-start | bytes 245768 | tf_op jit(solution)/shard_map/ppermute | solution.py:365
  18.1 2.2 %shard_map.93 = (bf16[240,400]{1,0:T(8,128)(2,1)}, bf16[240,400]{1,0:T(8,128)(2,1)}, bf16[400,240]{1,0:T(8,128)(2,1)}, bf16[400,240]{1,0:T(8,128)(2,1)}) custom-call(bf16[5,5,48,78]{3,2,1,0:T(8,128)(2,1)} %bitcast.30, bf16[5,5,48,78]{3,2,1,0:T(8,128)(2,1)} %bitcast.31), custom_call_target="tpu_custom_call" | custom-call | flops 4000000000 | bytes 1048576 | tf_op jit(solution)/shard_map/pallas_call | solution.py:288
  21.0 1.0 collective-permute-done.5.far_2
  22.6 22.7 %shard_map.94 = (bf16[64,96,128]{2,1,0:T(8,128)(2,1)}, bf16[96,128]{1,0:T(8,128)(2,1)}, bf16[96,128]{1,0:T(8,128)(2,1)}, bf16[2,96,128]{2,1,0:T(8,128)(2,1)}, bf...) custom-call(s32[11]{0:T(128)} %stack.65.rows_ref, bf16[2,64,80,128]{3,2,1,0:T(8,128)(2,1)} %get-tuple-element.23.main, ...), custom_call_target="tpu_custom_call" | custom-call | flops 30000001024 | bytes 1048576 | tf_op jit(solution)/shard_map/pallas_call | solution.py:288
  45.4 12.4 %all-to-all-start = ((bf16[128,16,128]{2,1,0:T(8,128)(2,1)}), bf16[128,16,128]{2,1,0:T(8,128)(2,1)S(1)}, u32[]{:S(2)}, u32[]{:S(2)}) async-start(bf16[128,16,128]{2,1,0:T(8,128)(2,1)} %bitcast.24), calls=%async_computation | async-start | bytes 1048576 | tf_op jit(solution)/shard_map/all_to_all | solution.py:392
  57.7 1.3 %collective-permute-start.6 = (bf16[96,128]{1,0:T(8,128)(2,1)}, bf16[96,128]{1,0:T(8,128)(2,1)S(1)}, u32[]{:S(2)}, u32[]{:S(2)}) collective-permute-start(bf16[96,128]{1,0:T(8,128)(2,1)} %get-tuple-element.31), channel_id=1, source_target_pairs={{8,0},{16,8},{24,16},{32,24},{40,32},{48,40},{56,48},{64,56},{72,6... | collective-permute-start | bytes 73736 | tf_op jit(solution)/shard_map/ppermute | solution.py:303
  59.0 2.2 %collective-permute-start.7 = (bf16[96,128]{1,0:T(8,128)(2,1)}, bf16[96,128]{1,0:T(8,128)(2,1)S(1)}, u32[]{:S(2)}, u32[]{:S(2)}) collective-permute-start(bf16[96,128]{1,0:T(8,128)(2,1)} %get-tuple-element.32), channel_id=1, source_target_pairs={{0,8},{8,16},{16,24},{24,32},{32,40},{40,48},{48,56},{56,64},{64,7... | collective-permute-start | bytes 73736 | tf_op jit(solution)/shard_map/ppermute | solution.py:304
  61.2 1.4 %collective-permute-start.8 = (bf16[2,96,128]{2,1,0:T(8,128)(2,1)}, bf16[2,96,128]{2,1,0:T(8,128)(2,1)S(1)}, u32[]{:S(2)}, u32[]{:S(2)}) collective-permute-start(bf16[2,96,128]{2,1,0:T(8,128)(2,1)} %get-tuple-element.33), channel_id=1, source_target_pairs={{0,1},{1,0},{2,3},{3,2},{4,5},{5,4},{6,7},{7,6},{8,9},{9,8},{10,11... | collective-permute-start | bytes 147464 | tf_op jit(solution)/shard_map/ppermute | solution.py:412
  62.6 2.7 %collective-permute-start.9 = (bf16[2,96,128]{2,1,0:T(8,128)(2,1)}, bf16[2,96,128]{2,1,0:T(8,128)(2,1)S(1)}, u32[]{:S(2)}, u32[]{:S(2)}) collective-permute-start(bf16[2,96,128]{2,1,0:T(8,128)(2,1)} %get-tuple-element.34), channel_id=1, source_target_pairs={{0,64},{1,2},{2,1},{3,4},{4,3},{5,6},{6,5},{7,71},{8,72},{9,10},{1... | collective-permute-start | bytes 147464 | tf_op jit(solution)/shard_map/ppermute | solution.py:413
  65.3 6.2 %all-to-all-done.got = bf16[128,16,128]{2,1,0:T(8,128)(2,1)S(1)} async-done(((bf16[128,16,128]{2,1,0:T(8,128)(2,1)}), bf16[128,16,128]{2,1,0:T(8,128)(2,1)S(1)}, u32[]{:S(2)}, u32[]{:S(2)}) %all-to-all-start) | async-done | bytes 524320 | tf_op jit(solution)/shard_map/all_to_all | solution.py:392
  72.3 2.0 %shard_map.97 = bf16[128,16,128]{2,1,0:T(8,128)(2,1)} custom-call(bf16[128,16,128]{2,1,0:T(8,128)(2,1)} %copy-done.1), custom_call_target="tpu_custom_call" | custom-call | flops 10000000000 | bytes 1048576 | tf_op jit(solution)/shard_map/pallas_call | solution.py:288
  74.3 4.8 %all-to-all-start.1 = ((bf16[128,16,128]{2,1,0:T(8,128)(2,1)}), bf16[128,16,128]{2,1,0:T(8,128)(2,1)S(1)}, u32[]{:S(2)}, u32[]{:S(2)}) async-start(bf16[128,16,128]{2,1,0:T(8,128)(2,1)} %shard_map.97), calls=%async_computation.1 | async-start | bytes 1048576 | tf_op jit(solution)/shard_map/all_to_all | solution.py:398
  79.1 3.1 %collective-permute-start.11 = (bf16[2,96,128]{2,1,0:T(8,128)(2,1)S(1)}, bf16[2,96,128]{2,1,0:T(8,128)(2,1)S(1)}, u32[]{:S(2)}, u32[]{:S(2)}) collective-permute-start(bf16[2,96,128]{2,1,0:T(8,128)(2,1)S(1)} %pad_maximum_fusion.1), channel_id=1, source_target_pairs={{0,64},{1,2},{2,1},{3,4},{4,3},{5,6},{6,5},{7,71},{8,72},{9,10},{1... | collective-permute-start | bytes 147464 | tf_op jit(solution)/shard_map/ppermute | solution.py:413
  82.2 3.2 %collective-permute-done.11.far_2 = bf16[2,96,128]{2,1,0:T(8,128)(2,1)S(1)} collective-permute-done((bf16[2,96,128]{2,1,0:T(8,128)(2,1)S(1)}, bf16[2,96,128]{2,1,0:T(8,128)(2,1)S(1)}, u32[]{:S(2)}, u32[]{:S(2)}) %collective-permute-start.11) | collective-permute-done | bytes 49184 | tf_op jit(solution)/shard_map/ppermute | solution.py:413
  85.5 2.8 %collective-permute-done.10.far_1 = bf16[2,96,128]{2,1,0:T(8,128)(2,1)S(1)} collective-permute-done((bf16[2,96,128]{2,1,0:T(8,128)(2,1)S(1)}, bf16[2,96,128]{2,1,0:T(8,128)(2,1)S(1)}, u32[]{:S(2)}, u32[]{:S(2)}) %collective-permute-start.10) | collective-permute-done | bytes 49184 | tf_op jit(solution)/shard_map/ppermute | solution.py:412
  88.9 8.6 %shard_map.96 = bf16[78,64,128]{2,1,0:T(8,128)(2,1)} custom-call(s32[11]{0:T(128)} %stack.65.rows_ref, bf16[64,96,128]{2,1,0:T(8,128)(2,1)} %get-tuple-element.30.both, bf16[96,128]{1,0:T(8,128)(2,1)} %copy-done.4, bf16[96,128]{1,0:T(8,128)(2,1)} %copy-done.5, bf16[2,96,128]{2,1,0:T(8,128)(2,1)} %copy-done.11, bf16[2,96,128]{2,1,0:T(8,128)(2,1)} %copy-done.12, ...), custom_call_target="tpu_custom_call" | custom-call | flops 2000000000 | bytes 1048576 | tf_op jit(solution)/shard_map/pallas_call | solution.py:288
  97.5 8.6 %shard_map.95 = bf16[78,64,128]{2,1,0:T(8,128)(2,1)} custom-call(s32[11]{0:T(128)} %stack.65.rows_ref, bf16[64,96,128]{2,1,0:T(8,128)(2,1)} %get-tuple-element.30.both, bf16[96,128]{1,0:T(8,128)(2,1)} %copy-done.4, bf16[96,128]{1,0:T(8,128)(2,1)} %copy-done.5, bf16[2,96,128]{2,1,0:T(8,128)(2,1)} %copy-done.11, bf16[2,96,128]{2,1,0:T(8,128)(2,1)} %copy-done.12, ...), custom_call_target="tpu_custom_call" | custom-call | flops 2000000000 | bytes 1048576 | tf_op jit(solution)/shard_map/pallas_call | solution.py:288
  106.8 2.4 %shard_map.98 = (f32[5,5,48,78]{3,2,1,0:T(8,128)}, f32[5,5,48,78]{3,2,1,0:T(8,128)}, f32[1,48]{1,0:T(1,128)}) custom-call(bf16[2048,128]{1,0:T(8,128)(2,1)} %bitcast.23), custom_call_target="tpu_custom_call" | custom-call | flops 20000000000 | bytes 1048576 | tf_op jit(solution)/shard_map/pallas_call | solution.py:288
  (45 shorter events, 4.3 us)
Async XLA Ops:
  7.8 8.2 %collective-permute-start = (bf16[2,80,128]{2,1,0:T(8,128)(2,1)}, bf16[2,80,128]{2,1,0:T(8,128)(2,1)S(1)}, u32[]{:S(2)}, u32[]{:S(2)}) collective-permute-start(bf16[2,80,128]{2,1,0:T(8,128)(2,1)} %get-tuple-element.24), channel_id=1, source_target_pairs={{8,0},{16,8},{24,16},{32,24},{40,32},{48,40},{56,48},{64,56},{72,6... | collective-permute-start | bytes 122888 | tf_op jit(solution)/shard_map/ppermute | solution.py:303
  9.2 6.8 %collective-permute-start.1 = (bf16[2,80,128]{2,1,0:T(8,128)(2,1)}, bf16[2,80,128]{2,1,0:T(8,128)(2,1)S(1)}, u32[]{:S(2)}, u32[]{:S(2)}) collective-permute-start(bf16[2,80,128]{2,1,0:T(8,128)(2,1)} %get-tuple-element.25), channel_id=1, source_target_pairs={{0,8},{8,16},{16,24},{24,32},{32,40},{40,48},{48,56},{56,64},{64,7... | collective-permute-start | bytes 122888 | tf_op jit(solution)/shard_map/ppermute | solution.py:304
  12.0 9.0 %collective-permute-start.2 = (bf16[2,2,80,128]{3,2,1,0:T(8,128)(2,1)}, bf16[2,2,80,128]{3,2,1,0:T(8,128)(2,1)S(1)}, u32[]{:S(2)}, u32[]{:S(2)}) collective-permute-start(bf16[2,2,80,128]{3,2,1,0:T(8,128)(2,1)} %get-tuple-element.26), channel_id=1, source_target_pairs={{0,1},{1,0},{2,3},{3,2},{4,5},{5,4},{6,7},{7,6},{8,9},{9,8},{10,11... | collective-permute-start | bytes 245768 | tf_op jit(solution)/shard_map/ppermute | solution.py:365
  13.1 7.9 %collective-permute-start.3 = (bf16[2,2,80,128]{3,2,1,0:T(8,128)(2,1)}, bf16[2,2,80,128]{3,2,1,0:T(8,128)(2,1)S(1)}, u32[]{:S(2)}, u32[]{:S(2)}) collective-permute-start(bf16[2,2,80,128]{3,2,1,0:T(8,128)(2,1)} %get-tuple-element.27), channel_id=1, source_target_pairs={{0,64},{1,2},{2,1},{3,4},{4,3},{5,6},{6,5},{7,71},{8,72},{9,10},{1... | collective-permute-start | bytes 245768 | tf_op jit(solution)/shard_map/ppermute | solution.py:366
  16.0 4.2 %copy-start.2 = (bf16[2,80,128]{2,1,0:T(8,128)(2,1)}, bf16[2,80,128]{2,1,0:T(8,128)(2,1)S(1)}, u32[]{:S(2)}) copy-start(bf16[2,80,128]{2,1,0:T(8,128)(2,1)S(1)} %collective-permute-done.right) | copy-start | bytes 122884
  16.0 4.2 %copy-start.3 = (bf16[2,80,128]{2,1,0:T(8,128)(2,1)}, bf16[2,80,128]{2,1,0:T(8,128)(2,1)S(1)}, u32[]{:S(2)}) copy-start(bf16[2,80,128]{2,1,0:T(8,128)(2,1)S(1)} %collective-permute-done.1.left) | copy-start | bytes 122884
  16.1 5.9 %collective-permute-start.5 = (bf16[2,2,80,128]{3,2,1,0:T(8,128)(2,1)S(1)}, bf16[2,2,80,128]{3,2,1,0:T(8,128)(2,1)S(1)}, u32[]{:S(2)}, u32[]{:S(2)}) collective-permute-start(bf16[2,2,80,128]{3,2,1,0:T(8,128)(2,1)S(1)} %pad_maximum_fusion), channel_id=1, source_target_pairs={{0,64},{1,2},{2,1},{3,4},{4,3},{5,6},{6,5},{7,71},{8,72},{9,10},{1... | collective-permute-start | bytes 245768 | tf_op jit(solution)/shard_map/ppermute | solution.py:366
  16.9 5.1 %collective-permute-start.4 = (bf16[2,2,80,128]{3,2,1,0:T(8,128)(2,1)S(1)}, bf16[2,2,80,128]{3,2,1,0:T(8,128)(2,1)S(1)}, u32[]{:S(2)}, u32[]{:S(2)}) collective-permute-start(bf16[2,2,80,128]{3,2,1,0:T(8,128)(2,1)S(1)} %pad_maximum_fusion), channel_id=1, source_target_pairs={{0,1},{1,0},{2,3},{3,2},{4,5},{5,4},{6,7},{7,6},{8,9},{9,8},{10,11... | collective-permute-start | bytes 245768 | tf_op jit(solution)/shard_map/ppermute | solution.py:365
  18.1 2.2 %copy-start.6 = (f32[48]{0:T(128)S(1)}, f32[48]{0:T(128)}, u32[]{:S(2)}) copy-start(f32[48]{0:T(128)} %param.7) | copy-start | bytes 580
  21.0 1.0 copy-start.7
  21.0 1.0 copy-start.8
  45.4 26.1 %all-to-all-start = ((bf16[128,16,128]{2,1,0:T(8,128)(2,1)}), bf16[128,16,128]{2,1,0:T(8,128)(2,1)S(1)}, u32[]{:S(2)}, u32[]{:S(2)}) async-start(bf16[128,16,128]{2,1,0:T(8,128)(2,1)} %bitcast.24), calls=%async_computation | async-start | bytes 1048576 | tf_op jit(solution)/shard_map/all_to_all | solution.py:392
  57.7 21.3 %collective-permute-start.6 = (bf16[96,128]{1,0:T(8,128)(2,1)}, bf16[96,128]{1,0:T(8,128)(2,1)S(1)}, u32[]{:S(2)}, u32[]{:S(2)}) collective-permute-start(bf16[96,128]{1,0:T(8,128)(2,1)} %get-tuple-element.31), channel_id=1, source_target_pairs={{8,0},{16,8},{24,16},{32,24},{40,32},{48,40},{56,48},{64,56},{72,6... | collective-permute-start | bytes 73736 | tf_op jit(solution)/shard_map/ppermute | solution.py:303
  59.0 20.0 %collective-permute-start.7 = (bf16[96,128]{1,0:T(8,128)(2,1)}, bf16[96,128]{1,0:T(8,128)(2,1)S(1)}, u32[]{:S(2)}, u32[]{:S(2)}) collective-permute-start(bf16[96,128]{1,0:T(8,128)(2,1)} %get-tuple-element.32), channel_id=1, source_target_pairs={{0,8},{8,16},{16,24},{24,32},{32,40},{40,48},{48,56},{56,64},{64,7... | collective-permute-start | bytes 73736 | tf_op jit(solution)/shard_map/ppermute | solution.py:304
  61.2 21.0 %collective-permute-start.8 = (bf16[2,96,128]{2,1,0:T(8,128)(2,1)}, bf16[2,96,128]{2,1,0:T(8,128)(2,1)S(1)}, u32[]{:S(2)}, u32[]{:S(2)}) collective-permute-start(bf16[2,96,128]{2,1,0:T(8,128)(2,1)} %get-tuple-element.33), channel_id=1, source_target_pairs={{0,1},{1,0},{2,3},{3,2},{4,5},{5,4},{6,7},{7,6},{8,9},{9,8},{10,11... | collective-permute-start | bytes 147464 | tf_op jit(solution)/shard_map/ppermute | solution.py:412
  62.6 19.6 %collective-permute-start.9 = (bf16[2,96,128]{2,1,0:T(8,128)(2,1)}, bf16[2,96,128]{2,1,0:T(8,128)(2,1)S(1)}, u32[]{:S(2)}, u32[]{:S(2)}) collective-permute-start(bf16[2,96,128]{2,1,0:T(8,128)(2,1)} %get-tuple-element.34), channel_id=1, source_target_pairs={{0,64},{1,2},{2,1},{3,4},{4,3},{5,6},{6,5},{7,71},{8,72},{9,10},{1... | collective-permute-start | bytes 147464 | tf_op jit(solution)/shard_map/ppermute | solution.py:413
  74.3 31.8 %all-to-all-start.1 = ((bf16[128,16,128]{2,1,0:T(8,128)(2,1)}), bf16[128,16,128]{2,1,0:T(8,128)(2,1)S(1)}, u32[]{:S(2)}, u32[]{:S(2)}) async-start(bf16[128,16,128]{2,1,0:T(8,128)(2,1)} %shard_map.97), calls=%async_computation.1 | async-start | bytes 1048576 | tf_op jit(solution)/shard_map/all_to_all | solution.py:398
  79.0 9.2 %copy-start.4 = (bf16[96,128]{1,0:T(8,128)(2,1)}, bf16[96,128]{1,0:T(8,128)(2,1)S(1)}, u32[]{:S(2)}) copy-start(bf16[96,128]{1,0:T(8,128)(2,1)S(1)} %collective-permute-done.6.right) | copy-start | bytes 73732
  79.1 9.2 %copy-start.5 = (bf16[96,128]{1,0:T(8,128)(2,1)}, bf16[96,128]{1,0:T(8,128)(2,1)S(1)}, u32[]{:S(2)}) copy-start(bf16[96,128]{1,0:T(8,128)(2,1)S(1)} %collective-permute-done.7.left) | copy-start | bytes 73732
  79.1 6.4 %collective-permute-start.11 = (bf16[2,96,128]{2,1,0:T(8,128)(2,1)S(1)}, bf16[2,96,128]{2,1,0:T(8,128)(2,1)S(1)}, u32[]{:S(2)}, u32[]{:S(2)}) collective-permute-start(bf16[2,96,128]{2,1,0:T(8,128)(2,1)S(1)} %pad_maximum_fusion.1), channel_id=1, source_target_pairs={{0,64},{1,2},{2,1},{3,4},{4,3},{5,6},{6,5},{7,71},{8,72},{9,10},{1... | collective-permute-start | bytes 147464 | tf_op jit(solution)/shard_map/ppermute | solution.py:413
  82.2 6.1 %collective-permute-start.10 = (bf16[2,96,128]{2,1,0:T(8,128)(2,1)S(1)}, bf16[2,96,128]{2,1,0:T(8,128)(2,1)S(1)}, u32[]{:S(2)}, u32[]{:S(2)}) collective-permute-start(bf16[2,96,128]{2,1,0:T(8,128)(2,1)S(1)} %pad_maximum_fusion.1), channel_id=1, source_target_pairs={{0,1},{1,0},{2,3},{3,2},{4,5},{5,4},{6,7},{7,6},{8,9},{9,8},{10,11... | collective-permute-start | bytes 147464 | tf_op jit(solution)/shard_map/ppermute | solution.py:412
  82.2 6.1 %copy-start.11 = (bf16[2,96,128]{2,1,0:T(8,128)(2,1)}, bf16[2,96,128]{2,1,0:T(8,128)(2,1)S(1)}, u32[]{:S(2)}) copy-start(bf16[2,96,128]{2,1,0:T(8,128)(2,1)S(1)} %collective-permute-done.8.rim_1) | copy-start | bytes 147460
  82.2 6.1 %copy-start.12 = (bf16[2,96,128]{2,1,0:T(8,128)(2,1)}, bf16[2,96,128]{2,1,0:T(8,128)(2,1)S(1)}, u32[]{:S(2)}) copy-start(bf16[2,96,128]{2,1,0:T(8,128)(2,1)S(1)} %collective-permute-done.9.rim_2) | copy-start | bytes 147460
  85.5 2.8 %copy-start.13 = (bf16[2,96,128]{2,1,0:T(8,128)(2,1)}, bf16[2,96,128]{2,1,0:T(8,128)(2,1)S(1)}, u32[]{:S(2)}) copy-start(bf16[2,96,128]{2,1,0:T(8,128)(2,1)S(1)} %collective-permute-done.11.far_2) | copy-start | bytes 147460
  (5 other events, 3.5 us)

commit v3 on v2

--- a/solution.py
+++ b/solution.py
@@ -39,7 +39,7 @@
         return low, high
 
     zero = jnp.zeros((channels, 128), BF)
-    return lax.fori_loop(0, rows, body, (zero, zero), unroll=16)
+    return lax.fori_loop(0, rows, body, (zero, zero), unroll=rows)
 
 
 def shifted(x, right, left, row):
@@ -67,7 +67,7 @@
         store_shifted(out, r + 2, read_main(r), right(), left(), r)
         return carry
 
-    lax.fori_loop(0, rows, body, 0, unroll=4)
+    lax.fori_loop(0, rows, body, 0, unroll=rows)
     for at, x, far_right, far_left, row in halo:
         store_shifted(out, at, x, far_right, far_left, row)
 
@@ -100,20 +100,68 @@
     return ref[pl.ds(i, 5)].reshape(5 * ref.shape[1], 128)
 
 
-def correlate(stack, grown, rows, flip=None):
-    inner = range(2, rows + 2)
-    right = jnp.concatenate([row_stack(grown, i) for i in inner], axis=1)
-    total = dot_nt(wide(stack, 2, rows), right)
-    outer = (0, 1, rows + 2, rows + 3)
+def correlate_outer(outer, grown, places, flip=None):
     pieces = []
-    for t, i in enumerate(outer):
+    for t, i in enumerate(places):
         piece = row_stack(grown, i)
         if flip is not None:
             turned = jnp.concatenate([grown[i + 4 - m] for m in range(5)], axis=0)
             piece = jnp.where(flip[t], turned, piece)
         pieces.append(piece)
-    left = jnp.concatenate([stack[i] for i in outer], axis=1)
-    return total + dot_nt(left, jnp.concatenate(pieces, axis=1))
+    return dot_nt(wide(outer, 0, 4), jnp.concatenate(pieces, axis=1))
+
+
+def shifted_alone(x):
+    lane = lanes_of(x.shape)
+    zero = jnp.zeros_like(x)
+    return [
+        jnp.where(lane < 2, zero, pltpu.roll(x, 2, 1)),
+        jnp.where(lane < 1, zero, pltpu.roll(x, 1, 1)),
+        x,
+        jnp.where(lane >= 127, zero, pltpu.roll(x, 127, 1)),
+        jnp.where(lane >= 126, zero, pltpu.roll(x, 126, 1)),
+    ]
+
+
+def four_slots(high, low):
+    source = lax.broadcasted_iota(jnp.int32, (256, 256), 0)
+    target = lax.broadcasted_iota(jnp.int32, (256, 256), 1)
+    side = (source >= 128).astype(jnp.int32)
+    place = 4 * ((source - 128 * side) // 2) + source % 2 + 2 * side
+    route = (target == place).astype(F32).astype(BF)
+    return dot(jnp.concatenate([high, low], axis=1), route).astype(BF)
+
+
+def edge_stack(right, left):
+    c = right.shape[0]
+    odd = lanes_of(right.shape) % 2 == 1
+    zero = jnp.zeros_like(right)
+    high = [zero, zero, zero, jnp.where(odd, pltpu.roll(right, 1, 1), zero), right]
+    low = [left, jnp.where(odd, zero, pltpu.roll(left, 127, 1)), zero, zero, zero]
+    return four_slots(jnp.concatenate(high, axis=0), jnp.concatenate(low, axis=0))
+
+
+def slid(x, rows):
+    by = 4 * rows
+    if by == 0:
+        return x
+    lane = lanes_of(x.shape)
+    inside = lane >= by if by > 0 else lane < 256 + by
+    return jnp.where(inside, pltpu.roll(x, by % 256, 1), jnp.zeros_like(x))
+
+
+def conv_alone(main, which, stack, weight, acc):
+    height = main.shape[1]
+
+    def body(r, carry):
+        for q, piece in enumerate(shifted_alone(main[which, r])):
+            stack[r, q * CP : (q + 1) * CP] = piece
+        return carry
+
+    lax.fori_loop(0, height, body, 0, unroll=8)
+    acc[...] = jnp.zeros(acc.shape, F32)
+    y = dot(weight[...], wide(stack, 0, height))
+    add_taps(acc, range(2, height + 2), y, acc.shape[1], height)
 
 
 def pack_kernel(rows_ref, field, cot, main, low, high, rim_1, rim_2):
@@ -130,7 +178,7 @@
             rim_2[which, t] = main[which, rows_ref[2 + t]]
 
 
-def halo_slabs(rows_ref, odd, rim_1, rim_2, far_1, far_2, which, lo, hi):
+def halo_slabs(rows_ref, odd, rim_1, rim_2, far_1, far_2, which):
     got = []
     for side in range(2):
         upper = side == 0
@@ -145,31 +193,45 @@
 def first_kernel_body(
     rows_ref, main, right, left, rim_1, rim_2, far_1, far_2, w_1, w_2, gain,
     both, low, high, out_1, out_2, flat,
-    stack_1, stack_2, acc_1, acc_2, grown_1, grown_2,
+    stack_1, stack_2, acc_1, acc_2, grown_1, grown_2, outer_1, outer_2, edge_1, edge_2, z_1, z_2,
 ):
-    height = main.shape[1]
+    height, _, _ = both.shape
     hid = gain.shape[0]
     odd = rows_ref[8] == 1
     top = rows_ref[9] == 1
     bottom = rows_ref[10] == 1
     flip = (top, top, bottom, bottom)
-    outer = (0, 1, height + 2, height + 3)
-    for which, stack in enumerate((stack_1, stack_2)):
-        halo = halo_slabs(rows_ref, odd, rim_1, rim_2, far_1, far_2, which, None, None)
-        fill_shifted(
-            stack, lambda r: main[which, r], lambda: right[which], lambda: left[which], height,
-            [(outer[t],) + halo[t] for t in range(4)],
-        )
-    conv_rows(acc_1, stack_1, w_1, hid, height)
-    conv_rows(acc_2, stack_2, w_2, hid, height, flip)
+    places = (0, 1, height + 2, height + 3)
     for grown in (grown_1, grown_2):
         grown[0:4] = jnp.zeros((4, hid, 128), BF)
         grown[height + 4 : height + 8] = jnp.zeros((4, hid, 128), BF)
-    spread = jnp.broadcast_to(gain[...], (hid, 128))
+    weights = (w_1, w_2)
+    for which, (outer, edge, z) in enumerate(((outer_1, edge_1, z_1), (outer_2, edge_2, z_2))):
+        halo = halo_slabs(rows_ref, odd, rim_1, rim_2, far_1, far_2, which)
+        for t in range(4):
+            store_shifted(outer, t, *halo[t])
+        edge[...] = edge_stack(right[which], left[which])
+        y = dot(weights[which][...], edge[...])
+        found = sum(slid(y[p * hid : (p + 1) * hid], 2 - p) for p in range(5))
+        z[0] = found[:, 0:128]
+        z[1] = found[:, 128:256]
+    conv_alone(main, 0, stack_1, w_1, acc_1)
+    conv_alone(main, 1, stack_2, w_2, acc_2)
+    for which, (outer, acc) in enumerate(((outer_1, acc_1), (outer_2, acc_2))):
+        y = dot(weights[which][...], wide(outer, 0, 4))
+        add_taps(acc, places, y, hid, 4, flip if which == 1 else None)
+    spread = gain[...]
+    lane = lanes_of((hid, 128))
+    side = jnp.logical_or(lane < 2, lane >= 126)
 
     def cells(r, total):
-        pre = acc_1[r + 4]
-        grad_act = acc_2[r + 4]
+        turn = lax.rem(382 - 4 * r, 128)
+
+        def with_edges(acc, z):
+            return acc[r + 4] + jnp.where(side, pltpu.roll(z[r // 32], turn, 1), 0.0)
+
+        pre = with_edges(acc_1, z_1)
+        grad_act = with_edges(acc_2, z_2)
         scale = lax.rsqrt(jnp.mean(pre * pre, axis=0, keepdims=True) + EPS)
         unit = pre * scale
         normed = unit * spread
@@ -185,23 +247,33 @@
         both[r, hid : 2 * hid] = grad_pre
         return total + grad_normed * unit
 
-    total = lax.fori_loop(0, height, cells, jnp.zeros((hid, 128), F32), unroll=4)
-    low[...], high[...] = edge_columns(lambda r: both[r], height, 2 * hid)
+    total = lax.fori_loop(0, height, cells, jnp.zeros((hid, 128), F32), unroll=16)
+    lows, highs = edge_columns(lambda r: both[r], height, 2 * hid)
+    low[...] = lows
+    high[...] = highs
     for t in range(2):
         out_1[t] = both[rows_ref[t]]
         out_2[t] = both[rows_ref[2 + t]]
     m = 5 * CP
+    slots = four_slots(highs, lows)
     spare = jnp.zeros((m, 256 - 5 * hid), F32)
-    for which, found in enumerate(
-        (correlate(stack_1, grown_1, height), correlate(stack_2, grown_2, height, flip))
+    for which, (stack, outer, edge, grown) in enumerate(
+        ((stack_1, outer_1, edge_1, grown_1), (stack_2, outer_2, edge_2, grown_2))
     ):
+        mine = slots[hid:] if which == 0 else slots[:hid]
+        mine = jnp.concatenate([slid(mine.astype(F32), 2 - k).astype(BF) for k in range(5)], axis=0)
+        found = dot_nt(edge[...], mine)
+        found = found + correlate_outer(outer, grown, places, flip if which == 1 else None)
+        right_side = jnp.concatenate([row_stack(grown, i + 2) for i in range(height)], axis=1)
+        found = found + dot_nt(wide(stack, 0, height), right_side)
         found = jnp.concatenate([found, spare], axis=1).astype(WIRE)
         flat[2 * which * m : (2 * which + 1) * m] = found[:, 0:128]
         flat[(2 * which + 1) * m : (2 * which + 2) * m] = found[:, 128:256]
     used = flat.shape[0] - 4 * m
     total = jnp.broadcast_to(jnp.sum(total, axis=1, keepdims=True), (hid, 128))
-    total = jnp.concatenate([total, jnp.zeros((used - hid, 128), F32)], axis=0)
-    flat[4 * m :] = total.astype(WIRE)
+    coarse = total.astype(WIRE)
+    total = jnp.where(lane < 64, coarse, (total - coarse.astype(F32)).astype(WIRE))
+    flat[4 * m :] = jnp.concatenate([total, jnp.zeros((used - hid, 128), WIRE)], axis=0)
 
 
 def second_kernel_body(
@@ -233,9 +305,10 @@
         out[:, rows, :] = (base[:, rows, :].astype(F32) + block).astype(BF)
 
 
-def weights_kernel(k_1, k_2, w_1, w_2, w_3, w_4):
+def weights_kernel(k_1, k_2, gain, w_1, w_2, w_3, w_4, spread):
     hid, channels = k_1.shape[2:]
     gap = jnp.zeros((hid, CP - channels), F32)
+    spread[...] = jnp.broadcast_to(gain[...], (128, hid)).T
 
     def plane(k, p, q):
         return jnp.concatenate([k[p, q].astype(F32), gap], axis=1)
@@ -249,7 +322,7 @@
         w_4[rows] = jnp.concatenate([plane(k_1, 4 - p, 4 - q) for q in range(5)], axis=0).T.astype(BF)
 
 
-def reduce_kernel(factor, got, out):
+def reduce_kernel(factor, rows_ref, got, out):
     devices = got.shape[0]
 
     def body(i, total):
@@ -257,6 +330,11 @@
 
     total = lax.fori_loop(0, devices, body, jnp.zeros(got.shape[1:], F32), unroll=16)
     mine = (total * factor).astype(BF)
+    whole = (total + pltpu.roll(total, 64, 1)) * factor
+    coarse = whole.astype(BF)
+    fine = (whole - coarse.astype(F32)).astype(BF)
+    pair = jnp.where(lanes_of(total.shape) < 64, coarse, fine)
+    mine = jnp.where(rows_ref[11] == 1, pair, mine)
     for i in range(devices):
         out[i] = mine
 
@@ -277,20 +355,24 @@
                     grad_1[4 - t, q] = piece
                 else:
                     grad_2[t, 4 - q] = piece
-    gain[...] = rows[4 * m : 4 * m + hid].astype(F32).T[0:1]
-
-
-def call(body, outs, scratch, args, flops, numbers=True):
-    vmem = pl.BlockSpec(memory_space=pltpu.VMEM)
-    in_specs = [vmem] * len(args)
+    pair = rows[4 * m : 4 * m + hid].astype(F32).T
+    gain[...] = pair[0:1] + pair[64:65]
+
+
+def call(body, outs, scratch, args, flops, numbers=True, far_in=(), far_out=()):
+    near = pl.BlockSpec(memory_space=pltpu.VMEM)
+    far = pl.BlockSpec(memory_space=pl.ANY)
+    in_specs = [far if i in far_in else near for i in range(len(args))]
     if numbers:
         in_specs[0] = pl.BlockSpec(memory_space=pltpu.SMEM)
     return pl.pallas_call(
         body,
         out_shape=[jax.ShapeDtypeStruct(s, t) for s, t in outs],
         in_specs=in_specs,
-        out_specs=[vmem] * len(outs),
-        scratch_shapes=[pltpu.VMEM(s, t) for s, t in scratch],
+        out_specs=[far if i in far_out else near for i in range(len(outs))],
+        scratch_shapes=[
+            pltpu.SemaphoreType.DMA(s) if t is None else pltpu.VMEM(s, t) for s, t in scratch
+        ],
         compiler_params=pltpu.CompilerParams(vmem_limit_bytes=VMEM),
         cost_estimate=pl.CostEstimate(flops=flops, bytes_accessed=1 << 20, transcendentals=0),
     )(*args)
@@ -320,7 +402,7 @@
     return one, two
 
 
-def place_numbers(height):
+def place_numbers(height, first, last_row, rows):
     lat = lax.axis_index("lat")
     last = lax.axis_size("lat") - 1
     odd = lat % 2
@@ -338,7 +420,9 @@
         jnp.where(bottom == 1, h - 1, 0),
         jnp.where(bottom == 1, h - 2, 1),
     ]
-    values = send_1 + send_2 + got + [odd, top, bottom]
+    begin = (lax.axis_index("lon") * lax.axis_size("lat") + lat) * rows
+    is_gain = jnp.logical_and(begin >= first, begin < last_row)
+    values = send_1 + send_2 + got + [odd, top, bottom, is_gain]
     return jnp.stack([jnp.asarray(v, jnp.int32) for v in values])
 
 
@@ -346,7 +430,8 @@
     channels, height, width = field.shape
     hid = norm_gain.shape[0]
     devices = lax.axis_size("lon") * lax.axis_size("lat")
-    numbers = place_numbers(height)
+    rows = -(-(4 * 5 * CP + hid) // (16 * devices)) * 16
+    numbers = place_numbers(height, 4 * 5 * CP, 4 * 5 * CP + hid, rows)
     one, two = row_routes(lax.axis_size("lon"), lax.axis_size("lat"))
     us = 10**9
 
@@ -365,15 +450,17 @@
     rim_1, far_1 = lax.ppermute((rim_1, sides), AXES, one)
     rim_2, far_2 = lax.ppermute((rim_2, sides), AXES, two)
 
-    w_1, w_2, w_3, w_4 = call(
+    w_1, w_2, w_3, w_4, spread = call(
         weights_kernel,
-        [((5 * hid, 5 * CP), BF)] * 2 + [((5 * CP, 5 * hid), BF)] * 2,
+        [((5 * hid, 5 * CP), BF)] * 2 + [((5 * CP, 5 * hid), BF)] * 2 + [((hid, 128), F32)],
         [],
-        (jnp.transpose(first_kernel, (2, 3, 0, 1)), jnp.transpose(second_kernel, (2, 3, 1, 0))),
+        (
+            jnp.transpose(first_kernel, (2, 3, 0, 1)), jnp.transpose(second_kernel, (2, 3, 1, 0)),
+            norm_gain[None],
+        ),
         4 * us,
         numbers=False,
     )
-    rows = -(-(4 * 5 * CP + hid) // (16 * devices)) * 16
     both, low, high, out_1, out_2, flat = call(
         first_kernel_body,
         [
@@ -381,20 +468,31 @@
             ((2, 2 * hid, 128), BF), ((2, 2 * hid, 128), BF), ((rows * devices, 128), WIRE),
         ],
         [
-            ((height + 4, 5 * CP, 128), BF), ((height + 4, 5 * CP, 128), BF),
+            ((height, 5 * CP, 128), BF), ((height, 5 * CP, 128), BF),
             ((height + 8, hid, 128), F32), ((height + 8, hid, 128), F32),
             ((height + 8, hid, 128), BF), ((height + 8, hid, 128), BF),
+            ((4, 5 * CP, 128), BF), ((4, 5 * CP, 128), BF),
+            ((5 * CP, 256), BF), ((5 * CP, 256), BF),
+            ((2, hid, 128), F32), ((2, hid, 128), F32),
         ],
-        (numbers, main, right, left, rim_1, rim_2, far_1, far_2, w_1, w_2, norm_gain[:, None]),
-        30 * us,
+        (
+            numbers, main, right, left, rim_1, rim_2, far_1, far_2, w_1, w_2, spread,
+        ),
+        12 * us,
     )
 
     got = lax.all_to_all(flat.reshape(devices, rows, 128), AXES, 0, 0)
+    right, left = exchange_columns(low, high)
+    sides = jnp.stack([right, left], axis=0)
+    out_1, far_1 = lax.ppermute((out_1, sides), AXES, one)
+    out_2, far_2 = lax.ppermute((out_2, sides), AXES, two)
     factor = (height * width * devices) ** -0.5
     (mine,) = call(
-        functools.partial(reduce_kernel, factor), [((devices, rows, 128), BF)], [], (got,), 10 * us,
-        numbers=False,
-    )
+        functools.partial(reduce_kernel, factor), [((devices, rows, 128), BF)], [],
+        (numbers, got),
+        10 * us,
+    )
+    mine, out_1, out_2, far_1, far_2 = lax.optimization_barrier((mine, out_1, out_2, far_1, far_2))
     summed = lax.all_to_all(mine, AXES, 0, 0).reshape(-1, 128)
     grad_1, grad_2, gain = call(
         unpack_kernel,
@@ -407,10 +505,6 @@
     grad_first = jnp.transpose(grad_1, (2, 3, 0, 1))
     grad_second = jnp.transpose(grad_2, (3, 2, 0, 1))
 
-    right, left = exchange_columns(low, high)
-    sides = jnp.stack([right, left], axis=0)
-    out_1, far_1 = lax.ppermute((out_1, sides), AXES, one)
-    out_2, far_2 = lax.ppermute((out_2, sides), AXES, two)
     results = []
     for which, weight, base in ((0, w_3, field), (1, w_4, cotangent)):
         results += call(

time: 110 us -> 94.2 us (0.86)
  Pallas kernels: 53 us -> 44.1 us
  waiting for transfers between devices: 13.2 us -> 5.45 us
  starting transfers between devices: 38 us -> 40.5 us
  local copies, waits for them, and re-layouts: 4.21 us -> 2.88 us
    pallas_call x7, Pallas kernels: 53 us -> 44.1 us  [call(): pl.pallas_call(body, out_shape=[jax.ShapeDtypeStruct(s, t) for s, t in ou...]
    all_to_all x1, waiting for transfers between devices: 6.17 us -> 1.25 us  [per_device(): got = lax.all_to_all(flat.reshape(devices, rows, 128), AXES, 0, 0)]
    ppermute x2, waiting for transfers between devices: 3.25 us -> 0.01 us  [per_device(): out_2, far_2 = lax.ppermute((out_2, sides), AXES, two)]
    all_to_all x1, starting transfers between devices: 4.75 us -> 7.74 us  [per_device(): summed = lax.all_to_all(mine, AXES, 0, 0).reshape(-1, 128)]
    ppermute x2, waiting for transfers between devices: 2.78 us -> 0.01 us  [per_device(): out_1, far_1 = lax.ppermute((out_1, sides), AXES, one)]
    ppermute x2, waiting for transfers between devices: 0.01 us -> 2.31 us  [exchange_columns(): right = lax.ppermute(low, 'lon', down)]
    unnamed x30 -> x28, local copies, waits for them, and re-layouts: 2.86 us -> 2.27 us
  transfers between devices with their start and end apart: 14 -> 14, of which waited for: 4 -> 4; matrix products, arithmetic and copies ran while one was open for 1% -> 0% of each run, Pallas kernels for 20% -> 19%
where the time goes in v3:
time: 94.2 us; the launch traced here: 93.8 us
  Pallas kernels  44.1 us (47%)
  starting transfers between devices  40.5 us (43%)
  waiting for transfers between devices  5.45 us (6%)
  local copies, waits for them, and re-layouts  2.88 us (3%)
    pallas_call x7, Pallas kernels, call(): pl.pallas_call(body, out_shape=[jax.ShapeDtypeStruct(s, t) for s, t in ou...  44.1 us
    all_to_all x1, starting transfers between devices, per_device(): got = lax.all_to_all(flat.reshape(devices, rows, 128), AXES, 0, 0)  12.4 us
    all_to_all x1, starting transfers between devices, per_device(): summed = lax.all_to_all(mine, AXES, 0, 0).reshape(-1, 128)  7.74 us
    ppermute x2, starting transfers between devices, per_device(): out_2, far_2 = lax.ppermute((out_2, sides), AXES, two)  5.46 us
    ppermute x2, starting transfers between devices, exchange_columns(): left = lax.ppermute(high, 'lon', up)  4.94 us
    ppermute x2, starting transfers between devices, per_device(): rim_2, far_2 = lax.ppermute((rim_2, sides), AXES, two)  3.71 us
    ppermute x2, starting transfers between devices, exchange_columns(): right = lax.ppermute(low, 'lon', down)  2.56 us
    ppermute x2, starting transfers between devices, per_device(): rim_1, far_1 = lax.ppermute((rim_1, sides), AXES, one)  2.32 us
  transfers between devices with their start and end apart: 14, of which 4 were waited for; matrix products, arithmetic and copies ran while one was open for 0% of the time, Pallas kernels for 19%

profile of v3, /device:TPU:1, one launch (start us, length us, event | category | flops | bytes accessed | tf_op | source)
XLA Modules:
  0.0 93.8 jit_solution(7452820866552023928)
XLA Ops:
  1.3 4.9 %shard_map.92 = (bf16[2,64,80,128]{3,2,1,0:T(8,128)(2,1)}, bf16[2,80,128]{2,1,0:T(8,128)(2,1)}, bf16[2,80,128]{2,1,0:T(8,128)(2,1)}, bf16[2,2,80,128]{3,2,1,0:T(8,128)(2,1)}, bf16[2,2,80,128]{3,2,1,0:T(8,128)(2,1)}) custom-call(s32[12]{0:T(128)} %stack.73.rows_ref, bf16[78,64,128]{2,1,0:T(8,128)(2,1)} %base.2, bf16[78,64,128]{2,1,0:T(8,128)(2,1)} %base.3), custom_call_target="tpu_custom_call" | custom-call | flops 5000000000 | bytes 1048576 | tf_op jit(solution)/shard_map/pallas_call | solution.py:368
  6.2 1.4 %collective-permute-start = (bf16[2,80,128]{2,1,0:T(8,128)(2,1)}, bf16[2,80,128]{2,1,0:T(8,128)(2,1)S(1)}, u32[]{:S(2)}, u32[]{:S(2)}) collective-permute-start(bf16[2,80,128]{2,1,0:T(8,128)(2,1)} %get-tuple-element.30), channel_id=1, source_target_pairs={{8,0},{16,8},{24,16},{32,24},{40,32},{48,40},{56,48},{64,56},{72,6... | collective-permute-start | bytes 122888 | tf_op jit(solution)/shard_map/ppermute | solution.py:385
  7.6 2.8 %collective-permute-start.1 = (bf16[2,80,128]{2,1,0:T(8,128)(2,1)}, bf16[2,80,128]{2,1,0:T(8,128)(2,1)S(1)}, u32[]{:S(2)}, u32[]{:S(2)}) collective-permute-start(bf16[2,80,128]{2,1,0:T(8,128)(2,1)} %get-tuple-element.31), channel_id=1, source_target_pairs={{0,8},{8,16},{16,24},{24,32},{32,40},{40,48},{48,56},{56,64},{64,7... | collective-permute-start | bytes 122888 | tf_op jit(solution)/shard_map/ppermute | solution.py:386
  10.4 1.1 %collective-permute-start.2 = (bf16[2,2,80,128]{3,2,1,0:T(8,128)(2,1)}, bf16[2,2,80,128]{3,2,1,0:T(8,128)(2,1)S(1)}, u32[]{:S(2)}, u32[]{:S(2)}) collective-permute-start(bf16[2,2,80,128]{3,2,1,0:T(8,128)(2,1)} %get-tuple-element.32), channel_id=1, source_target_pairs={{0,1},{1,0},{2,3},{3,2},{4,5},{5,4},{6,7},{7,6},{8,9},{9,8},{10,11... | collective-permute-start | bytes 245768 | tf_op jit(solution)/shard_map/ppermute | solution.py:450
  11.5 2.9 %collective-permute-start.3 = (bf16[2,2,80,128]{3,2,1,0:T(8,128)(2,1)}, bf16[2,2,80,128]{3,2,1,0:T(8,128)(2,1)S(1)}, u32[]{:S(2)}, u32[]{:S(2)}) collective-permute-start(bf16[2,2,80,128]{3,2,1,0:T(8,128)(2,1)} %get-tuple-element.33), channel_id=1, source_target_pairs={{0,64},{1,2},{2,1},{3,4},{4,3},{5,6},{6,5},{7,71},{8,72},{9,10},{1... | collective-permute-start | bytes 245768 | tf_op jit(solution)/shard_map/ppermute | solution.py:451
  14.4 0.8 collective-permute-start.5
  15.2 1.2 %collective-permute-start.4 = (bf16[2,2,80,128]{3,2,1,0:T(8,128)(2,1)S(1)}, bf16[2,2,80,128]{3,2,1,0:T(8,128)(2,1)S(1)}, u32[]{:S(2)}, u32[]{:S(2)}) collective-permute-start(bf16[2,2,80,128]{3,2,1,0:T(8,128)(2,1)S(1)} %pad_maximum_fusion), channel_id=1, source_target_pairs={{0,1},{1,0},{2,3},{3,2},{4,5},{5,4},{6,7},{7,6},{8,9},{9,8},{10,11... | collective-permute-start | bytes 245768 | tf_op jit(solution)/shard_map/ppermute | solution.py:450
  16.5 2.2 %shard_map.93 = (bf16[240,400]{1,0:T(8,128)(2,1)}, bf16[240,400]{1,0:T(8,128)(2,1)}, bf16[400,240]{1,0:T(8,128)(2,1)}, bf16[400,240]{1,0:T(8,128)(2,1)}, f32[48,128]{1,0:T(8,128)}) custom-call(bf16[5,5,48,78]{3,2,1,0:T(8,128)(2,1)} %bitcast.30, bf16[5,5,48,78]{3,2,1,0:T(8,128)(2,1)} %bitcast.31, f32[1,48]{1,0:T(1,128)} %bitcast.32), custom_call_target="tpu_custom_call" | custom-call | flops 4000000000 | bytes 1048576 | tf_op jit(solution)/shard_map/pallas_call | solution.py:368
  18.7 1.6 %collective-permute-done.5.far_2 = bf16[2,2,80,128]{3,2,1,0:T(8,128)(2,1)S(1)} collective-permute-done((bf16[2,2,80,128]{3,2,1,0:T(8,128)(2,1)S(1)}, bf16[2,2,80,128]{3,2,1,0:T(8,128)(2,1)S(1)}, u32[]{:S(2)}, u32[]{:S(2)}) %collective-permute-start.5) | collective-permute-done | bytes 81952 | tf_op jit(solution)/shard_map/ppermute | solution.py:451
  21.0 19.0 %shard_map.94 = (bf16[64,96,128]{2,1,0:T(8,128)(2,1)}, bf16[96,128]{1,0:T(8,128)(2,1)}, bf16[96,128]{1,0:T(8,128)(2,1)}, bf16[2,96,128]{2,1,0:T(8,128)(2,1)}, bf...) custom-call(s32[12]{0:T(128)} %stack.73.rows_ref, bf16[2,64,80,128]{3,2,1,0:T(8,128)(2,1)} %get-tuple-element.29.main, ...), custom_call_target="tpu_custom_call" | custom-call | flops 12000000000 | bytes 1048576 | tf_op jit(solution)/shard_map/pallas_call | solution.py:368
  40.0 12.4 %all-to-all-start = ((bf16[128,16,128]{2,1,0:T(8,128)(2,1)}), bf16[128,16,128]{2,1,0:T(8,128)(2,1)S(1)}, u32[]{:S(2)}, u32[]{:S(2)}) async-start(bf16[128,16,128]{2,1,0:T(8,128)(2,1)} %bitcast.24), calls=%async_computation | async-start | bytes 1048576 | tf_op jit(solution)/shard_map/all_to_all | solution.py:484
  52.4 1.1 %collective-permute-start.6 = (bf16[96,128]{1,0:T(8,128)(2,1)}, bf16[96,128]{1,0:T(8,128)(2,1)S(1)}, u32[]{:S(2)}, u32[]{:S(2)}) collective-permute-start(bf16[96,128]{1,0:T(8,128)(2,1)} %get-tuple-element.38), channel_id=1, source_target_pairs={{8,0},{16,8},{24,16},{32,24},{40,32},{48,40},{56,48},{64,56},{72,6... | collective-permute-start | bytes 73736 | tf_op jit(solution)/shard_map/ppermute | solution.py:385
  53.5 2.2 %collective-permute-start.7 = (bf16[96,128]{1,0:T(8,128)(2,1)}, bf16[96,128]{1,0:T(8,128)(2,1)S(1)}, u32[]{:S(2)}, u32[]{:S(2)}) collective-permute-start(bf16[96,128]{1,0:T(8,128)(2,1)} %get-tuple-element.39), channel_id=1, source_target_pairs={{0,8},{8,16},{16,24},{24,32},{32,40},{40,48},{48,56},{56,64},{64,7... | collective-permute-start | bytes 73736 | tf_op jit(solution)/shard_map/ppermute | solution.py:386
  55.7 1.4 %collective-permute-start.8 = (bf16[2,96,128]{2,1,0:T(8,128)(2,1)}, bf16[2,96,128]{2,1,0:T(8,128)(2,1)S(1)}, u32[]{:S(2)}, u32[]{:S(2)}) collective-permute-start(bf16[2,96,128]{2,1,0:T(8,128)(2,1)} %get-tuple-element.41), channel_id=1, source_target_pairs={{0,1},{1,0},{2,3},{3,2},{4,5},{5,4},{6,7},{7,6},{8,9},{9,8},{10,11... | collective-permute-start | bytes 147464 | tf_op jit(solution)/shard_map/ppermute | solution.py:487
  57.1 2.7 %collective-permute-start.9 = (bf16[2,96,128]{2,1,0:T(8,128)(2,1)}, bf16[2,96,128]{2,1,0:T(8,128)(2,1)S(1)}, u32[]{:S(2)}, u32[]{:S(2)}) collective-permute-start(bf16[2,96,128]{2,1,0:T(8,128)(2,1)} %get-tuple-element.42), channel_id=1, source_target_pairs={{0,64},{1,2},{2,1},{3,4},{4,3},{5,6},{6,5},{7,71},{8,72},{9,10},{1... | collective-permute-start | bytes 147464 | tf_op jit(solution)/shard_map/ppermute | solution.py:488
  59.8 2.3 %collective-permute-done.6.right = bf16[96,128]{1,0:T(8,128)(2,1)S(1)} collective-permute-done((bf16[96,128]{1,0:T(8,128)(2,1)}, bf16[96,128]{1,0:T(8,128)(2,1)S(1)}, u32[]{:S(2)}, u32[]{:S(2)}) %collective-permute-start.6) | collective-permute-done | bytes 24608 | tf_op jit(solution)/shard_map/ppermute | solution.py:385
  62.1 2.8 %collective-permute-start.11 = (bf16[2,96,128]{2,1,0:T(8,128)(2,1)S(1)}, bf16[2,96,128]{2,1,0:T(8,128)(2,1)S(1)}, u32[]{:S(2)}, u32[]{:S(2)}) collective-permute-start(bf16[2,96,128]{2,1,0:T(8,128)(2,1)S(1)} %pad_maximum_fusion.1), channel_id=1, source_target_pairs={{0,64},{1,2},{2,1},{3,4},{4,3},{5,6},{6,5},{7,71},{8,72},{9,10},{1... | collective-permute-start | bytes 147464 | tf_op jit(solution)/shard_map/ppermute | solution.py:488
  64.9 1.2 %all-to-all-done.got = bf16[128,16,128]{2,1,0:T(8,128)(2,1)S(1)} async-done(((bf16[128,16,128]{2,1,0:T(8,128)(2,1)}), bf16[128,16,128]{2,1,0:T(8,128)(2,1)S(1)}, u32[]{:S(2)}, u32[]{:S(2)}) %all-to-all-start) | async-done | bytes 524320 | tf_op jit(solution)/shard_map/all_to_all | solution.py:484
  66.1 0.8 copy-done
  66.9 2.1 %shard_map.95 = bf16[128,16,128]{2,1,0:T(8,128)(2,1)} custom-call(s32[12]{0:T(128)} %stack.73.rows_ref, bf16[128,16,128]{2,1,0:T(8,128)(2,1)} %copy-done), custom_call_target="tpu_custom_call" | custom-call | flops 10000000000 | bytes 1048576 | tf_op jit(solution)/shard_map/pallas_call | solution.py:368
  69.2 7.7 %all-to-all-start.1 = ((bf16[128,16,128]{2,1,0:T(8,128)(2,1)}), bf16[128,16,128]{2,1,0:T(8,128)(2,1)S(1)}, u32[]{:S(2)}, u32[]{:S(2)}) async-start(bf16[128,16,128]{2,1,0:T(8,128)(2,1)} %shard_map.95), calls=%async_computation.1 | async-start | bytes 1048576 | tf_op jit(solution)/shard_map/all_to_all | solution.py:496
  76.9 6.8 %shard_map.97 = bf16[78,64,128]{2,1,0:T(8,128)(2,1)} custom-call(s32[12]{0:T(128)} %stack.73.rows_ref, bf16[64,96,128]{2,1,0:T(8,128)(2,1)} %get-tuple-element.37.both, bf16[96,128]{1,0:T(8,128)(2,1)} %copy-done.4, bf16[96,128]{1,0:T(8,128)(2,1)} %copy-done.5, bf16[2,96,128]{2,1,0:T(8,128)(2,1)} %copy-done.10, bf16[2,96,128]{2,1,0:T(8,128)(2,1)} %copy-done.11, ...), custom_call_target="tpu_custom_call" | custom-call | flops 2000000000 | bytes 1048576 | tf_op jit(solution)/shard_map/pallas_call | solution.py:368
  83.7 6.7 %shard_map.96 = bf16[78,64,128]{2,1,0:T(8,128)(2,1)} custom-call(s32[12]{0:T(128)} %stack.73.rows_ref, bf16[64,96,128]{2,1,0:T(8,128)(2,1)} %get-tuple-element.37.both, bf16[96,128]{1,0:T(8,128)(2,1)} %copy-done.4, bf16[96,128]{1,0:T(8,128)(2,1)} %copy-done.5, bf16[2,96,128]{2,1,0:T(8,128)(2,1)} %copy-done.10, bf16[2,96,128]{2,1,0:T(8,128)(2,1)} %copy-done.11, ...), custom_call_target="tpu_custom_call" | custom-call | flops 2000000000 | bytes 1048576 | tf_op jit(solution)/shard_map/pallas_call | solution.py:368
  91.4 2.4 %shard_map.98 = (f32[5,5,48,78]{3,2,1,0:T(8,128)}, f32[5,5,48,78]{3,2,1,0:T(8,128)}, f32[1,48]{1,0:T(1,128)}) custom-call(bf16[2048,128]{1,0:T(8,128)(2,1)} %bitcast.25), custom_call_target="tpu_custom_call" | custom-call | flops 20000000000 | bytes 1048576 | tf_op jit(solution)/shard_map/pallas_call | solution.py:368
  (42 shorter events, 2.4 us)
Async XLA Ops:
  6.2 8.2 %collective-permute-start = (bf16[2,80,128]{2,1,0:T(8,128)(2,1)}, bf16[2,80,128]{2,1,0:T(8,128)(2,1)S(1)}, u32[]{:S(2)}, u32[]{:S(2)}) collective-permute-start(bf16[2,80,128]{2,1,0:T(8,128)(2,1)} %get-tuple-element.30), channel_id=1, source_target_pairs={{8,0},{16,8},{24,16},{32,24},{40,32},{48,40},{56,48},{64,56},{72,6... | collective-permute-start | bytes 122888 | tf_op jit(solution)/shard_map/ppermute | solution.py:385
  7.6 6.8 %collective-permute-start.1 = (bf16[2,80,128]{2,1,0:T(8,128)(2,1)}, bf16[2,80,128]{2,1,0:T(8,128)(2,1)S(1)}, u32[]{:S(2)}, u32[]{:S(2)}) collective-permute-start(bf16[2,80,128]{2,1,0:T(8,128)(2,1)} %get-tuple-element.31), channel_id=1, source_target_pairs={{0,8},{8,16},{16,24},{24,32},{32,40},{40,48},{48,56},{56,64},{64,7... | collective-permute-start | bytes 122888 | tf_op jit(solution)/shard_map/ppermute | solution.py:386
  10.4 8.3 %collective-permute-start.2 = (bf16[2,2,80,128]{3,2,1,0:T(8,128)(2,1)}, bf16[2,2,80,128]{3,2,1,0:T(8,128)(2,1)S(1)}, u32[]{:S(2)}, u32[]{:S(2)}) collective-permute-start(bf16[2,2,80,128]{3,2,1,0:T(8,128)(2,1)} %get-tuple-element.32), channel_id=1, source_target_pairs={{0,1},{1,0},{2,3},{3,2},{4,5},{5,4},{6,7},{7,6},{8,9},{9,8},{10,11... | collective-permute-start | bytes 245768 | tf_op jit(solution)/shard_map/ppermute | solution.py:450
  11.5 7.2 %collective-permute-start.3 = (bf16[2,2,80,128]{3,2,1,0:T(8,128)(2,1)}, bf16[2,2,80,128]{3,2,1,0:T(8,128)(2,1)S(1)}, u32[]{:S(2)}, u32[]{:S(2)}) collective-permute-start(bf16[2,2,80,128]{3,2,1,0:T(8,128)(2,1)} %get-tuple-element.33), channel_id=1, source_target_pairs={{0,64},{1,2},{2,1},{3,4},{4,3},{5,6},{6,5},{7,71},{8,72},{9,10},{1... | collective-permute-start | bytes 245768 | tf_op jit(solution)/shard_map/ppermute | solution.py:451
  14.4 4.3 %copy-start.2 = (bf16[2,80,128]{2,1,0:T(8,128)(2,1)}, bf16[2,80,128]{2,1,0:T(8,128)(2,1)S(1)}, u32[]{:S(2)}) copy-start(bf16[2,80,128]{2,1,0:T(8,128)(2,1)S(1)} %collective-permute-done.right) | copy-start | bytes 122884
  14.4 4.3 %copy-start.3 = (bf16[2,80,128]{2,1,0:T(8,128)(2,1)}, bf16[2,80,128]{2,1,0:T(8,128)(2,1)S(1)}, u32[]{:S(2)}) copy-start(bf16[2,80,128]{2,1,0:T(8,128)(2,1)S(1)} %collective-permute-done.1.left) | copy-start | bytes 122884
  14.4 5.9 %collective-permute-start.5 = (bf16[2,2,80,128]{3,2,1,0:T(8,128)(2,1)S(1)}, bf16[2,2,80,128]{3,2,1,0:T(8,128)(2,1)S(1)}, u32[]{:S(2)}, u32[]{:S(2)}) collective-permute-start(bf16[2,2,80,128]{3,2,1,0:T(8,128)(2,1)S(1)} %pad_maximum_fusion), channel_id=1, source_target_pairs={{0,64},{1,2},{2,1},{3,4},{4,3},{5,6},{6,5},{7,71},{8,72},{9,10},{1... | collective-permute-start | bytes 245768 | tf_op jit(solution)/shard_map/ppermute | solution.py:451
  15.2 5.1 %collective-permute-start.4 = (bf16[2,2,80,128]{3,2,1,0:T(8,128)(2,1)S(1)}, bf16[2,2,80,128]{3,2,1,0:T(8,128)(2,1)S(1)}, u32[]{:S(2)}, u32[]{:S(2)}) collective-permute-start(bf16[2,2,80,128]{3,2,1,0:T(8,128)(2,1)S(1)} %pad_maximum_fusion), channel_id=1, source_target_pairs={{0,1},{1,0},{2,3},{3,2},{4,5},{5,4},{6,7},{7,6},{8,9},{9,8},{10,11... | collective-permute-start | bytes 245768 | tf_op jit(solution)/shard_map/ppermute | solution.py:450
  18.7 1.7 %copy-start.6 = (bf16[2,2,80,128]{3,2,1,0:T(8,128)(2,1)}, bf16[2,2,80,128]{3,2,1,0:T(8,128)(2,1)S(1)}, u32[]{:S(2)}) copy-start(bf16[2,2,80,128]{3,2,1,0:T(8,128)(2,1)S(1)} %collective-permute-done.2.rim_1) | copy-start | bytes 245764
  18.7 1.7 %copy-start.7 = (bf16[2,2,80,128]{3,2,1,0:T(8,128)(2,1)}, bf16[2,2,80,128]{3,2,1,0:T(8,128)(2,1)S(1)}, u32[]{:S(2)}) copy-start(bf16[2,2,80,128]{3,2,1,0:T(8,128)(2,1)S(1)} %collective-permute-done.3.rim_2) | copy-start | bytes 245764
  40.0 26.1 %all-to-all-start = ((bf16[128,16,128]{2,1,0:T(8,128)(2,1)}), bf16[128,16,128]{2,1,0:T(8,128)(2,1)S(1)}, u32[]{:S(2)}, u32[]{:S(2)}) async-start(bf16[128,16,128]{2,1,0:T(8,128)(2,1)} %bitcast.24), calls=%async_computation | async-start | bytes 1048576 | tf_op jit(solution)/shard_map/all_to_all | solution.py:484
  52.4 9.7 %collective-permute-start.6 = (bf16[96,128]{1,0:T(8,128)(2,1)}, bf16[96,128]{1,0:T(8,128)(2,1)S(1)}, u32[]{:S(2)}, u32[]{:S(2)}) collective-permute-start(bf16[96,128]{1,0:T(8,128)(2,1)} %get-tuple-element.38), channel_id=1, source_target_pairs={{8,0},{16,8},{24,16},{32,24},{40,32},{48,40},{56,48},{64,56},{72,6... | collective-permute-start | bytes 73736 | tf_op jit(solution)/shard_map/ppermute | solution.py:385
  53.5 8.6 %collective-permute-start.7 = (bf16[96,128]{1,0:T(8,128)(2,1)}, bf16[96,128]{1,0:T(8,128)(2,1)S(1)}, u32[]{:S(2)}, u32[]{:S(2)}) collective-permute-start(bf16[96,128]{1,0:T(8,128)(2,1)} %get-tuple-element.39), channel_id=1, source_target_pairs={{0,8},{8,16},{16,24},{24,32},{32,40},{40,48},{48,56},{56,64},{64,7... | collective-permute-start | bytes 73736 | tf_op jit(solution)/shard_map/ppermute | solution.py:386
  55.7 13.4 %collective-permute-start.8 = (bf16[2,96,128]{2,1,0:T(8,128)(2,1)}, bf16[2,96,128]{2,1,0:T(8,128)(2,1)S(1)}, u32[]{:S(2)}, u32[]{:S(2)}) collective-permute-start(bf16[2,96,128]{2,1,0:T(8,128)(2,1)} %get-tuple-element.41), channel_id=1, source_target_pairs={{0,1},{1,0},{2,3},{3,2},{4,5},{5,4},{6,7},{7,6},{8,9},{9,8},{10,11... | collective-permute-start | bytes 147464 | tf_op jit(solution)/shard_map/ppermute | solution.py:487
  57.1 12.0 %collective-permute-start.9 = (bf16[2,96,128]{2,1,0:T(8,128)(2,1)}, bf16[2,96,128]{2,1,0:T(8,128)(2,1)S(1)}, u32[]{:S(2)}, u32[]{:S(2)}) collective-permute-start(bf16[2,96,128]{2,1,0:T(8,128)(2,1)} %get-tuple-element.42), channel_id=1, source_target_pairs={{0,64},{1,2},{2,1},{3,4},{4,3},{5,6},{6,5},{7,71},{8,72},{9,10},{1... | collective-permute-start | bytes 147464 | tf_op jit(solution)/shard_map/ppermute | solution.py:488
  62.1 7.0 %copy-start.4 = (bf16[96,128]{1,0:T(8,128)(2,1)}, bf16[96,128]{1,0:T(8,128)(2,1)S(1)}, u32[]{:S(2)}) copy-start(bf16[96,128]{1,0:T(8,128)(2,1)S(1)} %collective-permute-done.6.right) | copy-start | bytes 73732
  62.1 7.0 %copy-start.5 = (bf16[96,128]{1,0:T(8,128)(2,1)}, bf16[96,128]{1,0:T(8,128)(2,1)S(1)}, u32[]{:S(2)}) copy-start(bf16[96,128]{1,0:T(8,128)(2,1)S(1)} %collective-permute-done.7.left) | copy-start | bytes 73732
  62.1 7.0 %collective-permute-start.11 = (bf16[2,96,128]{2,1,0:T(8,128)(2,1)S(1)}, bf16[2,96,128]{2,1,0:T(8,128)(2,1)S(1)}, u32[]{:S(2)}, u32[]{:S(2)}) collective-permute-start(bf16[2,96,128]{2,1,0:T(8,128)(2,1)S(1)} %pad_maximum_fusion.1), channel_id=1, source_target_pairs={{0,64},{1,2},{2,1},{3,4},{4,3},{5,6},{6,5},{7,71},{8,72},{9,10},{1... | collective-permute-start | bytes 147464 | tf_op jit(solution)/shard_map/ppermute | solution.py:488
  64.9 4.3 %collective-permute-start.10 = (bf16[2,96,128]{2,1,0:T(8,128)(2,1)S(1)}, bf16[2,96,128]{2,1,0:T(8,128)(2,1)S(1)}, u32[]{:S(2)}, u32[]{:S(2)}) collective-permute-start(bf16[2,96,128]{2,1,0:T(8,128)(2,1)S(1)} %pad_maximum_fusion.1), channel_id=1, source_target_pairs={{0,1},{1,0},{2,3},{3,2},{4,5},{5,4},{6,7},{7,6},{8,9},{9,8},{10,11... | collective-permute-start | bytes 147464 | tf_op jit(solution)/shard_map/ppermute | solution.py:487
  69.1 7.8 %copy-start.10 = (bf16[2,96,128]{2,1,0:T(8,128)(2,1)}, bf16[2,96,128]{2,1,0:T(8,128)(2,1)S(1)}, u32[]{:S(2)}) copy-start(bf16[2,96,128]{2,1,0:T(8,128)(2,1)S(1)} %collective-permute-done.8.rim_1) | copy-start | bytes 147460
  69.1 7.8 %copy-start.11 = (bf16[2,96,128]{2,1,0:T(8,128)(2,1)}, bf16[2,96,128]{2,1,0:T(8,128)(2,1)S(1)}, u32[]{:S(2)}) copy-start(bf16[2,96,128]{2,1,0:T(8,128)(2,1)S(1)} %collective-permute-done.9.rim_2) | copy-start | bytes 147460
  69.1 7.8 %copy-start.12 = (bf16[2,96,128]{2,1,0:T(8,128)(2,1)}, bf16[2,96,128]{2,1,0:T(8,128)(2,1)S(1)}, u32[]{:S(2)}) copy-start(bf16[2,96,128]{2,1,0:T(8,128)(2,1)S(1)} %collective-permute-done.11.far_2) | copy-start | bytes 147460
  69.2 7.8 %copy-start.13 = (bf16[2,96,128]{2,1,0:T(8,128)(2,1)}, bf16[2,96,128]{2,1,0:T(8,128)(2,1)S(1)}, u32[]{:S(2)}) copy-start(bf16[2,96,128]{2,1,0:T(8,128)(2,1)S(1)} %collective-permute-done.10.far_1) | copy-start | bytes 147460
  69.2 21.5 %all-to-all-start.1 = ((bf16[128,16,128]{2,1,0:T(8,128)(2,1)}), bf16[128,16,128]{2,1,0:T(8,128)(2,1)S(1)}, u32[]{:S(2)}, u32[]{:S(2)}) async-start(bf16[128,16,128]{2,1,0:T(8,128)(2,1)} %shard_map.95), calls=%async_computation.1 | async-start | bytes 1048576 | tf_op jit(solution)/shard_map/all_to_all | solution.py:496
  (4 other events, 2.9 us)

commit v4 on v3

--- a/solution.py
+++ b/solution.py
@@ -178,20 +178,20 @@
             rim_2[which, t] = main[which, rows_ref[2 + t]]
 
 
-def halo_slabs(rows_ref, odd, rim_1, rim_2, far_1, far_2, which):
+def halo_slabs(rows_ref, odd, got_1, got_2, which):
     got = []
     for side in range(2):
         upper = side == 0
         pick = odd if upper else jnp.logical_not(odd)
-        far = [jnp.where(pick, far_1[which, k], far_2[which, k]) for k in range(2)]
+        far = [jnp.where(pick, got_1[which, 2 + k], got_2[which, 2 + k]) for k in range(2)]
         for t in range(2):
-            slab = jnp.where(pick, rim_1[which, t], rim_2[which, t])
+            slab = jnp.where(pick, got_1[which, t], got_2[which, t])
             got.append((slab, far[0], far[1], rows_ref[4 + 2 * side + t]))
     return got
 
 
 def first_kernel_body(
-    rows_ref, main, right, left, rim_1, rim_2, far_1, far_2, w_1, w_2, gain,
+    rows_ref, main, right, left, got_1, got_2, w_1, w_2, gain,
     both, low, high, out_1, out_2, flat,
     stack_1, stack_2, acc_1, acc_2, grown_1, grown_2, outer_1, outer_2, edge_1, edge_2, z_1, z_2,
 ):
@@ -207,7 +207,7 @@
         grown[height + 4 : height + 8] = jnp.zeros((4, hid, 128), BF)
     weights = (w_1, w_2)
     for which, (outer, edge, z) in enumerate(((outer_1, edge_1, z_1), (outer_2, edge_2, z_2))):
-        halo = halo_slabs(rows_ref, odd, rim_1, rim_2, far_1, far_2, which)
+        halo = halo_slabs(rows_ref, odd, got_1, got_2, which)
         for t in range(4):
             store_shifted(outer, t, *halo[t])
         edge[...] = edge_stack(right[which], left[which])
@@ -277,7 +277,7 @@
 
 
 def second_kernel_body(
-    which, rows_ref, both, right, left, rim_1, rim_2, far_1, far_2, weight, base, out, stack, acc,
+    which, rows_ref, both, right, left, got_1, got_2, weight, base, out, stack, acc,
 ):
     height = base.shape[1]
     channels = base.shape[0]
@@ -290,9 +290,9 @@
     halo = []
     for side in range(2):
         pick = odd if side == 0 else jnp.logical_not(odd)
-        far = [jnp.where(pick, far_1[k, part], far_2[k, part]) for k in range(2)]
+        far = [jnp.where(pick, got_1[2 + k, part], got_2[2 + k, part]) for k in range(2)]
         for t in range(2):
-            slab = jnp.where(pick, rim_1[t, part], rim_2[t, part])
+            slab = jnp.where(pick, got_1[t, part], got_2[t, part])
             halo.append((outer[2 * side + t], slab, far[0], far[1], rows_ref[4 + 2 * side + t]))
     fill_shifted(
         stack, lambda r: both[r, part], lambda: right[part], lambda: left[part], height, halo
@@ -447,8 +447,8 @@
     )
     right, left = exchange_columns(low, high)
     sides = jnp.stack([right, left], axis=1)
-    rim_1, far_1 = lax.ppermute((rim_1, sides), AXES, one)
-    rim_2, far_2 = lax.ppermute((rim_2, sides), AXES, two)
+    got_1 = lax.ppermute(jnp.concatenate([rim_1, sides], axis=1), AXES, one)
+    got_2 = lax.ppermute(jnp.concatenate([rim_2, sides], axis=1), AXES, two)
 
     w_1, w_2, w_3, w_4, spread = call(
         weights_kernel,
@@ -476,7 +476,7 @@
             ((2, hid, 128), F32), ((2, hid, 128), F32),
         ],
         (
-            numbers, main, right, left, rim_1, rim_2, far_1, far_2, w_1, w_2, spread,
+            numbers, main, right, left, got_1, got_2, w_1, w_2, spread,
         ),
         12 * us,
     )
@@ -484,15 +484,15 @@
     got = lax.all_to_all(flat.reshape(devices, rows, 128), AXES, 0, 0)
     right, left = exchange_columns(low, high)
     sides = jnp.stack([right, left], axis=0)
-    out_1, far_1 = lax.ppermute((out_1, sides), AXES, one)
-    out_2, far_2 = lax.ppermute((out_2, sides), AXES, two)
+    out_1 = lax.ppermute(jnp.concatenate([out_1, sides], axis=0), AXES, one)
+    out_2 = lax.ppermute(jnp.concatenate([out_2, sides], axis=0), AXES, two)
     factor = (height * width * devices) ** -0.5
     (mine,) = call(
         functools.partial(reduce_kernel, factor), [((devices, rows, 128), BF)], [],
         (numbers, got),
         10 * us,
     )
-    mine, out_1, out_2, far_1, far_2 = lax.optimization_barrier((mine, out_1, out_2, far_1, far_2))
+    mine, out_1, out_2 = lax.optimization_barrier((mine, out_1, out_2))
     summed = lax.all_to_all(mine, AXES, 0, 0).reshape(-1, 128)
     grad_1, grad_2, gain = call(
         unpack_kernel,
@@ -511,7 +511,7 @@
             functools.partial(second_kernel_body, which),
             [(field.shape, BF)],
             [((height + 4, 5 * hid, 128), BF), ((height + 8, CP, 128), F32)],
-            (numbers, both, right, left, out_1, out_2, far_1, far_2, weight, base),
+            (numbers, both, right, left, out_1, out_2, weight, base),
             2 * us,
         )
     return results[0], results[1], grad_first, grad_second, gain.reshape(hid)

time: 94.2 us -> 98.4 us (1.045)
  waiting for transfers between devices: 5.45 us -> 12.4 us
  starting transfers between devices: 40.5 us -> 35.8 us
  other arithmetic: 0.02 us -> 1.84 us
    ppermute x8 -> x4, starting transfers between devices: 12.9 us -> 5.69 us  [the longest x1 2.79 us: per_device(): out_2 = lax.ppermute(jnp.concatenate([out_2, sides], axis=0), AXES, two)]
    ppermute x2, waiting for transfers between devices: 2.31 us -> 8.14 us  [exchange_columns(): right = lax.ppermute(low, 'lon', down)]
    concatenate x0 -> x2, other arithmetic: none -> 1.84 us  [the longest x1 0.98 us: per_device(): got_2 = lax.ppermute(jnp.concatenate([rim_2, sides], axis=1), AXES, two)]
    ppermute x2, waiting for transfers between devices: 0.01 us -> 1.31 us  [exchange_columns(): left = lax.ppermute(high, 'lon', up)]
    all_to_all x1, starting transfers between devices: 7.74 us -> 9.03 us  [per_device(): summed = lax.all_to_all(mine, AXES, 0, 0).reshape(-1, 128)]
    all_to_all x1, starting transfers between devices: 12.4 us -> 13.6 us  [per_device(): got = lax.all_to_all(flat.reshape(devices, rows, 128), AXES, 0, 0)]
    ppermute x8 -> x4, waiting for transfers between devices: 1.65 us -> 2.24 us  [the longest x1 1.16 us: per_device(): got_1 = lax.ppermute(jnp.concatenate([rim_1, sides], axis=1), AXES, one)]
    unnamed x28 -> x20, local copies, waits for them, and re-layouts: 2.27 us -> 2.29 us
  transfers between devices with their start and end apart: 14 -> 10, of which waited for: 4 -> 7; matrix products, arithmetic and copies ran while one was open for 0% -> 1% of each run, Pallas kernels for 19% -> 18%
where the time goes in v4:
time: 98.4 us; the launch traced here: 97.9 us
  Pallas kernels  44.2 us (45%)
  starting transfers between devices  35.8 us (36%)
  waiting for transfers between devices  12.4 us (13%)
  local copies, waits for them, and re-layouts  2.93 us (3%)
  other arithmetic  1.84 us (2%)
    pallas_call x7, Pallas kernels, call(): pl.pallas_call(body, out_shape=[jax.ShapeDtypeStruct(s, t) for s, t in ou...  44.2 us
    all_to_all x1, starting transfers between devices, per_device(): got = lax.all_to_all(flat.reshape(devices, rows, 128), AXES, 0, 0)  13.6 us
    all_to_all x1, starting transfers between devices, per_device(): summed = lax.all_to_all(mine, AXES, 0, 0).reshape(-1, 128)  9.03 us
    ppermute x2, waiting for transfers between devices, exchange_columns(): right = lax.ppermute(low, 'lon', down)  8.14 us
    ppermute x2, starting transfers between devices, exchange_columns(): left = lax.ppermute(high, 'lon', up)  4.94 us
    ppermute x1, starting transfers between devices, per_device(): out_2 = lax.ppermute(jnp.concatenate([out_2, sides], axis=0), AXES, two)  2.79 us
    ppermute x2, starting transfers between devices, exchange_columns(): right = lax.ppermute(low, 'lon', down)  2.56 us
    unnamed x20, local copies, waits for them, and re-layouts  2.29 us
  transfers between devices with their start and end apart: 10, of which 7 were waited for; matrix products, arithmetic and copies ran while one was open for 1% of the time, Pallas kernels for 18%

profile of v4, /device:TPU:1, one launch (start us, length us, event | category | flops | bytes accessed | tf_op | source)
XLA Modules:
  0.0 97.9 jit_solution(2411339942044227278)
XLA Ops:
  1.3 4.9 %shard_map.92 = (bf16[2,64,80,128]{3,2,1,0:T(8,128)(2,1)}, bf16[2,80,128]{2,1,0:T(8,128)(2,1)}, bf16[2,80,128]{2,1,0:T(8,128)(2,1)}, bf16[2,2,80,128]{3,2,1,0:T(8,128)(2,1)}, bf16[2,2,80,128]{3,2,1,0:T(8,128)(2,1)}) custom-call(s32[12]{0:T(128)} %stack.69.rows_ref, bf16[78,64,128]{2,1,0:T(8,128)(2,1)} %base.2, bf16[78,64,128]{2,1,0:T(8,128)(2,1)} %base.3), custom_call_target="tpu_custom_call" | custom-call | flops 5000000000 | bytes 1048576 | tf_op jit(solution)/shard_map/pallas_call | solution.py:368
  6.2 1.4 %collective-permute-start = (bf16[2,80,128]{2,1,0:T(8,128)(2,1)}, bf16[2,80,128]{2,1,0:T(8,128)(2,1)S(1)}, u32[]{:S(2)}, u32[]{:S(2)}) collective-permute-start(bf16[2,80,128]{2,1,0:T(8,128)(2,1)} %get-tuple-element.28), channel_id=1, source_target_pairs={{8,0},{16,8},{24,16},{32,24},{40,32},{48,40},{56,48},{64,56},{72,6... | collective-permute-start | bytes 122888 | tf_op jit(solution)/shard_map/ppermute | solution.py:385
  7.6 2.8 %collective-permute-start.1 = (bf16[2,80,128]{2,1,0:T(8,128)(2,1)}, bf16[2,80,128]{2,1,0:T(8,128)(2,1)S(1)}, u32[]{:S(2)}, u32[]{:S(2)}) collective-permute-start(bf16[2,80,128]{2,1,0:T(8,128)(2,1)} %get-tuple-element.29), channel_id=1, source_target_pairs={{0,8},{8,16},{16,24},{24,32},{32,40},{40,48},{48,56},{56,64},{64,7... | collective-permute-start | bytes 122888 | tf_op jit(solution)/shard_map/ppermute | solution.py:386
  10.4 1.8 %collective-permute-done.right = bf16[2,80,128]{2,1,0:T(8,128)(2,1)S(1)} collective-permute-done((bf16[2,80,128]{2,1,0:T(8,128)(2,1)}, bf16[2,80,128]{2,1,0:T(8,128)(2,1)S(1)}, u32[]{:S(2)}, u32[]{:S(2)}) %collective-permute-start) | collective-permute-done | bytes 40992 | tf_op jit(solution)/shard_map/ppermute | solution.py:385
  12.2 1.3 %collective-permute-done.1.left = bf16[2,80,128]{2,1,0:T(8,128)(2,1)S(1)} collective-permute-done((bf16[2,80,128]{2,1,0:T(8,128)(2,1)}, bf16[2,80,128]{2,1,0:T(8,128)(2,1)S(1)}, u32[]{:S(2)}, u32[]{:S(2)}) %collective-permute-start.1) | collective-permute-done | bytes 40992 | tf_op jit(solution)/shard_map/ppermute | solution.py:386
  13.6 1.0 pad_maximum_fusion
  14.5 1.7 %collective-permute-start.3 = (bf16[2,4,80,128]{3,2,1,0:T(8,128)(2,1)S(1)}, bf16[2,4,80,128]{3,2,1,0:T(8,128)(2,1)S(1)}, u32[]{:S(2)}, u32[]{:S(2)}) collective-permute-start(bf16[2,4,80,128]{3,2,1,0:T(8,128)(2,1)S(1)} %get-tuple-element.49), channel_id=1, source_target_pairs={{0,64},{1,2},{2,1},{3,4},{4,3},{5,6},{6,5},{7,71},{8,72},{9,10},{1... | collective-permute-start | bytes 491528 | tf_op jit(solution)/shard_map/ppermute | solution.py:451
  16.2 1.2 %collective-permute-start.2 = (bf16[2,4,80,128]{3,2,1,0:T(8,128)(2,1)S(1)}, bf16[2,4,80,128]{3,2,1,0:T(8,128)(2,1)S(1)}, u32[]{:S(2)}, u32[]{:S(2)}) collective-permute-start(bf16[2,4,80,128]{3,2,1,0:T(8,128)(2,1)S(1)} %get-tuple-element.50), channel_id=1, source_target_pairs={{0,1},{1,0},{2,3},{3,2},{4,5},{5,4},{6,7},{7,6},{8,9},{9,8},{10,11... | collective-permute-start | bytes 491528 | tf_op jit(solution)/shard_map/ppermute | solution.py:450
  17.4 2.2 %shard_map.93 = (bf16[240,400]{1,0:T(8,128)(2,1)}, bf16[240,400]{1,0:T(8,128)(2,1)}, bf16[400,240]{1,0:T(8,128)(2,1)}, bf16[400,240]{1,0:T(8,128)(2,1)}, f32[48,128]{1,0:T(8,128)}) custom-call(bf16[5,5,48,78]{3,2,1,0:T(8,128)(2,1)} %bitcast.30, bf16[5,5,48,78]{3,2,1,0:T(8,128)(2,1)} %bitcast.31, f32[1,48]{1,0:T(1,128)} %bitcast.32), custom_call_target="tpu_custom_call" | custom-call | flops 4000000000 | bytes 1048576 | tf_op jit(solution)/shard_map/pallas_call | solution.py:368
  19.7 1.0 %collective-permute-done.3.got_2 = bf16[2,4,80,128]{3,2,1,0:T(8,128)(2,1)S(1)} collective-permute-done((bf16[2,4,80,128]{3,2,1,0:T(8,128)(2,1)S(1)}, bf16[2,4,80,128]{3,2,1,0:T(8,128)(2,1)S(1)}, u32[]{:S(2)}, u32[]{:S(2)}) %collective-permute-start.3) | collective-permute-done | bytes 163872 | tf_op jit(solution)/shard_map/ppermute | solution.py:451
  20.7 1.2 %collective-permute-done.2.got_1 = bf16[2,4,80,128]{3,2,1,0:T(8,128)(2,1)S(1)} collective-permute-done((bf16[2,4,80,128]{3,2,1,0:T(8,128)(2,1)S(1)}, bf16[2,4,80,128]{3,2,1,0:T(8,128)(2,1)S(1)}, u32[]{:S(2)}, u32[]{:S(2)}) %collective-permute-start.2) | collective-permute-done | bytes 163872 | tf_op jit(solution)/shard_map/ppermute | solution.py:450
  22.6 19.0 %shard_map.94 = (bf16[64,96,128]{2,1,0:T(8,128)(2,1)}, bf16[96,128]{1,0:T(8,128)(2,1)}, bf16[96,128]{1,0:T(8,128)(2,1)}, bf16[2,96,128]{2,1,0:T(8,128)(2,1)}, bf...) custom-call(s32[12]{0:T(128)} %stack.69.rows_ref, bf16[2,64,80,128]{3,2,1,0:T(8,128)(2,1)} %get-tuple-element.27.main, ...), custom_call_target="tpu_custom_call" | custom-call | flops 12000000000 | bytes 1048576 | tf_op jit(solution)/shard_map/pallas_call | solution.py:368
  41.6 13.6 %all-to-all-start = ((bf16[128,16,128]{2,1,0:T(8,128)(2,1)}), bf16[128,16,128]{2,1,0:T(8,128)(2,1)S(1)}, u32[]{:S(2)}, u32[]{:S(2)}) async-start(bf16[128,16,128]{2,1,0:T(8,128)(2,1)} %bitcast.24), calls=%async_computation | async-start | bytes 1048576 | tf_op jit(solution)/shard_map/all_to_all | solution.py:484
  55.2 1.1 %collective-permute-start.4 = (bf16[96,128]{1,0:T(8,128)(2,1)}, bf16[96,128]{1,0:T(8,128)(2,1)S(1)}, u32[]{:S(2)}, u32[]{:S(2)}) collective-permute-start(bf16[96,128]{1,0:T(8,128)(2,1)} %get-tuple-element.36), channel_id=1, source_target_pairs={{8,0},{16,8},{24,16},{32,24},{40,32},{48,40},{56,48},{64,56},{72,6... | collective-permute-start | bytes 73736 | tf_op jit(solution)/shard_map/ppermute | solution.py:385
  56.3 2.2 %collective-permute-start.5 = (bf16[96,128]{1,0:T(8,128)(2,1)}, bf16[96,128]{1,0:T(8,128)(2,1)S(1)}, u32[]{:S(2)}, u32[]{:S(2)}) collective-permute-start(bf16[96,128]{1,0:T(8,128)(2,1)} %get-tuple-element.37), channel_id=1, source_target_pairs={{0,8},{8,16},{16,24},{24,32},{32,40},{40,48},{48,56},{56,64},{64,7... | collective-permute-start | bytes 73736 | tf_op jit(solution)/shard_map/ppermute | solution.py:386
  58.5 6.3 %collective-permute-done.4.right = bf16[96,128]{1,0:T(8,128)(2,1)S(1)} collective-permute-done((bf16[96,128]{1,0:T(8,128)(2,1)}, bf16[96,128]{1,0:T(8,128)(2,1)S(1)}, u32[]{:S(2)}, u32[]{:S(2)}) %collective-permute-start.4) | collective-permute-done | bytes 24608 | tf_op jit(solution)/shard_map/ppermute | solution.py:385
  64.8 0.9 pad_maximum_fusion.4
  65.7 2.8 %collective-permute-start.7 = (bf16[4,96,128]{2,1,0:T(8,128)(2,1)S(1)}, bf16[4,96,128]{2,1,0:T(8,128)(2,1)S(1)}, u32[]{:S(2)}, u32[]{:S(2)}) collective-permute-start(bf16[4,96,128]{2,1,0:T(8,128)(2,1)S(1)} %get-tuple-element.51), channel_id=1, source_target_pairs={{0,64},{1,2},{2,1},{3,4},{4,3},{5,6},{6,5},{7,71},{8,72},{9,10},{1... | collective-permute-start | bytes 294920 | tf_op jit(solution)/shard_map/ppermute | solution.py:488
  69.7 2.1 %shard_map.95 = bf16[128,16,128]{2,1,0:T(8,128)(2,1)} custom-call(s32[12]{0:T(128)} %stack.69.rows_ref, bf16[128,16,128]{2,1,0:T(8,128)(2,1)} %copy-done), custom_call_target="tpu_custom_call" | custom-call | flops 10000000000 | bytes 1048576 | tf_op jit(solution)/shard_map/pallas_call | solution.py:368
  71.9 9.0 %all-to-all-start.1 = ((bf16[128,16,128]{2,1,0:T(8,128)(2,1)}), bf16[128,16,128]{2,1,0:T(8,128)(2,1)S(1)}, u32[]{:S(2)}, u32[]{:S(2)}) async-start(bf16[128,16,128]{2,1,0:T(8,128)(2,1)} %shard_map.95), calls=%async_computation.1 | async-start | bytes 1048576 | tf_op jit(solution)/shard_map/all_to_all | solution.py:496
  81.0 6.8 %shard_map.97 = bf16[78,64,128]{2,1,0:T(8,128)(2,1)} custom-call(s32[12]{0:T(128)} %stack.69.rows_ref, bf16[64,96,128]{2,1,0:T(8,128)(2,1)} %get-tuple-element.35.both, bf16[96,128]{1,0:T(8,128)(2,1)} %copy-done.4, bf16[96,128]{1,0:T(8,128)(2,1)} %copy-done.5, bf16[4,96,128]{2,1,0:T(8,128)(2,1)} %copy-done.9, bf16[4,96,128]{2,1,0:T(8,128)(2,1)} %copy-done.8, ...), custom_call_target="tpu_custom_call" | custom-call | flops 2000000000 | bytes 1048576 | tf_op jit(solution)/shard_map/pallas_call | solution.py:368
  87.8 6.7 %shard_map.96 = bf16[78,64,128]{2,1,0:T(8,128)(2,1)} custom-call(s32[12]{0:T(128)} %stack.69.rows_ref, bf16[64,96,128]{2,1,0:T(8,128)(2,1)} %get-tuple-element.35.both, bf16[96,128]{1,0:T(8,128)(2,1)} %copy-done.4, bf16[96,128]{1,0:T(8,128)(2,1)} %copy-done.5, bf16[4,96,128]{2,1,0:T(8,128)(2,1)} %copy-done.9, bf16[4,96,128]{2,1,0:T(8,128)(2,1)} %copy-done.8, ...), custom_call_target="tpu_custom_call" | custom-call | flops 2000000000 | bytes 1048576 | tf_op jit(solution)/shard_map/pallas_call | solution.py:368
  94.7 0.8 copy-done.1
  95.5 2.4 %shard_map.98 = (f32[5,5,48,78]{3,2,1,0:T(8,128)}, f32[5,5,48,78]{3,2,1,0:T(8,128)}, f32[1,48]{1,0:T(1,128)}) custom-call(bf16[2048,128]{1,0:T(8,128)(2,1)} %bitcast.25), custom_call_target="tpu_custom_call" | custom-call | flops 20000000000 | bytes 1048576 | tf_op jit(solution)/shard_map/pallas_call | solution.py:368
  (26 shorter events, 2.9 us)
Async XLA Ops:
  6.2 6.0 %collective-permute-start = (bf16[2,80,128]{2,1,0:T(8,128)(2,1)}, bf16[2,80,128]{2,1,0:T(8,128)(2,1)S(1)}, u32[]{:S(2)}, u32[]{:S(2)}) collective-permute-start(bf16[2,80,128]{2,1,0:T(8,128)(2,1)} %get-tuple-element.28), channel_id=1, source_target_pairs={{8,0},{16,8},{24,16},{32,24},{40,32},{48,40},{56,48},{64,56},{72,6... | collective-permute-start | bytes 122888 | tf_op jit(solution)/shard_map/ppermute | solution.py:385
  7.6 5.9 %collective-permute-start.1 = (bf16[2,80,128]{2,1,0:T(8,128)(2,1)}, bf16[2,80,128]{2,1,0:T(8,128)(2,1)S(1)}, u32[]{:S(2)}, u32[]{:S(2)}) collective-permute-start(bf16[2,80,128]{2,1,0:T(8,128)(2,1)} %get-tuple-element.29), channel_id=1, source_target_pairs={{0,8},{8,16},{16,24},{24,32},{32,40},{40,48},{48,56},{56,64},{64,7... | collective-permute-start | bytes 122888 | tf_op jit(solution)/shard_map/ppermute | solution.py:386
  12.2 7.4 %copy-start.2 = (bf16[2,80,128]{2,1,0:T(8,128)(2,1)}, bf16[2,80,128]{2,1,0:T(8,128)(2,1)S(1)}, u32[]{:S(2)}) copy-start(bf16[2,80,128]{2,1,0:T(8,128)(2,1)S(1)} %collective-permute-done.right) | copy-start | bytes 122884
  13.6 6.1 %copy-start.3 = (bf16[2,80,128]{2,1,0:T(8,128)(2,1)}, bf16[2,80,128]{2,1,0:T(8,128)(2,1)S(1)}, u32[]{:S(2)}) copy-start(bf16[2,80,128]{2,1,0:T(8,128)(2,1)S(1)} %collective-permute-done.1.left) | copy-start | bytes 122884
  14.5 6.2 %collective-permute-start.3 = (bf16[2,4,80,128]{3,2,1,0:T(8,128)(2,1)S(1)}, bf16[2,4,80,128]{3,2,1,0:T(8,128)(2,1)S(1)}, u32[]{:S(2)}, u32[]{:S(2)}) collective-permute-start(bf16[2,4,80,128]{3,2,1,0:T(8,128)(2,1)S(1)} %get-tuple-element.49), channel_id=1, source_target_pairs={{0,64},{1,2},{2,1},{3,4},{4,3},{5,6},{6,5},{7,71},{8,72},{9,10},{1... | collective-permute-start | bytes 491528 | tf_op jit(solution)/shard_map/ppermute | solution.py:451
  16.2 5.7 %collective-permute-start.2 = (bf16[2,4,80,128]{3,2,1,0:T(8,128)(2,1)S(1)}, bf16[2,4,80,128]{3,2,1,0:T(8,128)(2,1)S(1)}, u32[]{:S(2)}, u32[]{:S(2)}) collective-permute-start(bf16[2,4,80,128]{3,2,1,0:T(8,128)(2,1)S(1)} %get-tuple-element.50), channel_id=1, source_target_pairs={{0,1},{1,0},{2,3},{3,2},{4,5},{5,4},{6,7},{7,6},{8,9},{9,8},{10,11... | collective-permute-start | bytes 491528 | tf_op jit(solution)/shard_map/ppermute | solution.py:450
  20.7 1.2 %copy-start.6 = (bf16[2,4,80,128]{3,2,1,0:T(8,128)(2,1)}, bf16[2,4,80,128]{3,2,1,0:T(8,128)(2,1)S(1)}, u32[]{:S(2)}) copy-start(bf16[2,4,80,128]{3,2,1,0:T(8,128)(2,1)S(1)} %collective-permute-done.3.got_2) | copy-start | bytes 491524
  21.9 0.7 copy-start.7
  41.6 27.3 %all-to-all-start = ((bf16[128,16,128]{2,1,0:T(8,128)(2,1)}), bf16[128,16,128]{2,1,0:T(8,128)(2,1)S(1)}, u32[]{:S(2)}, u32[]{:S(2)}) async-start(bf16[128,16,128]{2,1,0:T(8,128)(2,1)} %bitcast.24), calls=%async_computation | async-start | bytes 1048576 | tf_op jit(solution)/shard_map/all_to_all | solution.py:484
  55.2 9.6 %collective-permute-start.4 = (bf16[96,128]{1,0:T(8,128)(2,1)}, bf16[96,128]{1,0:T(8,128)(2,1)S(1)}, u32[]{:S(2)}, u32[]{:S(2)}) collective-permute-start(bf16[96,128]{1,0:T(8,128)(2,1)} %get-tuple-element.36), channel_id=1, source_target_pairs={{8,0},{16,8},{24,16},{32,24},{40,32},{48,40},{56,48},{64,56},{72,6... | collective-permute-start | bytes 73736 | tf_op jit(solution)/shard_map/ppermute | solution.py:385
  56.3 8.5 %collective-permute-start.5 = (bf16[96,128]{1,0:T(8,128)(2,1)}, bf16[96,128]{1,0:T(8,128)(2,1)S(1)}, u32[]{:S(2)}, u32[]{:S(2)}) collective-permute-start(bf16[96,128]{1,0:T(8,128)(2,1)} %get-tuple-element.37), channel_id=1, source_target_pairs={{0,8},{8,16},{16,24},{24,32},{32,40},{40,48},{48,56},{56,64},{64,7... | collective-permute-start | bytes 73736 | tf_op jit(solution)/shard_map/ppermute | solution.py:386
  64.8 7.1 %copy-start.4 = (bf16[96,128]{1,0:T(8,128)(2,1)}, bf16[96,128]{1,0:T(8,128)(2,1)S(1)}, u32[]{:S(2)}) copy-start(bf16[96,128]{1,0:T(8,128)(2,1)S(1)} %collective-permute-done.4.right) | copy-start | bytes 73732
  64.8 7.1 %copy-start.5 = (bf16[96,128]{1,0:T(8,128)(2,1)}, bf16[96,128]{1,0:T(8,128)(2,1)S(1)}, u32[]{:S(2)}) copy-start(bf16[96,128]{1,0:T(8,128)(2,1)S(1)} %collective-permute-done.5.left) | copy-start | bytes 73732
  65.7 6.2 %collective-permute-start.7 = (bf16[4,96,128]{2,1,0:T(8,128)(2,1)S(1)}, bf16[4,96,128]{2,1,0:T(8,128)(2,1)S(1)}, u32[]{:S(2)}, u32[]{:S(2)}) collective-permute-start(bf16[4,96,128]{2,1,0:T(8,128)(2,1)S(1)} %get-tuple-element.51), channel_id=1, source_target_pairs={{0,64},{1,2},{2,1},{3,4},{4,3},{5,6},{6,5},{7,71},{8,72},{9,10},{1... | collective-permute-start | bytes 294920 | tf_op jit(solution)/shard_map/ppermute | solution.py:488
  68.4 3.5 %collective-permute-start.6 = (bf16[4,96,128]{2,1,0:T(8,128)(2,1)S(1)}, bf16[4,96,128]{2,1,0:T(8,128)(2,1)S(1)}, u32[]{:S(2)}, u32[]{:S(2)}) collective-permute-start(bf16[4,96,128]{2,1,0:T(8,128)(2,1)S(1)} %get-tuple-element.52), channel_id=1, source_target_pairs={{0,1},{1,0},{2,3},{3,2},{4,5},{5,4},{6,7},{7,6},{8,9},{9,8},{10,11... | collective-permute-start | bytes 294920 | tf_op jit(solution)/shard_map/ppermute | solution.py:487
  68.9 0.8 copy-start
  71.9 9.1 %copy-start.8 = (bf16[4,96,128]{2,1,0:T(8,128)(2,1)}, bf16[4,96,128]{2,1,0:T(8,128)(2,1)S(1)}, u32[]{:S(2)}) copy-start(bf16[4,96,128]{2,1,0:T(8,128)(2,1)S(1)} %collective-permute-done.7.got_2) | copy-start | bytes 294916
  71.9 9.1 %copy-start.9 = (bf16[4,96,128]{2,1,0:T(8,128)(2,1)}, bf16[4,96,128]{2,1,0:T(8,128)(2,1)S(1)}, u32[]{:S(2)}) copy-start(bf16[4,96,128]{2,1,0:T(8,128)(2,1)S(1)} %collective-permute-done.6.got_1) | copy-start | bytes 294916
  71.9 22.8 %all-to-all-start.1 = ((bf16[128,16,128]{2,1,0:T(8,128)(2,1)}), bf16[128,16,128]{2,1,0:T(8,128)(2,1)S(1)}, u32[]{:S(2)}, u32[]{:S(2)}) async-start(bf16[128,16,128]{2,1,0:T(8,128)(2,1)} %shard_map.95), calls=%async_computation.1 | async-start | bytes 1048576 | tf_op jit(solution)/shard_map/all_to_all | solution.py:496
  94.7 0.8 copy-start.1

commit v5 on v3

--- a/solution.py
+++ b/solution.py
@@ -13,7 +13,6 @@
 AXES = ("lon", "lat")
 CP = 80
 WIRE = BF
-VMEM = 56 * 1024 * 1024
 
 
 def dot(a, b):
@@ -86,11 +85,19 @@
             acc[start[t] + 4 - p] = acc[start[t] + 4 - p] + part
 
 
+def store_taps(acc, y, m, rows):
+    for k in range(rows + 8):
+        parts = [
+            y[p * m : (p + 1) * m, (k - 6 + p) * 128 : (k - 5 + p) * 128]
+            for p in range(5)
+            if 0 <= k - 6 + p < rows
+        ]
+        acc[k] = sum(parts[1:], parts[0]) if parts else jnp.zeros(acc.shape[1:], F32)
+
+
 def conv_rows(acc, stack, weight, m, rows, flip=None):
-    acc[...] = jnp.zeros(acc.shape, F32)
-
     y = dot(weight[...], wide(stack, 2, rows))
-    add_taps(acc, range(2, rows + 2), y, m, rows)
+    store_taps(acc, y, m, rows)
     outer = (0, 1, rows + 2, rows + 3)
     y = dot(weight[...], jnp.concatenate([stack[i] for i in outer], axis=1))
     add_taps(acc, outer, y, m, 4, flip)
@@ -159,9 +166,8 @@
         return carry
 
     lax.fori_loop(0, height, body, 0, unroll=8)
-    acc[...] = jnp.zeros(acc.shape, F32)
     y = dot(weight[...], wide(stack, 0, height))
-    add_taps(acc, range(2, height + 2), y, acc.shape[1], height)
+    store_taps(acc, y, acc.shape[1], height)
 
 
 def pack_kernel(rows_ref, field, cot, main, low, high, rim_1, rim_2):
@@ -359,21 +365,18 @@
     gain[...] = pair[0:1] + pair[64:65]
 
 
-def call(body, outs, scratch, args, flops, numbers=True, far_in=(), far_out=()):
+def call(body, outs, scratch, args, flops, mib, numbers=True):
     near = pl.BlockSpec(memory_space=pltpu.VMEM)
-    far = pl.BlockSpec(memory_space=pl.ANY)
-    in_specs = [far if i in far_in else near for i in range(len(args))]
+    in_specs = [near] * len(args)
     if numbers:
         in_specs[0] = pl.BlockSpec(memory_space=pltpu.SMEM)
     return pl.pallas_call(
         body,
         out_shape=[jax.ShapeDtypeStruct(s, t) for s, t in outs],
         in_specs=in_specs,
-        out_specs=[far if i in far_out else near for i in range(len(outs))],
-        scratch_shapes=[
-            pltpu.SemaphoreType.DMA(s) if t is None else pltpu.VMEM(s, t) for s, t in scratch
-        ],
-        compiler_params=pltpu.CompilerParams(vmem_limit_bytes=VMEM),
+        out_specs=[near] * len(outs),
+        scratch_shapes=[pltpu.VMEM(s, t) for s, t in scratch],
+        compiler_params=pltpu.CompilerParams(vmem_limit_bytes=mib << 20),
         cost_estimate=pl.CostEstimate(flops=flops, bytes_accessed=1 << 20, transcendentals=0),
     )(*args)
 
@@ -444,6 +447,7 @@
         [],
         (numbers, field, cotangent),
         5 * us,
+        24,
     )
     right, left = exchange_columns(low, high)
     sides = jnp.stack([right, left], axis=1)
@@ -459,6 +463,7 @@
             norm_gain[None],
         ),
         4 * us,
+        16,
         numbers=False,
     )
     both, low, high, out_1, out_2, flat = call(
@@ -479,6 +484,7 @@
             numbers, main, right, left, rim_1, rim_2, far_1, far_2, w_1, w_2, spread,
         ),
         12 * us,
+        48,
     )
 
     got = lax.all_to_all(flat.reshape(devices, rows, 128), AXES, 0, 0)
@@ -491,6 +497,7 @@
         functools.partial(reduce_kernel, factor), [((devices, rows, 128), BF)], [],
         (numbers, got),
         10 * us,
+        8,
     )
     mine, out_1, out_2, far_1, far_2 = lax.optimization_barrier((mine, out_1, out_2, far_1, far_2))
     summed = lax.all_to_all(mine, AXES, 0, 0).reshape(-1, 128)
@@ -500,6 +507,7 @@
         [],
         (summed,),
         20 * us,
+        16,
         numbers=False,
     )
     grad_first = jnp.transpose(grad_1, (2, 3, 0, 1))
@@ -513,6 +521,7 @@
             [((height + 4, 5 * hid, 128), BF), ((height + 8, CP, 128), F32)],
             (numbers, both, right, left, out_1, out_2, far_1, far_2, weight, base),
             2 * us,
+            36,
         )
     return results[0], results[1], grad_first, grad_second, gain.reshape(hid)
 

time: 94.2 us -> 90.8 us (0.964)
  Pallas kernels: 44.1 us -> 34 us
  waiting for transfers between devices: 5.45 us -> 8.98 us
  local copies, waits for them, and re-layouts: 2.88 us -> 5.29 us
    pallas_call x7, Pallas kernels: 44.1 us -> 34 us  [call(): pl.pallas_call(body, out_shape=[jax.ShapeDtypeStruct(s, t) for s, t in ou...]
    unnamed x28 -> x18, local copies, waits for them, and re-layouts: 2.27 us -> 5.2 us
    ppermute x2, waiting for transfers between devices: 1.63 us -> 3.45 us  [per_device(): rim_2, far_2 = lax.ppermute((rim_2, sides), AXES, two)]
    all_to_all x1, waiting for transfers between devices: 0.24 us -> 1.69 us  [per_device(): summed = lax.all_to_all(mine, AXES, 0, 0).reshape(-1, 128)]
    all_to_all x1, starting transfers between devices: 7.74 us -> 8.76 us  [per_device(): summed = lax.all_to_all(mine, AXES, 0, 0).reshape(-1, 128)]
  transfers between devices with their start and end apart: 14 -> 14, of which waited for: 4 -> 5; matrix products, arithmetic and copies ran while one was open for 0% -> 0% of each run, Pallas kernels for 19% -> 14%
where the time goes in v5:
time: 90.8 us; the launch traced here: 90.5 us
  starting transfers between devices  41.4 us (46%)
  Pallas kernels  34 us (37%)
  waiting for transfers between devices  8.98 us (10%)
  local copies, waits for them, and re-layouts  5.29 us (6%)
    pallas_call x7, Pallas kernels, call(): pl.pallas_call(body, out_shape=[jax.ShapeDtypeStruct(s, t) for s, t in ou...  34 us
    all_to_all x1, starting transfers between devices, per_device(): got = lax.all_to_all(flat.reshape(devices, rows, 128), AXES, 0, 0)  12.4 us
    all_to_all x1, starting transfers between devices, per_device(): summed = lax.all_to_all(mine, AXES, 0, 0).reshape(-1, 128)  8.76 us
    ppermute x2, starting transfers between devices, per_device(): out_2, far_2 = lax.ppermute((out_2, sides), AXES, two)  5.46 us
    unnamed x18, local copies, waits for them, and re-layouts  5.2 us
    ppermute x2, starting transfers between devices, exchange_columns(): left = lax.ppermute(high, 'lon', up)  4.98 us
    ppermute x2, starting transfers between devices, per_device(): rim_2, far_2 = lax.ppermute((rim_2, sides), AXES, two)  3.52 us
    ppermute x2, waiting for transfers between devices, per_device(): rim_2, far_2 = lax.ppermute((rim_2, sides), AXES, two)  3.45 us
  transfers between devices with their start and end apart: 14, of which 5 were waited for; matrix products, arithmetic and copies ran while one was open for 0% of the time, Pallas kernels for 14%

profile of v5, /device:TPU:1, one launch (start us, length us, event | category | flops | bytes accessed | tf_op | source)
XLA Modules:
  0.0 90.5 jit_solution(15740624628969713888)
XLA Ops:
  0.8 1.3 %copy-done = bf16[78,64,128]{2,1,0:T(8,128)(2,1)S(1)} copy-done((bf16[78,64,128]{2,1,0:T(8,128)(2,1)S(1)}, bf16[78,64,128]{2,1,0:T(8,128)(2,1)}, u32[]{:S(2)}) %copy-start) | copy-done | bytes 1277976
  2.1 1.3 %copy-done.2 = bf16[78,64,128]{2,1,0:T(8,128)(2,1)S(1)} copy-done((bf16[78,64,128]{2,1,0:T(8,128)(2,1)S(1)}, bf16[78,64,128]{2,1,0:T(8,128)(2,1)}, u32[]{:S(2)}) %copy-start.2) | copy-done | bytes 1277976
  3.4 2.4 %shard_map.92 = (bf16[2,64,80,128]{3,2,1,0:T(8,128)(2,1)S(1)}, bf16[2,80,128]{2,1,0:T(8,128)(2,1)S(1)}, bf16[2,80,128]{2,1,0:T(8,128)(2,1)S(1)}, bf16[2,2,80,128...) custom-call(s32[12]{0:T(128)S(1)} %stack.73.rows_ref, bf16[78,64,128]{2,1,0:T(8,128)(2,1)S(1)} %copy-done.2, ...), custom_call_target="tpu_custom_call" | custom-call | flops 5000000000 | bytes 1048576 | tf_op jit(solution)/shard_map/pallas_call | solution.py:373
  5.8 1.5 %collective-permute-start = (bf16[2,80,128]{2,1,0:T(8,128)(2,1)S(1)}, bf16[2,80,128]{2,1,0:T(8,128)(2,1)S(1)}, u32[]{:S(2)}, u32[]{:S(2)}) collective-permute-start(bf16[2,80,128]{2,1,0:T(8,128)(2,1)S(1)} %get-tuple-element.30), channel_id=1, source_target_pairs={{8,0},{16,8},{24,16},{32,24},{40,32},{48,40},{56,48},{64,56},{72,6... | collective-permute-start | bytes 122888 | tf_op jit(solution)/shard_map/ppermute | solution.py:388
  7.3 2.8 %collective-permute-start.1 = (bf16[2,80,128]{2,1,0:T(8,128)(2,1)S(1)}, bf16[2,80,128]{2,1,0:T(8,128)(2,1)S(1)}, u32[]{:S(2)}, u32[]{:S(2)}) collective-permute-start(bf16[2,80,128]{2,1,0:T(8,128)(2,1)S(1)} %get-tuple-element.31), channel_id=1, source_target_pairs={{0,8},{8,16},{16,24},{24,32},{32,40},{40,48},{48,56},{56,64},{64,7... | collective-permute-start | bytes 122888 | tf_op jit(solution)/shard_map/ppermute | solution.py:389
  11.2 2.9 %collective-permute-start.3 = (bf16[2,2,80,128]{3,2,1,0:T(8,128)(2,1)S(1)}, bf16[2,2,80,128]{3,2,1,0:T(8,128)(2,1)S(1)}, u32[]{:S(2)}, u32[]{:S(2)}) collective-permute-start(bf16[2,2,80,128]{3,2,1,0:T(8,128)(2,1)S(1)} %get-tuple-element.33), channel_id=1, source_target_pairs={{0,64},{1,2},{2,1},{3,4},{4,3},{5,6},{6,5},{7,71},{8,72},{9,10},{1... | collective-permute-start | bytes 245768 | tf_op jit(solution)/shard_map/ppermute | solution.py:455
  14.7 1.2 %collective-permute-start.4 = (bf16[2,2,80,128]{3,2,1,0:T(8,128)(2,1)S(1)}, bf16[2,2,80,128]{3,2,1,0:T(8,128)(2,1)S(1)}, u32[]{:S(2)}, u32[]{:S(2)}) collective-permute-start(bf16[2,2,80,128]{3,2,1,0:T(8,128)(2,1)S(1)} %pad_maximum_fusion), channel_id=1, source_target_pairs={{0,1},{1,0},{2,3},{3,2},{4,5},{5,4},{6,7},{7,6},{8,9},{9,8},{10,11... | collective-permute-start | bytes 245768 | tf_op jit(solution)/shard_map/ppermute | solution.py:454
  16.4 3.4 %collective-permute-done.5.far_2 = bf16[2,2,80,128]{3,2,1,0:T(8,128)(2,1)S(1)} collective-permute-done((bf16[2,2,80,128]{3,2,1,0:T(8,128)(2,1)S(1)}, bf16[2,2,80,128]{3,2,1,0:T(8,128)(2,1)S(1)}, u32[]{:S(2)}, u32[]{:S(2)}) %collective-permute-start.5) | collective-permute-done | bytes 81952 | tf_op jit(solution)/shard_map/ppermute | solution.py:455
  19.8 17.5 %shard_map.94 = (bf16[64,96,128]{2,1,0:T(8,128)(2,1)S(1)}, bf16[96,128]{1,0:T(8,128)(2,1)S(1)}, bf16[96,128]{1,0:T(8,128)(2,1)S(1)}, bf16[2,96,128]{2,1,0:T(8,12...) custom-call(s32[12]{0:T(128)S(1)} %stack.73.rows_ref, ...), custom_call_target="tpu_custom_call" | custom-call | flops 12000000000 | bytes 1048576 | tf_op jit(solution)/shard_map/pallas_call | solution.py:373
  37.4 1.2 %copy-done.7 = bf16[64,96,128]{2,1,0:T(8,128)(2,1)} copy-done((bf16[64,96,128]{2,1,0:T(8,128)(2,1)}, bf16[64,96,128]{2,1,0:T(8,128)(2,1)S(1)}, u32[]{:S(2)}) %copy-start.7) | copy-done | bytes 1572888
  38.5 12.4 %all-to-all-start = ((bf16[128,16,128]{2,1,0:T(8,128)(2,1)}), bf16[128,16,128]{2,1,0:T(8,128)(2,1)S(1)}, u32[]{:S(2)}, u32[]{:S(2)}) async-start(bf16[128,16,128]{2,1,0:T(8,128)(2,1)} %bitcast.17), calls=%async_computation | async-start | bytes 1048576 | tf_op jit(solution)/shard_map/all_to_all | solution.py:490
  50.9 1.1 %collective-permute-start.6 = (bf16[96,128]{1,0:T(8,128)(2,1)S(1)}, bf16[96,128]{1,0:T(8,128)(2,1)S(1)}, u32[]{:S(2)}, u32[]{:S(2)}) collective-permute-start(bf16[96,128]{1,0:T(8,128)(2,1)S(1)} %get-tuple-element.38), channel_id=1, source_target_pairs={{8,0},{16,8},{24,16},{32,24},{40,32},{48,40},{56,48},{64,56},{72,6... | collective-permute-start | bytes 73736 | tf_op jit(solution)/shard_map/ppermute | solution.py:388
  52.1 2.2 %collective-permute-start.7 = (bf16[96,128]{1,0:T(8,128)(2,1)S(1)}, bf16[96,128]{1,0:T(8,128)(2,1)S(1)}, u32[]{:S(2)}, u32[]{:S(2)}) collective-permute-start(bf16[96,128]{1,0:T(8,128)(2,1)S(1)} %get-tuple-element.39), channel_id=1, source_target_pairs={{0,8},{8,16},{16,24},{24,32},{32,40},{40,48},{48,56},{56,64},{64,7... | collective-permute-start | bytes 73736 | tf_op jit(solution)/shard_map/ppermute | solution.py:389
  54.3 1.4 %collective-permute-start.8 = (bf16[2,96,128]{2,1,0:T(8,128)(2,1)S(1)}, bf16[2,96,128]{2,1,0:T(8,128)(2,1)S(1)}, u32[]{:S(2)}, u32[]{:S(2)}) collective-permute-start(bf16[2,96,128]{2,1,0:T(8,128)(2,1)S(1)} %get-tuple-element.41), channel_id=1, source_target_pairs={{0,1},{1,0},{2,3},{3,2},{4,5},{5,4},{6,7},{7,6},{8,9},{9,8},{10,11... | collective-permute-start | bytes 147464 | tf_op jit(solution)/shard_map/ppermute | solution.py:493
  55.6 2.7 %collective-permute-start.9 = (bf16[2,96,128]{2,1,0:T(8,128)(2,1)S(1)}, bf16[2,96,128]{2,1,0:T(8,128)(2,1)S(1)}, u32[]{:S(2)}, u32[]{:S(2)}) collective-permute-start(bf16[2,96,128]{2,1,0:T(8,128)(2,1)S(1)} %get-tuple-element.42), channel_id=1, source_target_pairs={{0,64},{1,2},{2,1},{3,4},{4,3},{5,6},{6,5},{7,71},{8,72},{9,10},{1... | collective-permute-start | bytes 147464 | tf_op jit(solution)/shard_map/ppermute | solution.py:494
  58.3 2.5 %collective-permute-done.6.right = bf16[96,128]{1,0:T(8,128)(2,1)S(1)} collective-permute-done((bf16[96,128]{1,0:T(8,128)(2,1)S(1)}, bf16[96,128]{1,0:T(8,128)(2,1)S(1)}, u32[]{:S(2)}, u32[]{:S(2)}) %collective-permute-start.6) | collective-permute-done | bytes 24608 | tf_op jit(solution)/shard_map/ppermute | solution.py:388
  60.9 2.8 %collective-permute-start.11 = (bf16[2,96,128]{2,1,0:T(8,128)(2,1)S(1)}, bf16[2,96,128]{2,1,0:T(8,128)(2,1)S(1)}, u32[]{:S(2)}, u32[]{:S(2)}) collective-permute-start(bf16[2,96,128]{2,1,0:T(8,128)(2,1)S(1)} %pad_maximum_fusion.1), channel_id=1, source_target_pairs={{0,64},{1,2},{2,1},{3,4},{4,3},{5,6},{6,5},{7,71},{8,72},{9,10},{1... | collective-permute-start | bytes 147464 | tf_op jit(solution)/shard_map/ppermute | solution.py:494
  64.7 1.6 %shard_map.95 = bf16[128,16,128]{2,1,0:T(8,128)(2,1)} custom-call(s32[12]{0:T(128)S(1)} %stack.73.rows_ref, bf16[128,16,128]{2,1,0:T(8,128)(2,1)S(1)} %all-to-all-done.got), custom_call_target="tpu_custom_call" | custom-call | flops 10000000000 | bytes 1048576 | tf_op jit(solution)/shard_map/pallas_call | solution.py:373
  66.6 8.8 %all-to-all-start.1 = ((bf16[128,16,128]{2,1,0:T(8,128)(2,1)}), bf16[128,16,128]{2,1,0:T(8,128)(2,1)S(1)}, u32[]{:S(2)}, u32[]{:S(2)}) async-start(bf16[128,16,128]{2,1,0:T(8,128)(2,1)} %shard_map.95), calls=%async_computation.1 | async-start | bytes 1048576 | tf_op jit(solution)/shard_map/all_to_all | solution.py:503
  75.4 1.4 %copy-done.8 = bf16[64,96,128]{2,1,0:T(8,128)(2,1)S(1)} copy-done((bf16[64,96,128]{2,1,0:T(8,128)(2,1)S(1)}, bf16[64,96,128]{2,1,0:T(8,128)(2,1)}, u32[]{:S(2)}) %copy-start.8) | copy-done | bytes 1572888
  76.8 5.4 %shard_map.97 = bf16[78,64,128]{2,1,0:T(8,128)(2,1)} custom-call(s32[12]{0:T(128)S(1)} %stack.73.rows_ref, bf16[64,96,128]{2,1,0:T(8,128)(2,1)S(1)} %copy-done.8, bf16[96,128]{1,0:T(8,128)(2,1)S(1)} %collective-permute-done.6.right, bf16[96,128]{1,0:T(8,128)(2,1)S(1)} %collective-permute-done.7.left, bf16[2,96,128]{2,1,0:T(8,128)(2,1)S(1)} %collective-permute-done.8.rim_1, ...), custom_call_target="tpu_custom_call" | custom-call | flops 2000000000 | bytes 1048576 | tf_op jit(solution)/shard_map/pallas_call | solution.py:373
  82.2 5.3 %shard_map.96 = bf16[78,64,128]{2,1,0:T(8,128)(2,1)} custom-call(s32[12]{0:T(128)S(1)} %stack.73.rows_ref, bf16[64,96,128]{2,1,0:T(8,128)(2,1)S(1)} %copy-done.8, bf16[96,128]{1,0:T(8,128)(2,1)S(1)} %collective-permute-done.6.right, bf16[96,128]{1,0:T(8,128)(2,1)S(1)} %collective-permute-done.7.left, bf16[2,96,128]{2,1,0:T(8,128)(2,1)S(1)} %collective-permute-done.8.rim_1, ...), custom_call_target="tpu_custom_call" | custom-call | flops 2000000000 | bytes 1048576 | tf_op jit(solution)/shard_map/pallas_call | solution.py:373
  87.4 1.7 %all-to-all-done.1 = bf16[128,16,128]{2,1,0:T(8,128)(2,1)S(1)} async-done(((bf16[128,16,128]{2,1,0:T(8,128)(2,1)}), bf16[128,16,128]{2,1,0:T(8,128)(2,1)S(1)}, u32[]{:S(2)}, u32[]{:S(2)}) %all-to-all-start.1) | async-done | bytes 524320 | tf_op jit(solution)/shard_map/all_to_all | solution.py:503
  89.1 1.4 %shard_map.98 = (f32[5,5,48,78]{3,2,1,0:T(8,128)}, f32[5,5,48,78]{3,2,1,0:T(8,128)}, f32[1,48]{1,0:T(1,128)}) custom-call(bf16[2048,128]{1,0:T(8,128)(2,1)S(1)} %bitcast.24), custom_call_target="tpu_custom_call" | custom-call | flops 20000000000 | bytes 1048576 | tf_op jit(solution)/shard_map/pallas_call | solution.py:373
  (32 shorter events, 3.5 us)
Async XLA Ops:
  0.8 1.3 %copy-start = (bf16[78,64,128]{2,1,0:T(8,128)(2,1)S(1)}, bf16[78,64,128]{2,1,0:T(8,128)(2,1)}, u32[]{:S(2)}) copy-start(bf16[78,64,128]{2,1,0:T(8,128)(2,1)} %base.3) | copy-start | bytes 3833860
  2.1 1.3 %copy-start.2 = (bf16[78,64,128]{2,1,0:T(8,128)(2,1)S(1)}, bf16[78,64,128]{2,1,0:T(8,128)(2,1)}, u32[]{:S(2)}) copy-start(bf16[78,64,128]{2,1,0:T(8,128)(2,1)} %base.2) | copy-start | bytes 3833860
  3.4 12.6 %copy-start.4 = (bf16[48,78,5,5]{1,0,3,2:T(8,128)(2,1)S(1)}, bf16[48,78,5,5]{1,0,3,2:T(8,128)(2,1)}, u32[]{:S(2)}) copy-start(bf16[48,78,5,5]{1,0,3,2:T(8,128)(2,1)} %param.6) | copy-start | bytes 561604
  3.4 12.6 %copy-start.5 = (bf16[78,48,5,5]{0,1,3,2:T(8,128)(2,1)S(1)}, bf16[78,48,5,5]{0,1,3,2:T(8,128)(2,1)}, u32[]{:S(2)}) copy-start(bf16[78,48,5,5]{0,1,3,2:T(8,128)(2,1)} %param.8) | copy-start | bytes 561604
  3.4 12.6 %copy-start.6 = (f32[48]{0:T(128)S(1)}, f32[48]{0:T(128)}, u32[]{:S(2)}) copy-start(f32[48]{0:T(128)} %param.7) | copy-start | bytes 580
  5.8 8.3 %collective-permute-start = (bf16[2,80,128]{2,1,0:T(8,128)(2,1)S(1)}, bf16[2,80,128]{2,1,0:T(8,128)(2,1)S(1)}, u32[]{:S(2)}, u32[]{:S(2)}) collective-permute-start(bf16[2,80,128]{2,1,0:T(8,128)(2,1)S(1)} %get-tuple-element.30), channel_id=1, source_target_pairs={{8,0},{16,8},{24,16},{32,24},{40,32},{48,40},{56,48},{64,56},{72,6... | collective-permute-start | bytes 122888 | tf_op jit(solution)/shard_map/ppermute | solution.py:388
  7.3 6.8 %collective-permute-start.1 = (bf16[2,80,128]{2,1,0:T(8,128)(2,1)S(1)}, bf16[2,80,128]{2,1,0:T(8,128)(2,1)S(1)}, u32[]{:S(2)}, u32[]{:S(2)}) collective-permute-start(bf16[2,80,128]{2,1,0:T(8,128)(2,1)S(1)} %get-tuple-element.31), channel_id=1, source_target_pairs={{0,8},{8,16},{16,24},{24,32},{32,40},{40,48},{48,56},{56,64},{64,7... | collective-permute-start | bytes 122888 | tf_op jit(solution)/shard_map/ppermute | solution.py:389
  10.1 6.3 %collective-permute-start.2 = (bf16[2,2,80,128]{3,2,1,0:T(8,128)(2,1)S(1)}, bf16[2,2,80,128]{3,2,1,0:T(8,128)(2,1)S(1)}, u32[]{:S(2)}, u32[]{:S(2)}) collective-permute-start(bf16[2,2,80,128]{3,2,1,0:T(8,128)(2,1)S(1)} %get-tuple-element.32), channel_id=1, source_target_pairs={{0,1},{1,0},{2,3},{3,2},{4,5},{5,4},{6,7},{7,6},{8,9},{9,8},{10,11... | collective-permute-start | bytes 245768 | tf_op jit(solution)/shard_map/ppermute | solution.py:454
  11.2 5.2 %collective-permute-start.3 = (bf16[2,2,80,128]{3,2,1,0:T(8,128)(2,1)S(1)}, bf16[2,2,80,128]{3,2,1,0:T(8,128)(2,1)S(1)}, u32[]{:S(2)}, u32[]{:S(2)}) collective-permute-start(bf16[2,2,80,128]{3,2,1,0:T(8,128)(2,1)S(1)} %get-tuple-element.33), channel_id=1, source_target_pairs={{0,64},{1,2},{2,1},{3,4},{4,3},{5,6},{6,5},{7,71},{8,72},{9,10},{1... | collective-permute-start | bytes 245768 | tf_op jit(solution)/shard_map/ppermute | solution.py:455
  14.1 5.7 %collective-permute-start.5 = (bf16[2,2,80,128]{3,2,1,0:T(8,128)(2,1)S(1)}, bf16[2,2,80,128]{3,2,1,0:T(8,128)(2,1)S(1)}, u32[]{:S(2)}, u32[]{:S(2)}) collective-permute-start(bf16[2,2,80,128]{3,2,1,0:T(8,128)(2,1)S(1)} %pad_maximum_fusion), channel_id=1, source_target_pairs={{0,64},{1,2},{2,1},{3,4},{4,3},{5,6},{6,5},{7,71},{8,72},{9,10},{1... | collective-permute-start | bytes 245768 | tf_op jit(solution)/shard_map/ppermute | solution.py:455
  14.7 5.1 %collective-permute-start.4 = (bf16[2,2,80,128]{3,2,1,0:T(8,128)(2,1)S(1)}, bf16[2,2,80,128]{3,2,1,0:T(8,128)(2,1)S(1)}, u32[]{:S(2)}, u32[]{:S(2)}) collective-permute-start(bf16[2,2,80,128]{3,2,1,0:T(8,128)(2,1)S(1)} %pad_maximum_fusion), channel_id=1, source_target_pairs={{0,1},{1,0},{2,3},{3,2},{4,5},{5,4},{6,7},{7,6},{8,9},{9,8},{10,11... | collective-permute-start | bytes 245768 | tf_op jit(solution)/shard_map/ppermute | solution.py:454
  37.4 1.2 %copy-start.7 = (bf16[64,96,128]{2,1,0:T(8,128)(2,1)}, bf16[64,96,128]{2,1,0:T(8,128)(2,1)S(1)}, u32[]{:S(2)}) copy-start(bf16[64,96,128]{2,1,0:T(8,128)(2,1)S(1)} %get-tuple-element.37.both) | copy-start | bytes 4718596
  38.5 26.1 %all-to-all-start = ((bf16[128,16,128]{2,1,0:T(8,128)(2,1)}), bf16[128,16,128]{2,1,0:T(8,128)(2,1)S(1)}, u32[]{:S(2)}, u32[]{:S(2)}) async-start(bf16[128,16,128]{2,1,0:T(8,128)(2,1)} %bitcast.17), calls=%async_computation | async-start | bytes 1048576 | tf_op jit(solution)/shard_map/all_to_all | solution.py:490
  50.9 9.9 %collective-permute-start.6 = (bf16[96,128]{1,0:T(8,128)(2,1)S(1)}, bf16[96,128]{1,0:T(8,128)(2,1)S(1)}, u32[]{:S(2)}, u32[]{:S(2)}) collective-permute-start(bf16[96,128]{1,0:T(8,128)(2,1)S(1)} %get-tuple-element.38), channel_id=1, source_target_pairs={{8,0},{16,8},{24,16},{32,24},{40,32},{48,40},{56,48},{64,56},{72,6... | collective-permute-start | bytes 73736 | tf_op jit(solution)/shard_map/ppermute | solution.py:388
  52.1 8.8 %collective-permute-start.7 = (bf16[96,128]{1,0:T(8,128)(2,1)S(1)}, bf16[96,128]{1,0:T(8,128)(2,1)S(1)}, u32[]{:S(2)}, u32[]{:S(2)}) collective-permute-start(bf16[96,128]{1,0:T(8,128)(2,1)S(1)} %get-tuple-element.39), channel_id=1, source_target_pairs={{0,8},{8,16},{16,24},{24,32},{32,40},{40,48},{48,56},{56,64},{64,7... | collective-permute-start | bytes 73736 | tf_op jit(solution)/shard_map/ppermute | solution.py:389
  54.3 12.1 %collective-permute-start.8 = (bf16[2,96,128]{2,1,0:T(8,128)(2,1)S(1)}, bf16[2,96,128]{2,1,0:T(8,128)(2,1)S(1)}, u32[]{:S(2)}, u32[]{:S(2)}) collective-permute-start(bf16[2,96,128]{2,1,0:T(8,128)(2,1)S(1)} %get-tuple-element.41), channel_id=1, source_target_pairs={{0,1},{1,0},{2,3},{3,2},{4,5},{5,4},{6,7},{7,6},{8,9},{9,8},{10,11... | collective-permute-start | bytes 147464 | tf_op jit(solution)/shard_map/ppermute | solution.py:493
  55.6 10.7 %collective-permute-start.9 = (bf16[2,96,128]{2,1,0:T(8,128)(2,1)S(1)}, bf16[2,96,128]{2,1,0:T(8,128)(2,1)S(1)}, u32[]{:S(2)}, u32[]{:S(2)}) collective-permute-start(bf16[2,96,128]{2,1,0:T(8,128)(2,1)S(1)} %get-tuple-element.42), channel_id=1, source_target_pairs={{0,64},{1,2},{2,1},{3,4},{4,3},{5,6},{6,5},{7,71},{8,72},{9,10},{1... | collective-permute-start | bytes 147464 | tf_op jit(solution)/shard_map/ppermute | solution.py:494
  60.9 14.5 %copy-start.1 = (bf16[78,64,128]{2,1,0:T(8,128)(2,1)S(1)}, bf16[78,64,128]{2,1,0:T(8,128)(2,1)}, u32[]{:S(2)}) copy-start(bf16[78,64,128]{2,1,0:T(8,128)(2,1)} %base.3) | copy-start | bytes 3833860
  60.9 5.4 %collective-permute-start.11 = (bf16[2,96,128]{2,1,0:T(8,128)(2,1)S(1)}, bf16[2,96,128]{2,1,0:T(8,128)(2,1)S(1)}, u32[]{:S(2)}, u32[]{:S(2)}) collective-permute-start(bf16[2,96,128]{2,1,0:T(8,128)(2,1)S(1)} %pad_maximum_fusion.1), channel_id=1, source_target_pairs={{0,64},{1,2},{2,1},{3,4},{4,3},{5,6},{6,5},{7,71},{8,72},{9,10},{1... | collective-permute-start | bytes 147464 | tf_op jit(solution)/shard_map/ppermute | solution.py:494
  63.7 2.9 %collective-permute-start.10 = (bf16[2,96,128]{2,1,0:T(8,128)(2,1)S(1)}, bf16[2,96,128]{2,1,0:T(8,128)(2,1)S(1)}, u32[]{:S(2)}, u32[]{:S(2)}) collective-permute-start(bf16[2,96,128]{2,1,0:T(8,128)(2,1)S(1)} %pad_maximum_fusion.1), channel_id=1, source_target_pairs={{0,1},{1,0},{2,3},{3,2},{4,5},{5,4},{6,7},{7,6},{8,9},{9,8},{10,11... | collective-permute-start | bytes 147464 | tf_op jit(solution)/shard_map/ppermute | solution.py:493
  66.6 22.5 %all-to-all-start.1 = ((bf16[128,16,128]{2,1,0:T(8,128)(2,1)}), bf16[128,16,128]{2,1,0:T(8,128)(2,1)S(1)}, u32[]{:S(2)}, u32[]{:S(2)}) async-start(bf16[128,16,128]{2,1,0:T(8,128)(2,1)} %shard_map.95), calls=%async_computation.1 | async-start | bytes 1048576 | tf_op jit(solution)/shard_map/all_to_all | solution.py:503
  75.4 1.4 %copy-start.8 = (bf16[64,96,128]{2,1,0:T(8,128)(2,1)S(1)}, bf16[64,96,128]{2,1,0:T(8,128)(2,1)}, u32[]{:S(2)}) copy-start(bf16[64,96,128]{2,1,0:T(8,128)(2,1)} %copy-done.7) | copy-start | bytes 4718596
  76.8 5.4 %copy-start.3 = (bf16[78,64,128]{2,1,0:T(8,128)(2,1)S(1)}, bf16[78,64,128]{2,1,0:T(8,128)(2,1)}, u32[]{:S(2)}) copy-start(bf16[78,64,128]{2,1,0:T(8,128)(2,1)} %base.2) | copy-start | bytes 3833860

commit v6 on v5

--- a/solution.py
+++ b/solution.py
@@ -484,7 +484,7 @@
             numbers, main, right, left, rim_1, rim_2, far_1, far_2, w_1, w_2, spread,
         ),
         12 * us,
-        48,
+        34,
     )
 
     got = lax.all_to_all(flat.reshape(devices, rows, 128), AXES, 0, 0)
@@ -521,7 +521,7 @@
             [((height + 4, 5 * hid, 128), BF), ((height + 8, CP, 128), F32)],
             (numbers, both, right, left, out_1, out_2, far_1, far_2, weight, base),
             2 * us,
-            36,
+            28,
         )
     return results[0], results[1], grad_first, grad_second, gain.reshape(hid)
 

time: 90.8 us -> 90.8 us (level)
  no operation moved by 1% of the time
where the time goes in v6:
time: 90.8 us; the launch traced here: 90.5 us
  starting transfers between devices  41.4 us (46%)
  Pallas kernels  34 us (37%)
  waiting for transfers between devices  8.98 us (10%)
  local copies, waits for them, and re-layouts  5.29 us (6%)
    pallas_call x7, Pallas kernels, call(): pl.pallas_call(body, out_shape=[jax.ShapeDtypeStruct(s, t) for s, t in ou...  34 us
    all_to_all x1, starting transfers between devices, per_device(): got = lax.all_to_all(flat.reshape(devices, rows, 128), AXES, 0, 0)  12.4 us
    all_to_all x1, starting transfers between devices, per_device(): summed = lax.all_to_all(mine, AXES, 0, 0).reshape(-1, 128)  8.76 us
    ppermute x2, starting transfers between devices, per_device(): out_2, far_2 = lax.ppermute((out_2, sides), AXES, two)  5.46 us
    unnamed x18, local copies, waits for them, and re-layouts  5.2 us
    ppermute x2, starting transfers between devices, exchange_columns(): left = lax.ppermute(high, 'lon', up)  4.98 us
    ppermute x2, starting transfers between devices, per_device(): rim_2, far_2 = lax.ppermute((rim_2, sides), AXES, two)  3.52 us
    ppermute x2, waiting for transfers between devices, per_device(): rim_2, far_2 = lax.ppermute((rim_2, sides), AXES, two)  3.45 us
  transfers between devices with their start and end apart: 14, of which 5 were waited for; matrix products, arithmetic and copies ran while one was open for 0% of the time, Pallas kernels for 14%

profile of v6, /device:TPU:1, one launch (start us, length us, event | category | flops | bytes accessed | tf_op | source)
XLA Modules:
  0.0 90.5 jit_solution(17290526173205416415)
XLA Ops:
  0.8 1.3 %copy-done = bf16[78,64,128]{2,1,0:T(8,128)(2,1)S(1)} copy-done((bf16[78,64,128]{2,1,0:T(8,128)(2,1)S(1)}, bf16[78,64,128]{2,1,0:T(8,128)(2,1)}, u32[]{:S(2)}) %copy-start) | copy-done | bytes 1277976
  2.1 1.3 %copy-done.2 = bf16[78,64,128]{2,1,0:T(8,128)(2,1)S(1)} copy-done((bf16[78,64,128]{2,1,0:T(8,128)(2,1)S(1)}, bf16[78,64,128]{2,1,0:T(8,128)(2,1)}, u32[]{:S(2)}) %copy-start.2) | copy-done | bytes 1277976
  3.4 2.4 %shard_map.92 = (bf16[2,64,80,128]{3,2,1,0:T(8,128)(2,1)S(1)}, bf16[2,80,128]{2,1,0:T(8,128)(2,1)S(1)}, bf16[2,80,128]{2,1,0:T(8,128)(2,1)S(1)}, bf16[2,2,80,128...) custom-call(s32[12]{0:T(128)S(1)} %stack.73.rows_ref, bf16[78,64,128]{2,1,0:T(8,128)(2,1)S(1)} %copy-done.2, ...), custom_call_target="tpu_custom_call" | custom-call | flops 5000000000 | bytes 1048576 | tf_op jit(solution)/shard_map/pallas_call | solution.py:373
  5.8 1.5 %collective-permute-start = (bf16[2,80,128]{2,1,0:T(8,128)(2,1)S(1)}, bf16[2,80,128]{2,1,0:T(8,128)(2,1)S(1)}, u32[]{:S(2)}, u32[]{:S(2)}) collective-permute-start(bf16[2,80,128]{2,1,0:T(8,128)(2,1)S(1)} %get-tuple-element.30), channel_id=1, source_target_pairs={{8,0},{16,8},{24,16},{32,24},{40,32},{48,40},{56,48},{64,56},{72,6... | collective-permute-start | bytes 122888 | tf_op jit(solution)/shard_map/ppermute | solution.py:388
  7.3 2.8 %collective-permute-start.1 = (bf16[2,80,128]{2,1,0:T(8,128)(2,1)S(1)}, bf16[2,80,128]{2,1,0:T(8,128)(2,1)S(1)}, u32[]{:S(2)}, u32[]{:S(2)}) collective-permute-start(bf16[2,80,128]{2,1,0:T(8,128)(2,1)S(1)} %get-tuple-element.31), channel_id=1, source_target_pairs={{0,8},{8,16},{16,24},{24,32},{32,40},{40,48},{48,56},{56,64},{64,7... | collective-permute-start | bytes 122888 | tf_op jit(solution)/shard_map/ppermute | solution.py:389
  11.2 2.9 %collective-permute-start.3 = (bf16[2,2,80,128]{3,2,1,0:T(8,128)(2,1)S(1)}, bf16[2,2,80,128]{3,2,1,0:T(8,128)(2,1)S(1)}, u32[]{:S(2)}, u32[]{:S(2)}) collective-permute-start(bf16[2,2,80,128]{3,2,1,0:T(8,128)(2,1)S(1)} %get-tuple-element.33), channel_id=1, source_target_pairs={{0,64},{1,2},{2,1},{3,4},{4,3},{5,6},{6,5},{7,71},{8,72},{9,10},{1... | collective-permute-start | bytes 245768 | tf_op jit(solution)/shard_map/ppermute | solution.py:455
  14.7 1.2 %collective-permute-start.4 = (bf16[2,2,80,128]{3,2,1,0:T(8,128)(2,1)S(1)}, bf16[2,2,80,128]{3,2,1,0:T(8,128)(2,1)S(1)}, u32[]{:S(2)}, u32[]{:S(2)}) collective-permute-start(bf16[2,2,80,128]{3,2,1,0:T(8,128)(2,1)S(1)} %pad_maximum_fusion), channel_id=1, source_target_pairs={{0,1},{1,0},{2,3},{3,2},{4,5},{5,4},{6,7},{7,6},{8,9},{9,8},{10,11... | collective-permute-start | bytes 245768 | tf_op jit(solution)/shard_map/ppermute | solution.py:454
  16.4 3.4 %collective-permute-done.5.far_2 = bf16[2,2,80,128]{3,2,1,0:T(8,128)(2,1)S(1)} collective-permute-done((bf16[2,2,80,128]{3,2,1,0:T(8,128)(2,1)S(1)}, bf16[2,2,80,128]{3,2,1,0:T(8,128)(2,1)S(1)}, u32[]{:S(2)}, u32[]{:S(2)}) %collective-permute-start.5) | collective-permute-done | bytes 81952 | tf_op jit(solution)/shard_map/ppermute | solution.py:455
  19.8 17.5 %shard_map.94 = (bf16[64,96,128]{2,1,0:T(8,128)(2,1)S(1)}, bf16[96,128]{1,0:T(8,128)(2,1)S(1)}, bf16[96,128]{1,0:T(8,128)(2,1)S(1)}, bf16[2,96,128]{2,1,0:T(8,12...) custom-call(s32[12]{0:T(128)S(1)} %stack.73.rows_ref, ...), custom_call_target="tpu_custom_call" | custom-call | flops 12000000000 | bytes 1048576 | tf_op jit(solution)/shard_map/pallas_call | solution.py:373
  37.4 1.2 %copy-done.7 = bf16[64,96,128]{2,1,0:T(8,128)(2,1)} copy-done((bf16[64,96,128]{2,1,0:T(8,128)(2,1)}, bf16[64,96,128]{2,1,0:T(8,128)(2,1)S(1)}, u32[]{:S(2)}) %copy-start.7) | copy-done | bytes 1572888
  38.5 12.4 %all-to-all-start = ((bf16[128,16,128]{2,1,0:T(8,128)(2,1)}), bf16[128,16,128]{2,1,0:T(8,128)(2,1)S(1)}, u32[]{:S(2)}, u32[]{:S(2)}) async-start(bf16[128,16,128]{2,1,0:T(8,128)(2,1)} %bitcast.17), calls=%async_computation | async-start | bytes 1048576 | tf_op jit(solution)/shard_map/all_to_all | solution.py:490
  50.9 1.1 %collective-permute-start.6 = (bf16[96,128]{1,0:T(8,128)(2,1)S(1)}, bf16[96,128]{1,0:T(8,128)(2,1)S(1)}, u32[]{:S(2)}, u32[]{:S(2)}) collective-permute-start(bf16[96,128]{1,0:T(8,128)(2,1)S(1)} %get-tuple-element.38), channel_id=1, source_target_pairs={{8,0},{16,8},{24,16},{32,24},{40,32},{48,40},{56,48},{64,56},{72,6... | collective-permute-start | bytes 73736 | tf_op jit(solution)/shard_map/ppermute | solution.py:388
  52.1 2.2 %collective-permute-start.7 = (bf16[96,128]{1,0:T(8,128)(2,1)S(1)}, bf16[96,128]{1,0:T(8,128)(2,1)S(1)}, u32[]{:S(2)}, u32[]{:S(2)}) collective-permute-start(bf16[96,128]{1,0:T(8,128)(2,1)S(1)} %get-tuple-element.39), channel_id=1, source_target_pairs={{0,8},{8,16},{16,24},{24,32},{32,40},{40,48},{48,56},{56,64},{64,7... | collective-permute-start | bytes 73736 | tf_op jit(solution)/shard_map/ppermute | solution.py:389
  54.3 1.4 %collective-permute-start.8 = (bf16[2,96,128]{2,1,0:T(8,128)(2,1)S(1)}, bf16[2,96,128]{2,1,0:T(8,128)(2,1)S(1)}, u32[]{:S(2)}, u32[]{:S(2)}) collective-permute-start(bf16[2,96,128]{2,1,0:T(8,128)(2,1)S(1)} %get-tuple-element.41), channel_id=1, source_target_pairs={{0,1},{1,0},{2,3},{3,2},{4,5},{5,4},{6,7},{7,6},{8,9},{9,8},{10,11... | collective-permute-start | bytes 147464 | tf_op jit(solution)/shard_map/ppermute | solution.py:493
  55.6 2.7 %collective-permute-start.9 = (bf16[2,96,128]{2,1,0:T(8,128)(2,1)S(1)}, bf16[2,96,128]{2,1,0:T(8,128)(2,1)S(1)}, u32[]{:S(2)}, u32[]{:S(2)}) collective-permute-start(bf16[2,96,128]{2,1,0:T(8,128)(2,1)S(1)} %get-tuple-element.42), channel_id=1, source_target_pairs={{0,64},{1,2},{2,1},{3,4},{4,3},{5,6},{6,5},{7,71},{8,72},{9,10},{1... | collective-permute-start | bytes 147464 | tf_op jit(solution)/shard_map/ppermute | solution.py:494
  58.3 2.5 %collective-permute-done.6.right = bf16[96,128]{1,0:T(8,128)(2,1)S(1)} collective-permute-done((bf16[96,128]{1,0:T(8,128)(2,1)S(1)}, bf16[96,128]{1,0:T(8,128)(2,1)S(1)}, u32[]{:S(2)}, u32[]{:S(2)}) %collective-permute-start.6) | collective-permute-done | bytes 24608 | tf_op jit(solution)/shard_map/ppermute | solution.py:388
  60.9 2.8 %collective-permute-start.11 = (bf16[2,96,128]{2,1,0:T(8,128)(2,1)S(1)}, bf16[2,96,128]{2,1,0:T(8,128)(2,1)S(1)}, u32[]{:S(2)}, u32[]{:S(2)}) collective-permute-start(bf16[2,96,128]{2,1,0:T(8,128)(2,1)S(1)} %pad_maximum_fusion.1), channel_id=1, source_target_pairs={{0,64},{1,2},{2,1},{3,4},{4,3},{5,6},{6,5},{7,71},{8,72},{9,10},{1... | collective-permute-start | bytes 147464 | tf_op jit(solution)/shard_map/ppermute | solution.py:494
  64.7 1.6 %shard_map.95 = bf16[128,16,128]{2,1,0:T(8,128)(2,1)} custom-call(s32[12]{0:T(128)S(1)} %stack.73.rows_ref, bf16[128,16,128]{2,1,0:T(8,128)(2,1)S(1)} %all-to-all-done.got), custom_call_target="tpu_custom_call" | custom-call | flops 10000000000 | bytes 1048576 | tf_op jit(solution)/shard_map/pallas_call | solution.py:373
  66.6 8.8 %all-to-all-start.1 = ((bf16[128,16,128]{2,1,0:T(8,128)(2,1)}), bf16[128,16,128]{2,1,0:T(8,128)(2,1)S(1)}, u32[]{:S(2)}, u32[]{:S(2)}) async-start(bf16[128,16,128]{2,1,0:T(8,128)(2,1)} %shard_map.95), calls=%async_computation.1 | async-start | bytes 1048576 | tf_op jit(solution)/shard_map/all_to_all | solution.py:503
  75.4 1.4 %copy-done.8 = bf16[64,96,128]{2,1,0:T(8,128)(2,1)S(1)} copy-done((bf16[64,96,128]{2,1,0:T(8,128)(2,1)S(1)}, bf16[64,96,128]{2,1,0:T(8,128)(2,1)}, u32[]{:S(2)}) %copy-start.8) | copy-done | bytes 1572888
  76.8 5.4 %shard_map.97 = bf16[78,64,128]{2,1,0:T(8,128)(2,1)} custom-call(s32[12]{0:T(128)S(1)} %stack.73.rows_ref, bf16[64,96,128]{2,1,0:T(8,128)(2,1)S(1)} %copy-done.8, bf16[96,128]{1,0:T(8,128)(2,1)S(1)} %collective-permute-done.6.right, bf16[96,128]{1,0:T(8,128)(2,1)S(1)} %collective-permute-done.7.left, bf16[2,96,128]{2,1,0:T(8,128)(2,1)S(1)} %collective-permute-done.8.rim_1, ...), custom_call_target="tpu_custom_call" | custom-call | flops 2000000000 | bytes 1048576 | tf_op jit(solution)/shard_map/pallas_call | solution.py:373
  82.2 5.3 %shard_map.96 = bf16[78,64,128]{2,1,0:T(8,128)(2,1)} custom-call(s32[12]{0:T(128)S(1)} %stack.73.rows_ref, bf16[64,96,128]{2,1,0:T(8,128)(2,1)S(1)} %copy-done.8, bf16[96,128]{1,0:T(8,128)(2,1)S(1)} %collective-permute-done.6.right, bf16[96,128]{1,0:T(8,128)(2,1)S(1)} %collective-permute-done.7.left, bf16[2,96,128]{2,1,0:T(8,128)(2,1)S(1)} %collective-permute-done.8.rim_1, ...), custom_call_target="tpu_custom_call" | custom-call | flops 2000000000 | bytes 1048576 | tf_op jit(solution)/shard_map/pallas_call | solution.py:373
  87.4 1.7 %all-to-all-done.1 = bf16[128,16,128]{2,1,0:T(8,128)(2,1)S(1)} async-done(((bf16[128,16,128]{2,1,0:T(8,128)(2,1)}), bf16[128,16,128]{2,1,0:T(8,128)(2,1)S(1)}, u32[]{:S(2)}, u32[]{:S(2)}) %all-to-all-start.1) | async-done | bytes 524320 | tf_op jit(solution)/shard_map/all_to_all | solution.py:503
  89.1 1.4 %shard_map.98 = (f32[5,5,48,78]{3,2,1,0:T(8,128)}, f32[5,5,48,78]{3,2,1,0:T(8,128)}, f32[1,48]{1,0:T(1,128)}) custom-call(bf16[2048,128]{1,0:T(8,128)(2,1)S(1)} %bitcast.24), custom_call_target="tpu_custom_call" | custom-call | flops 20000000000 | bytes 1048576 | tf_op jit(solution)/shard_map/pallas_call | solution.py:373
  (32 shorter events, 3.5 us)
Async XLA Ops:
  0.8 1.3 %copy-start = (bf16[78,64,128]{2,1,0:T(8,128)(2,1)S(1)}, bf16[78,64,128]{2,1,0:T(8,128)(2,1)}, u32[]{:S(2)}) copy-start(bf16[78,64,128]{2,1,0:T(8,128)(2,1)} %base.3) | copy-start | bytes 3833860
  2.1 1.3 %copy-start.2 = (bf16[78,64,128]{2,1,0:T(8,128)(2,1)S(1)}, bf16[78,64,128]{2,1,0:T(8,128)(2,1)}, u32[]{:S(2)}) copy-start(bf16[78,64,128]{2,1,0:T(8,128)(2,1)} %base.2) | copy-start | bytes 3833860
  3.4 12.6 %copy-start.4 = (bf16[48,78,5,5]{1,0,3,2:T(8,128)(2,1)S(1)}, bf16[48,78,5,5]{1,0,3,2:T(8,128)(2,1)}, u32[]{:S(2)}) copy-start(bf16[48,78,5,5]{1,0,3,2:T(8,128)(2,1)} %param.6) | copy-start | bytes 561604
  3.4 12.6 %copy-start.5 = (bf16[78,48,5,5]{0,1,3,2:T(8,128)(2,1)S(1)}, bf16[78,48,5,5]{0,1,3,2:T(8,128)(2,1)}, u32[]{:S(2)}) copy-start(bf16[78,48,5,5]{0,1,3,2:T(8,128)(2,1)} %param.8) | copy-start | bytes 561604
  3.4 12.6 %copy-start.6 = (f32[48]{0:T(128)S(1)}, f32[48]{0:T(128)}, u32[]{:S(2)}) copy-start(f32[48]{0:T(128)} %param.7) | copy-start | bytes 580
  5.8 8.3 %collective-permute-start = (bf16[2,80,128]{2,1,0:T(8,128)(2,1)S(1)}, bf16[2,80,128]{2,1,0:T(8,128)(2,1)S(1)}, u32[]{:S(2)}, u32[]{:S(2)}) collective-permute-start(bf16[2,80,128]{2,1,0:T(8,128)(2,1)S(1)} %get-tuple-element.30), channel_id=1, source_target_pairs={{8,0},{16,8},{24,16},{32,24},{40,32},{48,40},{56,48},{64,56},{72,6... | collective-permute-start | bytes 122888 | tf_op jit(solution)/shard_map/ppermute | solution.py:388
  7.3 6.8 %collective-permute-start.1 = (bf16[2,80,128]{2,1,0:T(8,128)(2,1)S(1)}, bf16[2,80,128]{2,1,0:T(8,128)(2,1)S(1)}, u32[]{:S(2)}, u32[]{:S(2)}) collective-permute-start(bf16[2,80,128]{2,1,0:T(8,128)(2,1)S(1)} %get-tuple-element.31), channel_id=1, source_target_pairs={{0,8},{8,16},{16,24},{24,32},{32,40},{40,48},{48,56},{56,64},{64,7... | collective-permute-start | bytes 122888 | tf_op jit(solution)/shard_map/ppermute | solution.py:389
  10.1 6.3 %collective-permute-start.2 = (bf16[2,2,80,128]{3,2,1,0:T(8,128)(2,1)S(1)}, bf16[2,2,80,128]{3,2,1,0:T(8,128)(2,1)S(1)}, u32[]{:S(2)}, u32[]{:S(2)}) collective-permute-start(bf16[2,2,80,128]{3,2,1,0:T(8,128)(2,1)S(1)} %get-tuple-element.32), channel_id=1, source_target_pairs={{0,1},{1,0},{2,3},{3,2},{4,5},{5,4},{6,7},{7,6},{8,9},{9,8},{10,11... | collective-permute-start | bytes 245768 | tf_op jit(solution)/shard_map/ppermute | solution.py:454
  11.2 5.2 %collective-permute-start.3 = (bf16[2,2,80,128]{3,2,1,0:T(8,128)(2,1)S(1)}, bf16[2,2,80,128]{3,2,1,0:T(8,128)(2,1)S(1)}, u32[]{:S(2)}, u32[]{:S(2)}) collective-permute-start(bf16[2,2,80,128]{3,2,1,0:T(8,128)(2,1)S(1)} %get-tuple-element.33), channel_id=1, source_target_pairs={{0,64},{1,2},{2,1},{3,4},{4,3},{5,6},{6,5},{7,71},{8,72},{9,10},{1... | collective-permute-start | bytes 245768 | tf_op jit(solution)/shard_map/ppermute | solution.py:455
  14.1 5.7 %collective-permute-start.5 = (bf16[2,2,80,128]{3,2,1,0:T(8,128)(2,1)S(1)}, bf16[2,2,80,128]{3,2,1,0:T(8,128)(2,1)S(1)}, u32[]{:S(2)}, u32[]{:S(2)}) collective-permute-start(bf16[2,2,80,128]{3,2,1,0:T(8,128)(2,1)S(1)} %pad_maximum_fusion), channel_id=1, source_target_pairs={{0,64},{1,2},{2,1},{3,4},{4,3},{5,6},{6,5},{7,71},{8,72},{9,10},{1... | collective-permute-start | bytes 245768 | tf_op jit(solution)/shard_map/ppermute | solution.py:455
  14.7 5.1 %collective-permute-start.4 = (bf16[2,2,80,128]{3,2,1,0:T(8,128)(2,1)S(1)}, bf16[2,2,80,128]{3,2,1,0:T(8,128)(2,1)S(1)}, u32[]{:S(2)}, u32[]{:S(2)}) collective-permute-start(bf16[2,2,80,128]{3,2,1,0:T(8,128)(2,1)S(1)} %pad_maximum_fusion), channel_id=1, source_target_pairs={{0,1},{1,0},{2,3},{3,2},{4,5},{5,4},{6,7},{7,6},{8,9},{9,8},{10,11... | collective-permute-start | bytes 245768 | tf_op jit(solution)/shard_map/ppermute | solution.py:454
  37.4 1.2 %copy-start.7 = (bf16[64,96,128]{2,1,0:T(8,128)(2,1)}, bf16[64,96,128]{2,1,0:T(8,128)(2,1)S(1)}, u32[]{:S(2)}) copy-start(bf16[64,96,128]{2,1,0:T(8,128)(2,1)S(1)} %get-tuple-element.37.both) | copy-start | bytes 4718596
  38.5 26.1 %all-to-all-start = ((bf16[128,16,128]{2,1,0:T(8,128)(2,1)}), bf16[128,16,128]{2,1,0:T(8,128)(2,1)S(1)}, u32[]{:S(2)}, u32[]{:S(2)}) async-start(bf16[128,16,128]{2,1,0:T(8,128)(2,1)} %bitcast.17), calls=%async_computation | async-start | bytes 1048576 | tf_op jit(solution)/shard_map/all_to_all | solution.py:490
  50.9 9.9 %collective-permute-start.6 = (bf16[96,128]{1,0:T(8,128)(2,1)S(1)}, bf16[96,128]{1,0:T(8,128)(2,1)S(1)}, u32[]{:S(2)}, u32[]{:S(2)}) collective-permute-start(bf16[96,128]{1,0:T(8,128)(2,1)S(1)} %get-tuple-element.38), channel_id=1, source_target_pairs={{8,0},{16,8},{24,16},{32,24},{40,32},{48,40},{56,48},{64,56},{72,6... | collective-permute-start | bytes 73736 | tf_op jit(solution)/shard_map/ppermute | solution.py:388
  52.1 8.8 %collective-permute-start.7 = (bf16[96,128]{1,0:T(8,128)(2,1)S(1)}, bf16[96,128]{1,0:T(8,128)(2,1)S(1)}, u32[]{:S(2)}, u32[]{:S(2)}) collective-permute-start(bf16[96,128]{1,0:T(8,128)(2,1)S(1)} %get-tuple-element.39), channel_id=1, source_target_pairs={{0,8},{8,16},{16,24},{24,32},{32,40},{40,48},{48,56},{56,64},{64,7... | collective-permute-start | bytes 73736 | tf_op jit(solution)/shard_map/ppermute | solution.py:389
  54.3 12.1 %collective-permute-start.8 = (bf16[2,96,128]{2,1,0:T(8,128)(2,1)S(1)}, bf16[2,96,128]{2,1,0:T(8,128)(2,1)S(1)}, u32[]{:S(2)}, u32[]{:S(2)}) collective-permute-start(bf16[2,96,128]{2,1,0:T(8,128)(2,1)S(1)} %get-tuple-element.41), channel_id=1, source_target_pairs={{0,1},{1,0},{2,3},{3,2},{4,5},{5,4},{6,7},{7,6},{8,9},{9,8},{10,11... | collective-permute-start | bytes 147464 | tf_op jit(solution)/shard_map/ppermute | solution.py:493
  55.6 10.7 %collective-permute-start.9 = (bf16[2,96,128]{2,1,0:T(8,128)(2,1)S(1)}, bf16[2,96,128]{2,1,0:T(8,128)(2,1)S(1)}, u32[]{:S(2)}, u32[]{:S(2)}) collective-permute-start(bf16[2,96,128]{2,1,0:T(8,128)(2,1)S(1)} %get-tuple-element.42), channel_id=1, source_target_pairs={{0,64},{1,2},{2,1},{3,4},{4,3},{5,6},{6,5},{7,71},{8,72},{9,10},{1... | collective-permute-start | bytes 147464 | tf_op jit(solution)/shard_map/ppermute | solution.py:494
  60.9 14.5 %copy-start.1 = (bf16[78,64,128]{2,1,0:T(8,128)(2,1)S(1)}, bf16[78,64,128]{2,1,0:T(8,128)(2,1)}, u32[]{:S(2)}) copy-start(bf16[78,64,128]{2,1,0:T(8,128)(2,1)} %base.3) | copy-start | bytes 3833860
  60.9 5.4 %collective-permute-start.11 = (bf16[2,96,128]{2,1,0:T(8,128)(2,1)S(1)}, bf16[2,96,128]{2,1,0:T(8,128)(2,1)S(1)}, u32[]{:S(2)}, u32[]{:S(2)}) collective-permute-start(bf16[2,96,128]{2,1,0:T(8,128)(2,1)S(1)} %pad_maximum_fusion.1), channel_id=1, source_target_pairs={{0,64},{1,2},{2,1},{3,4},{4,3},{5,6},{6,5},{7,71},{8,72},{9,10},{1... | collective-permute-start | bytes 147464 | tf_op jit(solution)/shard_map/ppermute | solution.py:494
  63.7 2.9 %collective-permute-start.10 = (bf16[2,96,128]{2,1,0:T(8,128)(2,1)S(1)}, bf16[2,96,128]{2,1,0:T(8,128)(2,1)S(1)}, u32[]{:S(2)}, u32[]{:S(2)}) collective-permute-start(bf16[2,96,128]{2,1,0:T(8,128)(2,1)S(1)} %pad_maximum_fusion.1), channel_id=1, source_target_pairs={{0,1},{1,0},{2,3},{3,2},{4,5},{5,4},{6,7},{7,6},{8,9},{9,8},{10,11... | collective-permute-start | bytes 147464 | tf_op jit(solution)/shard_map/ppermute | solution.py:493
  66.6 22.5 %all-to-all-start.1 = ((bf16[128,16,128]{2,1,0:T(8,128)(2,1)}), bf16[128,16,128]{2,1,0:T(8,128)(2,1)S(1)}, u32[]{:S(2)}, u32[]{:S(2)}) async-start(bf16[128,16,128]{2,1,0:T(8,128)(2,1)} %shard_map.95), calls=%async_computation.1 | async-start | bytes 1048576 | tf_op jit(solution)/shard_map/all_to_all | solution.py:503
  75.4 1.4 %copy-start.8 = (bf16[64,96,128]{2,1,0:T(8,128)(2,1)S(1)}, bf16[64,96,128]{2,1,0:T(8,128)(2,1)}, u32[]{:S(2)}) copy-start(bf16[64,96,128]{2,1,0:T(8,128)(2,1)} %copy-done.7) | copy-start | bytes 4718596
  76.8 5.4 %copy-start.3 = (bf16[78,64,128]{2,1,0:T(8,128)(2,1)S(1)}, bf16[78,64,128]{2,1,0:T(8,128)(2,1)}, u32[]{:S(2)}) copy-start(bf16[78,64,128]{2,1,0:T(8,128)(2,1)} %base.2) | copy-start | bytes 3833860

commit v7 on v5

--- a/solution.py
+++ b/solution.py
@@ -165,7 +165,7 @@
             stack[r, q * CP : (q + 1) * CP] = piece
         return carry
 
-    lax.fori_loop(0, height, body, 0, unroll=8)
+    lax.fori_loop(0, height, body, 0, unroll=32)
     y = dot(weight[...], wide(stack, 0, height))
     store_taps(acc, y, acc.shape[1], height)
 
@@ -253,7 +253,7 @@
         both[r, hid : 2 * hid] = grad_pre
         return total + grad_normed * unit
 
-    total = lax.fori_loop(0, height, cells, jnp.zeros((hid, 128), F32), unroll=16)
+    total = lax.fori_loop(0, height, cells, jnp.zeros((hid, 128), F32), unroll=32)
     lows, highs = edge_columns(lambda r: both[r], height, 2 * hid)
     low[...] = lows
     high[...] = highs

time: 90.8 us -> 89.8 us (0.989)
  Pallas kernels: 34 us -> 33 us
    pallas_call x7, Pallas kernels: 34 us -> 33 us  [call(): pl.pallas_call(body, out_shape=[jax.ShapeDtypeStruct(s, t) for s, t in ou...]
where the time goes in v7:
time: 89.8 us; the launch traced here: 89.5 us
  starting transfers between devices  41.4 us (46%)
  Pallas kernels  33 us (37%)
  waiting for transfers between devices  8.97 us (10%)
  local copies, waits for them, and re-layouts  5.29 us (6%)
    pallas_call x7, Pallas kernels, call(): pl.pallas_call(body, out_shape=[jax.ShapeDtypeStruct(s, t) for s, t in ou...  33 us
    all_to_all x1, starting transfers between devices, per_device(): got = lax.all_to_all(flat.reshape(devices, rows, 128), AXES, 0, 0)  12.4 us
    all_to_all x1, starting transfers between devices, per_device(): summed = lax.all_to_all(mine, AXES, 0, 0).reshape(-1, 128)  8.76 us
    ppermute x2, starting transfers between devices, per_device(): out_2, far_2 = lax.ppermute((out_2, sides), AXES, two)  5.47 us
    unnamed x18, local copies, waits for them, and re-layouts  5.2 us
    ppermute x2, starting transfers between devices, exchange_columns(): left = lax.ppermute(high, 'lon', up)  4.98 us
    ppermute x2, starting transfers between devices, per_device(): rim_2, far_2 = lax.ppermute((rim_2, sides), AXES, two)  3.52 us
    ppermute x2, waiting for transfers between devices, per_device(): rim_2, far_2 = lax.ppermute((rim_2, sides), AXES, two)  3.45 us
  transfers between devices with their start and end apart: 14, of which 5 were waited for; matrix products, arithmetic and copies ran while one was open for 0% of the time, Pallas kernels for 14%

profile of v7, /device:TPU:1, one launch (start us, length us, event | category | flops | bytes accessed | tf_op | source)
XLA Modules:
  0.0 89.5 jit_solution(16158920199400199803)
XLA Ops:
  0.8 1.3 %copy-done = bf16[78,64,128]{2,1,0:T(8,128)(2,1)S(1)} copy-done((bf16[78,64,128]{2,1,0:T(8,128)(2,1)S(1)}, bf16[78,64,128]{2,1,0:T(8,128)(2,1)}, u32[]{:S(2)}) %copy-start) | copy-done | bytes 1277976
  2.1 1.3 %copy-done.2 = bf16[78,64,128]{2,1,0:T(8,128)(2,1)S(1)} copy-done((bf16[78,64,128]{2,1,0:T(8,128)(2,1)S(1)}, bf16[78,64,128]{2,1,0:T(8,128)(2,1)}, u32[]{:S(2)}) %copy-start.2) | copy-done | bytes 1277976
  3.4 2.4 %shard_map.92 = (bf16[2,64,80,128]{3,2,1,0:T(8,128)(2,1)S(1)}, bf16[2,80,128]{2,1,0:T(8,128)(2,1)S(1)}, bf16[2,80,128]{2,1,0:T(8,128)(2,1)S(1)}, bf16[2,2,80,128...) custom-call(s32[12]{0:T(128)S(1)} %stack.73.rows_ref, bf16[78,64,128]{2,1,0:T(8,128)(2,1)S(1)} %copy-done.2, ...), custom_call_target="tpu_custom_call" | custom-call | flops 5000000000 | bytes 1048576 | tf_op jit(solution)/shard_map/pallas_call | solution.py:373
  5.8 1.5 %collective-permute-start = (bf16[2,80,128]{2,1,0:T(8,128)(2,1)S(1)}, bf16[2,80,128]{2,1,0:T(8,128)(2,1)S(1)}, u32[]{:S(2)}, u32[]{:S(2)}) collective-permute-start(bf16[2,80,128]{2,1,0:T(8,128)(2,1)S(1)} %get-tuple-element.30), channel_id=1, source_target_pairs={{8,0},{16,8},{24,16},{32,24},{40,32},{48,40},{56,48},{64,56},{72,6... | collective-permute-start | bytes 122888 | tf_op jit(solution)/shard_map/ppermute | solution.py:388
  7.3 2.8 %collective-permute-start.1 = (bf16[2,80,128]{2,1,0:T(8,128)(2,1)S(1)}, bf16[2,80,128]{2,1,0:T(8,128)(2,1)S(1)}, u32[]{:S(2)}, u32[]{:S(2)}) collective-permute-start(bf16[2,80,128]{2,1,0:T(8,128)(2,1)S(1)} %get-tuple-element.31), channel_id=1, source_target_pairs={{0,8},{8,16},{16,24},{24,32},{32,40},{40,48},{48,56},{56,64},{64,7... | collective-permute-start | bytes 122888 | tf_op jit(solution)/shard_map/ppermute | solution.py:389
  11.2 2.9 %collective-permute-start.3 = (bf16[2,2,80,128]{3,2,1,0:T(8,128)(2,1)S(1)}, bf16[2,2,80,128]{3,2,1,0:T(8,128)(2,1)S(1)}, u32[]{:S(2)}, u32[]{:S(2)}) collective-permute-start(bf16[2,2,80,128]{3,2,1,0:T(8,128)(2,1)S(1)} %get-tuple-element.33), channel_id=1, source_target_pairs={{0,64},{1,2},{2,1},{3,4},{4,3},{5,6},{6,5},{7,71},{8,72},{9,10},{1... | collective-permute-start | bytes 245768 | tf_op jit(solution)/shard_map/ppermute | solution.py:455
  14.7 1.2 %collective-permute-start.4 = (bf16[2,2,80,128]{3,2,1,0:T(8,128)(2,1)S(1)}, bf16[2,2,80,128]{3,2,1,0:T(8,128)(2,1)S(1)}, u32[]{:S(2)}, u32[]{:S(2)}) collective-permute-start(bf16[2,2,80,128]{3,2,1,0:T(8,128)(2,1)S(1)} %pad_maximum_fusion), channel_id=1, source_target_pairs={{0,1},{1,0},{2,3},{3,2},{4,5},{5,4},{6,7},{7,6},{8,9},{9,8},{10,11... | collective-permute-start | bytes 245768 | tf_op jit(solution)/shard_map/ppermute | solution.py:454
  16.4 3.4 %collective-permute-done.5.far_2 = bf16[2,2,80,128]{3,2,1,0:T(8,128)(2,1)S(1)} collective-permute-done((bf16[2,2,80,128]{3,2,1,0:T(8,128)(2,1)S(1)}, bf16[2,2,80,128]{3,2,1,0:T(8,128)(2,1)S(1)}, u32[]{:S(2)}, u32[]{:S(2)}) %collective-permute-start.5) | collective-permute-done | bytes 81952 | tf_op jit(solution)/shard_map/ppermute | solution.py:455
  19.8 16.5 %shard_map.94 = (bf16[64,96,128]{2,1,0:T(8,128)(2,1)S(1)}, bf16[96,128]{1,0:T(8,128)(2,1)S(1)}, bf16[96,128]{1,0:T(8,128)(2,1)S(1)}, bf16[2,96,128]{2,1,0:T(8,12...) custom-call(s32[12]{0:T(128)S(1)} %stack.73.rows_ref, ...), custom_call_target="tpu_custom_call" | custom-call | flops 12000000000 | bytes 1048576 | tf_op jit(solution)/shard_map/pallas_call | solution.py:373
  36.3 1.2 %copy-done.7 = bf16[64,96,128]{2,1,0:T(8,128)(2,1)} copy-done((bf16[64,96,128]{2,1,0:T(8,128)(2,1)}, bf16[64,96,128]{2,1,0:T(8,128)(2,1)S(1)}, u32[]{:S(2)}) %copy-start.7) | copy-done | bytes 1572888
  37.5 12.4 %all-to-all-start = ((bf16[128,16,128]{2,1,0:T(8,128)(2,1)}), bf16[128,16,128]{2,1,0:T(8,128)(2,1)S(1)}, u32[]{:S(2)}, u32[]{:S(2)}) async-start(bf16[128,16,128]{2,1,0:T(8,128)(2,1)} %bitcast.17), calls=%async_computation | async-start | bytes 1048576 | tf_op jit(solution)/shard_map/all_to_all | solution.py:490
  49.9 1.1 %collective-permute-start.6 = (bf16[96,128]{1,0:T(8,128)(2,1)S(1)}, bf16[96,128]{1,0:T(8,128)(2,1)S(1)}, u32[]{:S(2)}, u32[]{:S(2)}) collective-permute-start(bf16[96,128]{1,0:T(8,128)(2,1)S(1)} %get-tuple-element.38), channel_id=1, source_target_pairs={{8,0},{16,8},{24,16},{32,24},{40,32},{48,40},{56,48},{64,56},{72,6... | collective-permute-start | bytes 73736 | tf_op jit(solution)/shard_map/ppermute | solution.py:388
  51.0 2.2 %collective-permute-start.7 = (bf16[96,128]{1,0:T(8,128)(2,1)S(1)}, bf16[96,128]{1,0:T(8,128)(2,1)S(1)}, u32[]{:S(2)}, u32[]{:S(2)}) collective-permute-start(bf16[96,128]{1,0:T(8,128)(2,1)S(1)} %get-tuple-element.39), channel_id=1, source_target_pairs={{0,8},{8,16},{16,24},{24,32},{32,40},{40,48},{48,56},{56,64},{64,7... | collective-permute-start | bytes 73736 | tf_op jit(solution)/shard_map/ppermute | solution.py:389
  53.2 1.4 %collective-permute-start.8 = (bf16[2,96,128]{2,1,0:T(8,128)(2,1)S(1)}, bf16[2,96,128]{2,1,0:T(8,128)(2,1)S(1)}, u32[]{:S(2)}, u32[]{:S(2)}) collective-permute-start(bf16[2,96,128]{2,1,0:T(8,128)(2,1)S(1)} %get-tuple-element.41), channel_id=1, source_target_pairs={{0,1},{1,0},{2,3},{3,2},{4,5},{5,4},{6,7},{7,6},{8,9},{9,8},{10,11... | collective-permute-start | bytes 147464 | tf_op jit(solution)/shard_map/ppermute | solution.py:493
  54.6 2.7 %collective-permute-start.9 = (bf16[2,96,128]{2,1,0:T(8,128)(2,1)S(1)}, bf16[2,96,128]{2,1,0:T(8,128)(2,1)S(1)}, u32[]{:S(2)}, u32[]{:S(2)}) collective-permute-start(bf16[2,96,128]{2,1,0:T(8,128)(2,1)S(1)} %get-tuple-element.42), channel_id=1, source_target_pairs={{0,64},{1,2},{2,1},{3,4},{4,3},{5,6},{6,5},{7,71},{8,72},{9,10},{1... | collective-permute-start | bytes 147464 | tf_op jit(solution)/shard_map/ppermute | solution.py:494
  57.3 2.5 %collective-permute-done.6.right = bf16[96,128]{1,0:T(8,128)(2,1)S(1)} collective-permute-done((bf16[96,128]{1,0:T(8,128)(2,1)S(1)}, bf16[96,128]{1,0:T(8,128)(2,1)S(1)}, u32[]{:S(2)}, u32[]{:S(2)}) %collective-permute-start.6) | collective-permute-done | bytes 24608 | tf_op jit(solution)/shard_map/ppermute | solution.py:388
  59.8 2.8 %collective-permute-start.11 = (bf16[2,96,128]{2,1,0:T(8,128)(2,1)S(1)}, bf16[2,96,128]{2,1,0:T(8,128)(2,1)S(1)}, u32[]{:S(2)}, u32[]{:S(2)}) collective-permute-start(bf16[2,96,128]{2,1,0:T(8,128)(2,1)S(1)} %pad_maximum_fusion.1), channel_id=1, source_target_pairs={{0,64},{1,2},{2,1},{3,4},{4,3},{5,6},{6,5},{7,71},{8,72},{9,10},{1... | collective-permute-start | bytes 147464 | tf_op jit(solution)/shard_map/ppermute | solution.py:494
  63.6 1.6 %shard_map.95 = bf16[128,16,128]{2,1,0:T(8,128)(2,1)} custom-call(s32[12]{0:T(128)S(1)} %stack.73.rows_ref, bf16[128,16,128]{2,1,0:T(8,128)(2,1)S(1)} %all-to-all-done.got), custom_call_target="tpu_custom_call" | custom-call | flops 10000000000 | bytes 1048576 | tf_op jit(solution)/shard_map/pallas_call | solution.py:373
  65.5 8.8 %all-to-all-start.1 = ((bf16[128,16,128]{2,1,0:T(8,128)(2,1)}), bf16[128,16,128]{2,1,0:T(8,128)(2,1)S(1)}, u32[]{:S(2)}, u32[]{:S(2)}) async-start(bf16[128,16,128]{2,1,0:T(8,128)(2,1)} %shard_map.95), calls=%async_computation.1 | async-start | bytes 1048576 | tf_op jit(solution)/shard_map/all_to_all | solution.py:503
  74.3 1.4 %copy-done.8 = bf16[64,96,128]{2,1,0:T(8,128)(2,1)S(1)} copy-done((bf16[64,96,128]{2,1,0:T(8,128)(2,1)S(1)}, bf16[64,96,128]{2,1,0:T(8,128)(2,1)}, u32[]{:S(2)}) %copy-start.8) | copy-done | bytes 1572888
  75.7 5.4 %shard_map.97 = bf16[78,64,128]{2,1,0:T(8,128)(2,1)} custom-call(s32[12]{0:T(128)S(1)} %stack.73.rows_ref, bf16[64,96,128]{2,1,0:T(8,128)(2,1)S(1)} %copy-done.8, bf16[96,128]{1,0:T(8,128)(2,1)S(1)} %collective-permute-done.6.right, bf16[96,128]{1,0:T(8,128)(2,1)S(1)} %collective-permute-done.7.left, bf16[2,96,128]{2,1,0:T(8,128)(2,1)S(1)} %collective-permute-done.8.rim_1, ...), custom_call_target="tpu_custom_call" | custom-call | flops 2000000000 | bytes 1048576 | tf_op jit(solution)/shard_map/pallas_call | solution.py:373
  81.1 5.3 %shard_map.96 = bf16[78,64,128]{2,1,0:T(8,128)(2,1)} custom-call(s32[12]{0:T(128)S(1)} %stack.73.rows_ref, bf16[64,96,128]{2,1,0:T(8,128)(2,1)S(1)} %copy-done.8, bf16[96,128]{1,0:T(8,128)(2,1)S(1)} %collective-permute-done.6.right, bf16[96,128]{1,0:T(8,128)(2,1)S(1)} %collective-permute-done.7.left, bf16[2,96,128]{2,1,0:T(8,128)(2,1)S(1)} %collective-permute-done.8.rim_1, ...), custom_call_target="tpu_custom_call" | custom-call | flops 2000000000 | bytes 1048576 | tf_op jit(solution)/shard_map/pallas_call | solution.py:373
  86.4 1.7 %all-to-all-done.1 = bf16[128,16,128]{2,1,0:T(8,128)(2,1)S(1)} async-done(((bf16[128,16,128]{2,1,0:T(8,128)(2,1)}), bf16[128,16,128]{2,1,0:T(8,128)(2,1)S(1)}, u32[]{:S(2)}, u32[]{:S(2)}) %all-to-all-start.1) | async-done | bytes 524320 | tf_op jit(solution)/shard_map/all_to_all | solution.py:503
  88.1 1.4 %shard_map.98 = (f32[5,5,48,78]{3,2,1,0:T(8,128)}, f32[5,5,48,78]{3,2,1,0:T(8,128)}, f32[1,48]{1,0:T(1,128)}) custom-call(bf16[2048,128]{1,0:T(8,128)(2,1)S(1)} %bitcast.24), custom_call_target="tpu_custom_call" | custom-call | flops 20000000000 | bytes 1048576 | tf_op jit(solution)/shard_map/pallas_call | solution.py:373
  (32 shorter events, 3.5 us)
Async XLA Ops:
  0.8 1.3 %copy-start = (bf16[78,64,128]{2,1,0:T(8,128)(2,1)S(1)}, bf16[78,64,128]{2,1,0:T(8,128)(2,1)}, u32[]{:S(2)}) copy-start(bf16[78,64,128]{2,1,0:T(8,128)(2,1)} %base.3) | copy-start | bytes 3833860
  2.1 1.3 %copy-start.2 = (bf16[78,64,128]{2,1,0:T(8,128)(2,1)S(1)}, bf16[78,64,128]{2,1,0:T(8,128)(2,1)}, u32[]{:S(2)}) copy-start(bf16[78,64,128]{2,1,0:T(8,128)(2,1)} %base.2) | copy-start | bytes 3833860
  3.4 12.6 %copy-start.4 = (bf16[48,78,5,5]{1,0,3,2:T(8,128)(2,1)S(1)}, bf16[48,78,5,5]{1,0,3,2:T(8,128)(2,1)}, u32[]{:S(2)}) copy-start(bf16[48,78,5,5]{1,0,3,2:T(8,128)(2,1)} %param.6) | copy-start | bytes 561604
  3.4 12.6 %copy-start.5 = (bf16[78,48,5,5]{0,1,3,2:T(8,128)(2,1)S(1)}, bf16[78,48,5,5]{0,1,3,2:T(8,128)(2,1)}, u32[]{:S(2)}) copy-start(bf16[78,48,5,5]{0,1,3,2:T(8,128)(2,1)} %param.8) | copy-start | bytes 561604
  3.4 12.6 %copy-start.6 = (f32[48]{0:T(128)S(1)}, f32[48]{0:T(128)}, u32[]{:S(2)}) copy-start(f32[48]{0:T(128)} %param.7) | copy-start | bytes 580
  5.8 8.3 %collective-permute-start = (bf16[2,80,128]{2,1,0:T(8,128)(2,1)S(1)}, bf16[2,80,128]{2,1,0:T(8,128)(2,1)S(1)}, u32[]{:S(2)}, u32[]{:S(2)}) collective-permute-start(bf16[2,80,128]{2,1,0:T(8,128)(2,1)S(1)} %get-tuple-element.30), channel_id=1, source_target_pairs={{8,0},{16,8},{24,16},{32,24},{40,32},{48,40},{56,48},{64,56},{72,6... | collective-permute-start | bytes 122888 | tf_op jit(solution)/shard_map/ppermute | solution.py:388
  7.3 6.8 %collective-permute-start.1 = (bf16[2,80,128]{2,1,0:T(8,128)(2,1)S(1)}, bf16[2,80,128]{2,1,0:T(8,128)(2,1)S(1)}, u32[]{:S(2)}, u32[]{:S(2)}) collective-permute-start(bf16[2,80,128]{2,1,0:T(8,128)(2,1)S(1)} %get-tuple-element.31), channel_id=1, source_target_pairs={{0,8},{8,16},{16,24},{24,32},{32,40},{40,48},{48,56},{56,64},{64,7... | collective-permute-start | bytes 122888 | tf_op jit(solution)/shard_map/ppermute | solution.py:389
  10.1 6.3 %collective-permute-start.2 = (bf16[2,2,80,128]{3,2,1,0:T(8,128)(2,1)S(1)}, bf16[2,2,80,128]{3,2,1,0:T(8,128)(2,1)S(1)}, u32[]{:S(2)}, u32[]{:S(2)}) collective-permute-start(bf16[2,2,80,128]{3,2,1,0:T(8,128)(2,1)S(1)} %get-tuple-element.32), channel_id=1, source_target_pairs={{0,1},{1,0},{2,3},{3,2},{4,5},{5,4},{6,7},{7,6},{8,9},{9,8},{10,11... | collective-permute-start | bytes 245768 | tf_op jit(solution)/shard_map/ppermute | solution.py:454
  11.2 5.2 %collective-permute-start.3 = (bf16[2,2,80,128]{3,2,1,0:T(8,128)(2,1)S(1)}, bf16[2,2,80,128]{3,2,1,0:T(8,128)(2,1)S(1)}, u32[]{:S(2)}, u32[]{:S(2)}) collective-permute-start(bf16[2,2,80,128]{3,2,1,0:T(8,128)(2,1)S(1)} %get-tuple-element.33), channel_id=1, source_target_pairs={{0,64},{1,2},{2,1},{3,4},{4,3},{5,6},{6,5},{7,71},{8,72},{9,10},{1... | collective-permute-start | bytes 245768 | tf_op jit(solution)/shard_map/ppermute | solution.py:455
  14.1 5.7 %collective-permute-start.5 = (bf16[2,2,80,128]{3,2,1,0:T(8,128)(2,1)S(1)}, bf16[2,2,80,128]{3,2,1,0:T(8,128)(2,1)S(1)}, u32[]{:S(2)}, u32[]{:S(2)}) collective-permute-start(bf16[2,2,80,128]{3,2,1,0:T(8,128)(2,1)S(1)} %pad_maximum_fusion), channel_id=1, source_target_pairs={{0,64},{1,2},{2,1},{3,4},{4,3},{5,6},{6,5},{7,71},{8,72},{9,10},{1... | collective-permute-start | bytes 245768 | tf_op jit(solution)/shard_map/ppermute | solution.py:455
  14.7 5.1 %collective-permute-start.4 = (bf16[2,2,80,128]{3,2,1,0:T(8,128)(2,1)S(1)}, bf16[2,2,80,128]{3,2,1,0:T(8,128)(2,1)S(1)}, u32[]{:S(2)}, u32[]{:S(2)}) collective-permute-start(bf16[2,2,80,128]{3,2,1,0:T(8,128)(2,1)S(1)} %pad_maximum_fusion), channel_id=1, source_target_pairs={{0,1},{1,0},{2,3},{3,2},{4,5},{5,4},{6,7},{7,6},{8,9},{9,8},{10,11... | collective-permute-start | bytes 245768 | tf_op jit(solution)/shard_map/ppermute | solution.py:454
  36.3 1.2 %copy-start.7 = (bf16[64,96,128]{2,1,0:T(8,128)(2,1)}, bf16[64,96,128]{2,1,0:T(8,128)(2,1)S(1)}, u32[]{:S(2)}) copy-start(bf16[64,96,128]{2,1,0:T(8,128)(2,1)S(1)} %get-tuple-element.37.both) | copy-start | bytes 4718596
  37.5 26.1 %all-to-all-start = ((bf16[128,16,128]{2,1,0:T(8,128)(2,1)}), bf16[128,16,128]{2,1,0:T(8,128)(2,1)S(1)}, u32[]{:S(2)}, u32[]{:S(2)}) async-start(bf16[128,16,128]{2,1,0:T(8,128)(2,1)} %bitcast.17), calls=%async_computation | async-start | bytes 1048576 | tf_op jit(solution)/shard_map/all_to_all | solution.py:490
  49.9 9.9 %collective-permute-start.6 = (bf16[96,128]{1,0:T(8,128)(2,1)S(1)}, bf16[96,128]{1,0:T(8,128)(2,1)S(1)}, u32[]{:S(2)}, u32[]{:S(2)}) collective-permute-start(bf16[96,128]{1,0:T(8,128)(2,1)S(1)} %get-tuple-element.38), channel_id=1, source_target_pairs={{8,0},{16,8},{24,16},{32,24},{40,32},{48,40},{56,48},{64,56},{72,6... | collective-permute-start | bytes 73736 | tf_op jit(solution)/shard_map/ppermute | solution.py:388
  51.0 8.8 %collective-permute-start.7 = (bf16[96,128]{1,0:T(8,128)(2,1)S(1)}, bf16[96,128]{1,0:T(8,128)(2,1)S(1)}, u32[]{:S(2)}, u32[]{:S(2)}) collective-permute-start(bf16[96,128]{1,0:T(8,128)(2,1)S(1)} %get-tuple-element.39), channel_id=1, source_target_pairs={{0,8},{8,16},{16,24},{24,32},{32,40},{40,48},{48,56},{56,64},{64,7... | collective-permute-start | bytes 73736 | tf_op jit(solution)/shard_map/ppermute | solution.py:389
  53.2 12.1 %collective-permute-start.8 = (bf16[2,96,128]{2,1,0:T(8,128)(2,1)S(1)}, bf16[2,96,128]{2,1,0:T(8,128)(2,1)S(1)}, u32[]{:S(2)}, u32[]{:S(2)}) collective-permute-start(bf16[2,96,128]{2,1,0:T(8,128)(2,1)S(1)} %get-tuple-element.41), channel_id=1, source_target_pairs={{0,1},{1,0},{2,3},{3,2},{4,5},{5,4},{6,7},{7,6},{8,9},{9,8},{10,11... | collective-permute-start | bytes 147464 | tf_op jit(solution)/shard_map/ppermute | solution.py:493
  54.6 10.7 %collective-permute-start.9 = (bf16[2,96,128]{2,1,0:T(8,128)(2,1)S(1)}, bf16[2,96,128]{2,1,0:T(8,128)(2,1)S(1)}, u32[]{:S(2)}, u32[]{:S(2)}) collective-permute-start(bf16[2,96,128]{2,1,0:T(8,128)(2,1)S(1)} %get-tuple-element.42), channel_id=1, source_target_pairs={{0,64},{1,2},{2,1},{3,4},{4,3},{5,6},{6,5},{7,71},{8,72},{9,10},{1... | collective-permute-start | bytes 147464 | tf_op jit(solution)/shard_map/ppermute | solution.py:494
  59.8 14.5 %copy-start.1 = (bf16[78,64,128]{2,1,0:T(8,128)(2,1)S(1)}, bf16[78,64,128]{2,1,0:T(8,128)(2,1)}, u32[]{:S(2)}) copy-start(bf16[78,64,128]{2,1,0:T(8,128)(2,1)} %base.3) | copy-start | bytes 3833860
  59.8 5.4 %collective-permute-start.11 = (bf16[2,96,128]{2,1,0:T(8,128)(2,1)S(1)}, bf16[2,96,128]{2,1,0:T(8,128)(2,1)S(1)}, u32[]{:S(2)}, u32[]{:S(2)}) collective-permute-start(bf16[2,96,128]{2,1,0:T(8,128)(2,1)S(1)} %pad_maximum_fusion.1), channel_id=1, source_target_pairs={{0,64},{1,2},{2,1},{3,4},{4,3},{5,6},{6,5},{7,71},{8,72},{9,10},{1... | collective-permute-start | bytes 147464 | tf_op jit(solution)/shard_map/ppermute | solution.py:494
  62.6 2.9 %collective-permute-start.10 = (bf16[2,96,128]{2,1,0:T(8,128)(2,1)S(1)}, bf16[2,96,128]{2,1,0:T(8,128)(2,1)S(1)}, u32[]{:S(2)}, u32[]{:S(2)}) collective-permute-start(bf16[2,96,128]{2,1,0:T(8,128)(2,1)S(1)} %pad_maximum_fusion.1), channel_id=1, source_target_pairs={{0,1},{1,0},{2,3},{3,2},{4,5},{5,4},{6,7},{7,6},{8,9},{9,8},{10,11... | collective-permute-start | bytes 147464 | tf_op jit(solution)/shard_map/ppermute | solution.py:493
  65.5 22.5 %all-to-all-start.1 = ((bf16[128,16,128]{2,1,0:T(8,128)(2,1)}), bf16[128,16,128]{2,1,0:T(8,128)(2,1)S(1)}, u32[]{:S(2)}, u32[]{:S(2)}) async-start(bf16[128,16,128]{2,1,0:T(8,128)(2,1)} %shard_map.95), calls=%async_computation.1 | async-start | bytes 1048576 | tf_op jit(solution)/shard_map/all_to_all | solution.py:503
  74.3 1.4 %copy-start.8 = (bf16[64,96,128]{2,1,0:T(8,128)(2,1)S(1)}, bf16[64,96,128]{2,1,0:T(8,128)(2,1)}, u32[]{:S(2)}) copy-start(bf16[64,96,128]{2,1,0:T(8,128)(2,1)} %copy-done.7) | copy-start | bytes 4718596
  75.7 5.4 %copy-start.3 = (bf16[78,64,128]{2,1,0:T(8,128)(2,1)S(1)}, bf16[78,64,128]{2,1,0:T(8,128)(2,1)}, u32[]{:S(2)}) copy-start(bf16[78,64,128]{2,1,0:T(8,128)(2,1)} %base.2) | copy-start | bytes 3833860
